TPU v7x, 128 devices: a whole 4x4x4 slice. The times are simulated.
128 devices in a mesh: fsdp: 4 (over x), ctx: 16 (over z_hi, y, core), tp: 2 (over z_lo).
Axes of the slice: x: 4, y: 4, z: 4 (z_hi: 2, z_lo: 2; z = z_hi * 2 + z_lo), core: 2. Of those that a mesh axis runs over, the one named last changes fastest.
Arguments:
- tokens: bfloat16 [4, 4096, 1024], P('fsdp', 'ctx'), may hold values from -12 to 12, as said below
- ln1_gain: bfloat16 [1024], P(('fsdp', 'ctx')), may hold values from 0.5 to 1.5
- ln1_bias: bfloat16 [1024], P(('fsdp', 'ctx')), may hold values from -1.5 to 1.5
- qkv_weight: bfloat16 [1024, 3, 1024], P(('fsdp', 'ctx'), None, 'tp'), may hold values from -0.1875 to 0.1875
- qv_bias: bfloat16 [2, 1024], P(None, 'tp'), may hold values from -1.5 to 1.5
- proj_weight: bfloat16 [1024, 1024], P('tp', ('fsdp', 'ctx')), may hold values from -0.75 to 0.75
- proj_bias: bfloat16 [1024], P(('fsdp', 'ctx')), may hold values from -1.5 to 1.5
- ln2_gain: bfloat16 [1024], P(('fsdp', 'ctx')), may hold values from 0.5 to 1.5
- ln2_bias: bfloat16 [1024], P(('fsdp', 'ctx')), may hold values from -1.5 to 1.5
- fc_weight: bfloat16 [1024, 4096], P(('fsdp', 'ctx'), 'tp'), may hold values from -0.1875 to 0.1875
- fc_bias: bfloat16 [4096], P('tp'), may hold values from -2.5 to 2.5
- out_weight: bfloat16 [4096, 1024], P('tp', ('fsdp', 'ctx')), may hold values from -0.09375 to 0.09375
- out_bias: bfloat16 [1024], P(('fsdp', 'ctx')), may hold values from -1.5 to 1.5
- piece_starts: int32 [4, 2], P('fsdp'), may hold values from 0 to 3840, as said below
- seq_lengths: int32 [4], replicated, may hold values from 3968 to 4096, as said below
- cotangent: bfloat16 [4, 4096, 1024], P('fsdp', 'ctx'), may hold values from -6 to 6
Outputs:
- layer_out: bfloat16 [4, 4096, 1024], P('fsdp', 'ctx')
- grad_tokens: bfloat16 [4, 4096, 1024], P('fsdp', 'ctx')
- grad_ln1_gain: float32 [1024], P(('fsdp', 'ctx'))
- grad_ln1_bias: float32 [1024], P(('fsdp', 'ctx'))
- grad_qkv: float32 [1024, 3, 1024], P(('fsdp', 'ctx'), None, 'tp')
- grad_qv_bias: float32 [2, 1024], P(None, 'tp')
- grad_proj: float32 [1024, 1024], P('tp', ('fsdp', 'ctx'))
- grad_proj_bias: float32 [1024], P(('fsdp', 'ctx'))
- grad_ln2_gain: float32 [1024], P(('fsdp', 'ctx'))
- grad_ln2_bias: float32 [1024], P(('fsdp', 'ctx'))
- grad_fc: float32 [1024, 4096], P(('fsdp', 'ctx'), 'tp')
- grad_fc_bias: float32 [4096], P('tp')
- grad_out: float32 [4096, 1024], P('tp', ('fsdp', 'ctx'))
- grad_out_bias: float32 [1024], P(('fsdp', 'ctx'))
- root_squares: float32 [4], replicated
Inputs may be any that keep to these rules, and one draw needn't show every extreme that they name: `tokens`: each row is a value drawn near zero scaled by a factor that depends on the row. `piece_starts`: piece k of a sequence starts at k * (2048) or later and ends by (k + 1) * 2048; pieces never intersect. `seq_lengths`: some sequence is full in every draw.
All inputs are finite; a program needn't handle non-finite values.
Results may differ from a plain program's by a relative error of at most 0.02.
Values may be sent and summed in bfloat16 or wider, within the bound.
No kernel may reach another device: no remote copies, remote signals or barrier semaphores. Data moves between devices by JAX's collectives and lax.ppermute only.
A program may use at most 128 MiB of HBM per device.

v0:
```python
from functools import partial

import jax
import jax.numpy as jnp
from jax import lax
from jax.experimental import pallas as pl
from jax.experimental.pallas import tpu as pltpu
from jax.sharding import Mesh
from jax.sharding import PartitionSpec as P

f32 = jnp.float32
bf16 = jnp.bfloat16
NORM_EPS = 1e-05
ROOT_EPS = 1e-06
B=256; E=64; NB=16; MASKED=-1e30; PIECE=256

class Facts:
    def __init__(self, lengths_ref, starts_ref):
        self.core = lax.axis_index("c")
        self.items = (self.core, lengths_ref[lax.axis_index("x")], starts_ref[0, 0], starts_ref[0, 1])

    def __getitem__(self, at):
        return self.items[at]


def piece_of(pos, info_ref):
    n0=(pos>=info_ref[2])&(pos<info_ref[2]+PIECE)
    n1=(pos>=info_ref[3])&(pos<info_ref[3]+PIECE)
    return jnp.where(n0,1,0)+jnp.where(n1,2,0)

def allowed_block(key_block, query_block, info_ref):
    kpos=key_block*B+lax.broadcasted_iota(jnp.int32,(B,1),0)
    qpos=query_block*B+lax.broadcasted_iota(jnp.int32,(1,B),1)
    kp=piece_of(kpos,info_ref); qp=piece_of(qpos,info_ref)
    qp=jnp.where(qp==0,-1,qp)
    kp=jnp.where(kpos<info_ref[1],kp,-2)
    kpos=jnp.where(kpos<info_ref[1],kpos,1<<20)
    return (kpos<=qpos)|(kp==qp)

def extra_blocks(p, info_ref):
    edge=(2*p+2)*B
    crosses=((info_ref[2]<edge)&(edge<info_ref[2]+PIECE))|((info_ref[3]<edge)&(edge<info_ref[3]+PIECE))
    return jnp.where((info_ref[0]==1)&(p<NB//2-1)&crosses,1,0)

def dot(a,b): return jnp.dot(a,b,preferred_element_type=f32)

SAFE = 60.0


def split3(row):
    top = row.astype(bf16).astype(f32)
    mid = (row - top).astype(bf16).astype(f32)
    rows = jnp.concatenate([top, mid, row - top - mid, jnp.zeros((13, B), f32)], axis=0)
    return rows.astype(bf16)


def ones_beside(block):
    lane = lax.broadcasted_iota(jnp.int32, (B, 16), 1)
    return jnp.concatenate([block, jnp.where(lane < 3, 1.0, 0.0).astype(bf16)], axis=1)


CHUNK = 1024


def walk(m, odd, extra, step, carry):
    first = pl.multiple_of(m * CHUNK, CHUNK)
    carry = lax.fori_loop(
        0, m, lambda i, c: step(pl.multiple_of(i * CHUNK, CHUNK), CHUNK, 0, c), carry
    )
    carry = step(first, 2 * B * (1 + odd), 2, carry)
    end = pl.multiple_of(first + 2 * B * (1 + odd), B)
    return lax.fori_loop(0, extra, lambda i, c: step(end, B, 1, c), carry)


def masked_from(e, first, count, masked, query_block, info_ref):
    if not masked:
        return e
    keep = count - masked * B
    parts = [e[:keep]] if keep else []
    for at in range(keep, count, B):
        allowed = allowed_block((first + at) // B, query_block, info_ref)
        parts.append(jnp.where(allowed, e[at : at + B], 0.0))
    return jnp.concatenate(parts, axis=0)


def place(block):
    return pl.ds(pl.multiple_of(block * B, B), B)


def walk_all(p, extra, step, carry, chunk):
    end = 2 * B * (p + 1)
    for first in range(0, end, chunk):
        last = min(first + chunk, end)
        carry = step(first, last - first, max(0, last - (end - 2 * B)) // B, carry)
    if p == NB // 2 - 1:
        return carry
    return lax.fori_loop(0, extra, lambda i, c: step(end, B, 1, c), carry)


def forward_kernel(lengths_ref, starts_ref, own_ref, other_ref, out_ref, low_ref, lse_ref, key_ref, value_ref):
    info_ref = Facts(lengths_ref, starts_ref)
    core = info_ref[0]
    sublane = lax.broadcasted_iota(jnp.int32, (16, NB * B), 0)
    value_ref[E:, :] = jnp.where(sublane == 0, 1.0, 0.0).astype(bf16)

    def squares(block):
        field = block.astype(f32)
        return jnp.sum(field * field, axis=0, keepdims=True)

    query_top = jnp.zeros((1, B), f32)
    key_top = jnp.zeros((1, B), f32)
    for p in range(NB // 2):
        mine, theirs = own_ref[p, E : 2 * E, :], other_ref[p, :E, :]
        here, there = place(2 * p + core), place(2 * p + 1 - core)
        key_ref[here, :] = mine.T
        key_ref[there, :] = theirs.T
        value_ref[:E, here] = own_ref[p, 2 * E :, :]
        value_ref[:E, there] = other_ref[p, E:, :]
        query_top = jnp.maximum(query_top, squares(own_ref[p, :E, :]))
        key_top = jnp.maximum(key_top, jnp.maximum(squares(mine), squares(theirs)))
    bound = jnp.max(query_top) * jnp.max(key_top)

    def finish(p, top, acc):
        total = acc[E : E + 1]
        o = acc[:E] / total
        out_ref[p] = o
        low_ref[p, 0] = o.astype(bf16)
        low_ref[p, 1] = o.astype(bf16)
        lse_ref[p] = top + jnp.log(total)

    @pl.when(bound <= (8.0 * SAFE) ** 2)
    def _():
        for p in range(NB // 2):
            query = own_ref[p, :E, :] * jnp.asarray(0.125, bf16)
            qb = 2 * p + core

            def step(first, count, masked, acc):
                e = jnp.exp(dot(key_ref[first : first + count, :], query))
                e = masked_from(e, first, count, masked, qb, info_ref)
                return acc + dot(value_ref[:, first : first + count], e.astype(bf16))

            acc = walk_all(p, extra_blocks(p, info_ref), step, jnp.zeros((E + 16, B), f32), CHUNK)
            finish(p, 0.0, acc)

    @pl.when(bound > (8.0 * SAFE) ** 2)
    def _():
        def one(p, _):
            query = own_ref[p, :E, :] * jnp.asarray(0.125, bf16)
            qb = 2 * p + core

            def step(blocks, masked, carry):
                top, acc = carry
                scores = [dot(key_ref[place(j), :], query) for j in blocks]
                if masked:
                    scores = [
                        jnp.where(allowed_block(j, qb, info_ref), s, MASKED)
                        for j, s in zip(blocks, scores)
                    ]
                new = top
                for s in scores:
                    new = jnp.maximum(new, jnp.max(s, axis=0, keepdims=True))
                acc = acc * jnp.exp(top - new)
                for j, s in zip(blocks, scores):
                    acc = acc + dot(value_ref[:, place(j)], jnp.exp(s - new).astype(bf16))
                return new, acc

            carry = (jnp.full((1, B), MASKED, f32), jnp.zeros((E + 16, B), f32))
            carry = step((2 * p, 2 * p + 1), True, carry)
            carry = lax.fori_loop(0, p, lambda i, c: step((2 * i, 2 * i + 1), False, c), carry)
            carry = lax.fori_loop(
                0, extra_blocks(p, info_ref), lambda i, c: step((2 * p + 2,), True, c), carry
            )
            finish(p, *carry)
            return 0

        lax.fori_loop(0, NB // 2, one, 0)


def backward_kernel(
    lengths_ref,
    starts_ref,
    own_ref,
    other_ref,
    gout_ref,
    out_ref,
    lse_ref,
    gq_ref,
    gown_ref,
    gother_ref,
    key_ref,
    keyt_ref,
    value_ref,
    grad_ref,
):
    info_ref = Facts(lengths_ref, starts_ref)
    core = info_ref[0]
    for p in range(NB // 2):
        mine, theirs = own_ref[p, E : 2 * E, :], other_ref[p, :E, :]
        here, there = place(2 * p + core), place(2 * p + 1 - core)
        keyt_ref[:, here] = mine
        keyt_ref[:, there] = theirs
        key_ref[here, :] = ones_beside(mine.T)
        key_ref[there, :] = ones_beside(theirs.T)
        value_ref[here, :] = ones_beside(own_ref[p, 2 * E :, :].T)
        value_ref[there, :] = ones_beside(other_ref[p, E:, :].T)
    grad_ref[...] = jnp.zeros_like(grad_ref)
    blank = jnp.zeros((B, E), bf16)

    def one(m, odd):
        p = 2 * m + odd
        query = own_ref[p, :E, :] * jnp.asarray(0.125, bf16)
        gout = gout_ref[p]
        delta = jnp.sum(gout.astype(f32) * out_ref[p], axis=0, keepdims=True)
        rows = jnp.concatenate([blank, query.T], axis=1)
        gout_rows = jnp.concatenate([gout.T, blank], axis=1)
        query = jnp.concatenate([query, split3(-lse_ref[p])], axis=0)
        gout = jnp.concatenate([gout, split3(-delta)], axis=0)
        qb = 2 * p + core

        def step(first, count, masked, acc):
            at = pl.ds(first, count)
            e = jnp.exp(dot(key_ref[at, :], query))
            e = masked_from(e, first, count, masked, qb, info_ref)
            gs = (e * dot(value_ref[at, :], gout)).astype(bf16)
            grad_ref[at, :] += dot(e.astype(bf16), gout_rows) + dot(gs, rows)
            return acc + dot(keyt_ref[:, at], gs)

        acc = walk(m, odd, extra_blocks(p, info_ref), step, jnp.zeros((E, B), f32))
        gq_ref[p] = (acc * 0.125).astype(bf16)

    def both(m, _):
        one(m, 0)
        one(m, 1)
        return 0

    lax.fori_loop(0, NB // 4, both, 0)
    for p in range(NB // 2):
        mine = grad_ref[place(2 * p + core), :].T
        theirs = grad_ref[place(2 * p + 1 - core), :].T.astype(bf16)
        gown_ref[p, :E, :] = mine[E:]
        gown_ref[p, E:, :] = mine[:E]
        gother_ref[p, :E, :] = theirs[E:]
        gother_ref[p, E:, :] = theirs[:E]


VM=pl.BlockSpec(memory_space=pltpu.VMEM); SM=pl.BlockSpec(memory_space=pltpu.SMEM)
LIMIT=40*1024*1024
def attn_forward(lengths,starts,own,other):
    H=NB//2
    return pl.pallas_call(forward_kernel,
        out_shape=(jax.ShapeDtypeStruct((H,E,B),f32),jax.ShapeDtypeStruct((H,2,E,B),bf16),jax.ShapeDtypeStruct((H,1,B),f32)),
        in_specs=[SM,SM,VM,VM],out_specs=(VM,VM,VM),
        scratch_shapes=[pltpu.VMEM((NB*B,E),bf16),pltpu.VMEM((E+16,NB*B),bf16)],
        compiler_params=pltpu.CompilerParams(vmem_limit_bytes=LIMIT),
        cost_estimate=takes(8),
        name="attention_forward")(lengths,starts,own,other)
def attn_backward(lengths,starts,own,other,gout,out,lse):
    H=NB//2
    def full(*dims): return pl.BlockSpec(dims,lambda i:(0,)*len(dims))
    return pl.pallas_call(backward_kernel,grid=(1,),
        out_shape=(jax.ShapeDtypeStruct((H,E,B),bf16),jax.ShapeDtypeStruct((H,2*E,B),f32),jax.ShapeDtypeStruct((H,2*E,B),bf16)),
        in_specs=[SM,SM,full(H,192,B),full(H,128,B),full(H,E,B),full(H,E,B),full(H,1,B)],out_specs=(full(H,E,B),full(H,128,B),full(H,128,B)),
        scratch_shapes=[pltpu.VMEM((NB*B,E+16),bf16),pltpu.VMEM((E,NB*B),bf16),pltpu.VMEM((NB*B,E+16),bf16),pltpu.VMEM((NB*B,2*E),f32)],
        compiler_params=pltpu.CompilerParams(vmem_limit_bytes=LIMIT),
        cost_estimate=takes(26),
        name="attention_backward")(lengths,starts,own,other,gout,far(out),lse)


SPREAD = ("x", "y", "zh")
LINE = ("zh", "y")
VM = pl.BlockSpec(memory_space=pltpu.VMEM)
SM = pl.BlockSpec(memory_space=pltpu.SMEM)
ANY = pl.BlockSpec(memory_space=pl.ANY)
ROOMY = pltpu.CompilerParams(vmem_limit_bytes=40 * 1024 * 1024)
WHOLE = pltpu.CompilerParams(vmem_limit_bytes=50 * 1024 * 1024)
ALL = pltpu.CompilerParams(vmem_limit_bytes=62 * 1024 * 1024)


def takes(microseconds):
    return pl.CostEstimate(
        flops=int(microseconds * 1.15e9), bytes_accessed=1 << 20, transcendentals=0
    )


def low(field):
    return field.astype(bf16)


def swap(field, axis):
    return lax.ppermute(field, axis, [(0, 1), (1, 0)])


def exchange(field, axes):
    return lax.all_to_all(field, axes, split_axis=0, concat_axis=0, tiled=True)


def after(field, *others):
    return lax.optimization_barrier((field, *others))[0]


def contract(a, b, dim_a, dim_b):
    return lax.dot_general(a, b, (((dim_a,), (dim_b,)), ((), ())), preferred_element_type=f32)


def shape(*dims, kind=bf16):
    return jax.ShapeDtypeStruct(dims, kind)


def far(field):
    return pltpu.with_memory_space_constraint(field, pltpu.HBM)


def block_of(array):
    dims = len(array.shape)
    return pl.BlockSpec(array.shape, lambda *_: (0,) * dims)


def call(kernel, name, outs, *args, scalars=0, cost=1, scratch=(), memory=ROOMY):
    return pl.pallas_call(
        kernel,
        grid=(1,),
        out_shape=outs,
        in_specs=[SM] * scalars + [block_of(a) for a in args[scalars:]],
        out_specs=jax.tree.map(block_of, outs),
        scratch_shapes=list(scratch),
        compiler_params=memory,
        cost_estimate=takes(cost),
        name=name,
    )(*args)


def feature_order(order_ref):
    place = lax.broadcasted_iota(jnp.int32, (1, 1024), 1)
    x, core, y, zh = place >> 8, (place >> 7) & 1, (place >> 5) & 3, (place >> 4) & 1
    feature = ((((x * 2 + zh) * 4 + y) * 2 + core) << 4) + (place & 15)
    for at in range(0, 1024, 256):
        rows = at + lax.broadcasted_iota(jnp.int32, (256, 1024), 0)
        order_ref[at : at + 256, :] = jnp.where(rows == feature, 1.0, 0.0).astype(bf16)


def core_lanes(side):
    core = lax.axis_index("c") ^ side
    return [pl.ds(pl.multiple_of(256 * x + 128 * core, 128), 128) for x in range(4)]


def of_core(ref, side):
    return jnp.concatenate([ref[:, lanes] for lanes in core_lanes(side)], axis=1)


def valid_rows(lengths_ref):
    ctx = (lax.axis_index("zh") * 4 + lax.axis_index("y")) * 2 + lax.axis_index("c")
    position = ctx * 256 + lax.broadcasted_iota(jnp.int32, (256, 1), 0)
    return jnp.where(position < lengths_ref[lax.axis_index("x")], 1.0, 0.0)


def norm_parts(values):
    center = values - jnp.mean(values, axis=-1, keepdims=True)
    inverse = lax.rsqrt(jnp.mean(center * center, axis=-1, keepdims=True) + NORM_EPS)
    return center * inverse, inverse


def norm_back(grad, gain, norm, inverse):
    scaled = grad * gain
    return inverse * (
        scaled
        - jnp.mean(scaled, axis=-1, keepdims=True)
        - norm * jnp.mean(scaled * norm, axis=-1, keepdims=True)
    )


def gelu_pair(u):
    k = 0.7978845608028654
    square = u * u
    t = jnp.tanh(u * (k + (k * 0.044715) * square))
    half = 0.5 + 0.5 * t
    value = u * half
    slope = half + (0.5 * u) * (1.0 - t * t) * (k + (3 * 0.044715 * k) * square)
    return value, slope


def prepare_kernel(qkv_ref, a_ref, b_ref, c_ref, d_ref, e_ref, g_ref, out_ref):
    rows = [r[...].astype(f32) for r in (a_ref, b_ref, c_ref, d_ref, e_ref, g_ref)]
    small = jnp.concatenate(rows + [jnp.zeros((2, 16), f32)], axis=0).T
    small = low(jnp.concatenate([small, jnp.zeros((16, 120), f32)], axis=1))

    def one(k, _):
        for c in range(3):
            out_ref[k, :, 512 * c : 512 * (c + 1)] = qkv_ref[:, c, :]
        out_ref[k, :, 1536:] = small
        return 0

    lax.fori_loop(0, 32, one, 0)


def prepare_rest_kernel(proj_ref, fc_ref, out_ref, rest_ref):
    rest_ref[:, :512] = proj_ref[...]
    rest_ref[:, 512:2560] = fc_ref[...]
    rest_ref[:, 2560:] = out_ref[...]


def pair_kernel(mine_ref, by_zh_ref, by_tp_ref, by_both_ref, out_ref):
    zh, tp = lax.axis_index("zh"), lax.axis_index("tp")
    here = pl.ds(pl.multiple_of(zh * 16, 16), 16)
    there = pl.ds(pl.multiple_of(16 - zh * 16, 16), 16)
    near = pl.ds(pl.multiple_of(tp * 512, 512), 512)
    far_off = pl.ds(pl.multiple_of(512 - tp * 512, 512), 512)
    for rows, ref, other_ref in ((here, mine_ref, by_tp_ref), (there, by_zh_ref, by_both_ref)):
        out_ref[rows, near] = ref[:, :512]
        out_ref[rows, far_off] = other_ref[...]
        out_ref[rows, 1024:] = ref[:, 512:]


def inputs_kernel(lengths_ref, tokens_ref, cotangent_ref, inputs_ref, grad_ref, order_ref):
    feature_order(order_ref)
    inputs_ref[...] = low(dot(tokens_ref[...], order_ref[...]))
    grad = dot(cotangent_ref[...], order_ref[...]) * valid_rows(lengths_ref)
    grad_ref[...] = low(grad)


def qkv_kernel(
    inputs_ref, own_ref, other_ref, bias_ref, heads_ref, own_n_ref, other_n_ref, vectors_ref, normed_ref
):
    for side, ref in ((0, own_ref), (1, other_ref)):
        small = ref[:, 1536:].astype(f32).T[:8]
        for x, lanes in enumerate(core_lanes(side)):
            vectors_ref[:, lanes] = small[:, 128 * x : 128 * (x + 1)]
    norm, _ = norm_parts(inputs_ref[...].astype(f32))
    normed_ref[...] = low(norm * vectors_ref[0:1, :] + vectors_ref[1:2, :])
    own_n_ref[...] = of_core(normed_ref, 0)
    other_n_ref[...] = of_core(normed_ref, 1)
    for c in range(3):
        cols = slice(512 * c, 512 * (c + 1))
        field = dot(own_n_ref[...], own_ref[:, cols]) + dot(other_n_ref[...], other_ref[:, cols])
        if c != 1:
            field = field + bias_ref[c // 2 : c // 2 + 1, :].astype(f32)
        field = low(field).T
        for h in range(8):
            heads_ref[h, 64 * c : 64 * (c + 1), :] = field[64 * h : 64 * (h + 1)]


def attn_end_kernel(heads_ref, weight_ref, inputs_ref, vectors_ref, middle_ref, n_ref, own_ref, wide_ref):
    tp = lax.axis_index("tp")
    for h in range(8):
        for t in range(2):
            at = 512 * t + 64 * h
            wide_ref[at : at + 64, :] = heads_ref[2 * h + t]
        own_ref[64 * h : 64 * (h + 1), :] = heads_ref[2 * h + tp]
    attn_out = contract(wide_ref[...].T, weight_ref[...], 1, 1) + vectors_ref[2:3, :]
    middle = inputs_ref[...].astype(f32) + attn_out
    middle_ref[...] = middle
    norm, _ = norm_parts(middle)
    n_ref[...] = low(norm * vectors_ref[3:4, :] + vectors_ref[4:5, :])


def attention_end(heads_all, rest, inputs, vectors):
    wide = pl.BlockSpec((256, 1024), lambda i: (0, 0))
    return pl.pallas_call(
        attn_end_kernel,
        grid=(1,),
        out_shape=(shape(256, 1024, kind=f32), shape(256, 1024), shape(512, 256)),
        in_specs=[
            pl.BlockSpec((16, 64, 256), lambda i: (0, 0, 0)),
            pl.BlockSpec((1024, 1024), lambda i: (0, 0)),
            wide,
            pl.BlockSpec((8, 1024), lambda i: (0, 0)),
        ],
        out_specs=(wide, wide, pl.BlockSpec((512, 256), lambda i: (0, 0))),
        scratch_shapes=[pltpu.VMEM((1024, 256), bf16)],
        compiler_params=ROOMY,
        cost_estimate=takes(3),
        name="attn_end",
    )(heads_all, far(rest), far(inputs), vectors)


def grad_act_kernel(gm_ref, weight_ref, out_ref):
    out_ref[...] = dot(gm_ref[...], weight_ref[...])


def grad_activated(grad_mlp, rest):
    return pl.pallas_call(
        grad_act_kernel,
        grid=(4,),
        out_shape=shape(256, 2048, kind=f32),
        in_specs=[
            pl.BlockSpec((256, 1024), lambda i: (0, 0)),
            pl.BlockSpec((1024, 512), lambda i: (0, 6 + i)),
        ],
        out_specs=pl.BlockSpec((256, 512), lambda i: (0, i)),
        compiler_params=ROOMY,
        cost_estimate=takes(3),
        name="grad_act",
    )(far(grad_mlp), far(rest))


def feed_kernel(n_ref, gact_ref, bias_ref, weight_ref, act_ref, gh_ref, part_ref, total_ref):
    i = pl.program_id(0)

    @pl.when(i == 0)
    def _():
        total_ref[...] = jnp.zeros_like(total_ref)

    halves = (slice(0, 256), slice(256, 512))
    hidden = [
        dot(n_ref[...], weight_ref[:, cols]) + bias_ref[:, cols].astype(f32) for cols in halves
    ]
    for cols, field in zip(halves, hidden):
        value, slope = gelu_pair(field)
        act_ref[:, cols] = low(value)
        gh_ref[:, cols] = low(gact_ref[:, cols] * slope)
    total_ref[...] += contract(gh_ref[...], weight_ref[...], 1, 1)

    @pl.when(i == 3)
    def _():
        part_ref[...] = low(total_ref[...])


def feed_forward(normed_two, grad_act, fc_bias, rest):
    def tile(rows, first):
        return pl.BlockSpec((rows, 512), lambda i: (0, first + i))

    wide = pl.BlockSpec((256, 1024), lambda i: (0, 0))
    return pl.pallas_call(
        feed_kernel,
        grid=(4,),
        out_shape=(shape(256, 2048), shape(256, 2048), shape(256, 1024)),
        in_specs=[wide, tile(256, 0), tile(1, 0), tile(1024, 2)],
        out_specs=(tile(256, 0), tile(256, 0), wide),
        scratch_shapes=[pltpu.VMEM((256, 1024), f32)],
        compiler_params=ROOMY,
        cost_estimate=takes(6),
        name="feed_forward",
    )(normed_two, grad_act, fc_bias, far(rest))


def wide_kernel(n_ref, gh_ref, gm_ref, act_ref, weight_ref, out_ref, part_ref, left_ref, total_ref):
    i = pl.program_id(0)

    @pl.when(i == 0)
    def _():
        left_ref[0] = n_ref[...].T
        left_ref[1] = gm_ref[...].T
        total_ref[...] = jnp.zeros_like(total_ref)

    @pl.when(i < 4)
    def _():
        out_ref[...] = low(dot(left_ref[0], gh_ref[...]))

    @pl.when(i >= 4)
    def _():
        out_ref[...] = low(dot(left_ref[1], act_ref[...]))
        total_ref[...] += contract(act_ref[...], weight_ref[...], 1, 1)

    @pl.when(i == 7)
    def _():
        part_ref[...] = low(total_ref[...])


def wide_grads(normed_two, grad_hidden, grad_mlp, activated, rest):
    whole = pl.BlockSpec((256, 1024), lambda i: (0, 0))
    return pl.pallas_call(
        wide_kernel,
        grid=(8,),
        out_shape=(shape(1024, 4096), shape(256, 1024)),
        in_specs=[
            whole,
            pl.BlockSpec((256, 512), lambda i: (0, jnp.minimum(i, 3))),
            whole,
            pl.BlockSpec((256, 512), lambda i: (0, jnp.maximum(i - 4, 0))),
            pl.BlockSpec((1024, 512), lambda i: (0, 6 + jnp.maximum(i - 4, 0))),
        ],
        out_specs=(pl.BlockSpec((1024, 512), lambda i: (0, i)), whole),
        scratch_shapes=[pltpu.VMEM((2, 1024, 256), bf16), pltpu.VMEM((256, 1024), f32)],
        compiler_params=WHOLE,
        cost_estimate=takes(8),
        name="wide_grads",
    )(normed_two, grad_hidden, far(grad_mlp), activated, far(rest))


def middle_back_kernel(
    middle_ref, mine_ref, swapped_ref, vectors_ref, gm_ref, weight_ref, out_ref, ga_ref, gheads_ref, cols_ref
):
    gm = gm_ref[...].astype(f32)
    norm, inverse = norm_parts(middle_ref[...])
    grad = mine_ref[...].astype(f32) + swapped_ref[...].astype(f32)
    out = gm + norm_back(grad, vectors_ref[3:4, :], norm, inverse)
    out_ref[...] = out
    low_out = low(out)
    ga_ref[...] = low_out
    tp = lax.axis_index("tp")
    field = low(dot(low_out, weight_ref[:, pl.ds(pl.multiple_of(tp * 512, 512), 512)])).T
    for h in range(8):
        gheads_ref[h] = field[64 * h : 64 * (h + 1)]
    rows = [low_out.astype(f32), grad * norm, grad, gm]
    rows = [jnp.sum(r, axis=0, keepdims=True) for r in rows]
    cols_ref[...] = jnp.concatenate(rows + [jnp.zeros((4, 1024), f32)], axis=0)


def middle_back(middle, mine, swapped, vectors, grad_mlp, rest):
    def whole(*dims):
        return pl.BlockSpec(dims, lambda i: (0,) * len(dims))

    wide = whole(256, 1024)
    return pl.pallas_call(
        middle_back_kernel,
        grid=(1,),
        out_shape=(
            shape(256, 1024, kind=f32),
            shape(256, 1024),
            shape(8, 64, 256),
            shape(8, 1024, kind=f32),
        ),
        in_specs=[wide, wide, wide, whole(8, 1024), wide, whole(1024, 1024)],
        out_specs=(wide, wide, whole(8, 64, 256), whole(8, 1024)),
        compiler_params=ALL,
        cost_estimate=takes(3),
        name="middle_back",
    )(far(middle), mine, swapped, vectors, far(grad_mlp), far(rest))


def put_block(ref, at, block):
    for g in range(32):
        ref[16 * g : 16 * (g + 1), at : at + 128] = block


def merge_kernel(query_ref, own_ref, other_ref, out_ref):
    out_ref[:, :64, :] = query_ref[...]
    out_ref[:, 64:, :] = low(own_ref[...] + other_ref[...].astype(f32))


def final_kernel(
    lengths_ref, inputs_ref, middle_ref, mine_ref, swapped_ref, vectors_ref, out_ref, roots_ref, order_ref
):
    feature_order(order_ref)
    valid = valid_rows(lengths_ref)
    inputs = inputs_ref[...].astype(f32)
    middle = middle_ref[...]
    mlp_out = mine_ref[...].astype(f32) + swapped_ref[...].astype(f32) + vectors_ref[5:6, :]
    final = middle + mlp_out
    out_ref[...] = low(contract(low(final), order_ref[...], 1, 1))
    lane = lax.broadcasted_iota(jnp.int32, (1, 128), 1)
    total = jnp.zeros((1, 128), f32)
    for k, field in enumerate((inputs, middle - inputs, mlp_out, final)):
        total = jnp.where(lane == k, jnp.sum(valid * field * field), total)
    roots_ref[...] = total


def side_kernel(ga_ref, heads_ref, rows_ref, mine_ref, theirs_ref):
    for side, ref in ((0, mine_ref), (1, theirs_ref)):
        ref[:, :512] = low(contract(of_core(ga_ref, side).T, heads_ref[...], 1, 1))
        cols = jnp.concatenate([of_core(rows_ref, side), jnp.zeros((120, 512), f32)], axis=0)
        ref[:, 512:] = low(cols.T)


def grads_into(ref, normed, grads_ref, sums, rows):
    left = normed.T
    for c in range(3):
        cols = slice(512 * c, 512 * (c + 1))
        ref[:, cols] = low(contract(left, grads_ref[cols, :], 1, 1))
    put_block(ref, 1536, sums[0])
    put_block(ref, 1664, sums[1])
    cols = [jnp.zeros((4, 512), f32), rows[:2], jnp.zeros((122, 512), f32)]
    ref[:, 1792:] = low(jnp.concatenate(cols, axis=0).T)


def sum_rows(field, dim, count, extra):
    sums = contract(jnp.ones((8, 256), bf16), field, 1, dim)[0:1]
    sums = [sums[:, 128 * r : 128 * (r + 1)] for r in range(count)]
    return low(jnp.concatenate(sums + extra, axis=0))


def back_kernel(
    gback_ref,
    own_ref,
    other_ref,
    inputs_ref,
    other_n_ref,
    roots_ref,
    gh_ref,
    keep_ref,
    send_ref,
    rows_ref,
    theirs_ref,
    grads_ref,
    sums_ref,
    norm_ref,
    part_ref,
):
    for c in range(3):
        for h in range(8):
            at = 512 * c + 64 * h
            grads_ref[at : at + 64, :] = gback_ref[h, 64 * c : 64 * (c + 1), :]
    sides = [grads_ref[512 * c : 512 * (c + 1), :].T for c in range(3)]
    norm_ref[...], _ = norm_parts(inputs_ref[...].astype(f32))
    parts = []
    for side, ref in ((0, own_ref), (1, other_ref)):
        part = sum(contract(sides[c], ref[:, 512 * c : 512 * (c + 1)], 1, 1) for c in range(3))
        part = low(part)
        for x, lanes in enumerate(core_lanes(side)):
            part_ref[:, lanes] = part[:, 128 * x : 128 * (x + 1)]
        part = part.astype(f32)
        gain = jnp.sum(part * of_core(norm_ref, side), axis=0, keepdims=True)
        shift = jnp.sum(part, axis=0, keepdims=True)
        parts.append(jnp.concatenate([gain, shift, jnp.zeros((6, 512), f32)], axis=0))
    rows_ref[...] = parts[0]
    tp = lax.axis_index("tp")
    keep_ref[...] = part_ref[pl.ds(pl.multiple_of(tp * 128, 128), 128), :]
    send_ref[...] = part_ref[pl.ds(pl.multiple_of(128 - tp * 128, 128), 128), :]
    extra = [roots_ref[...], jnp.zeros((3, 128), f32)]
    sums_ref[0] = sum_rows(grads_ref[...], 1, 12, extra)
    sums_ref[1] = sum_rows(gh_ref[...], 0, 16, [])
    grads_into(theirs_ref, other_n_ref[...], grads_ref, sums_ref, parts[1])


def core_add_kernel(
    grads_ref, own_n_ref, sums_ref, b_ref, p_ref, q_ref, rows_ref, out_ref, left_ref
):
    i = pl.program_id(0)

    @pl.when(i == 0)
    def _():
        left_ref[...] = own_n_ref[...].T

    rows = pl.ds(pl.multiple_of(i * 128, 128), 128)
    for c in range(3):
        cols = slice(512 * c, 512 * (c + 1))
        mine = low(contract(left_ref[rows, :], grads_ref[cols, :], 1, 1)).astype(f32)
        out_ref[:, cols] = low(mine + b_ref[:, cols].astype(f32))
    for k in range(2):
        at = 1536 + 128 * k
        for g in range(8):
            theirs = b_ref[16 * g : 16 * (g + 1), at : at + 128].astype(f32)
            out_ref[16 * g : 16 * (g + 1), at : at + 128] = low(sums_ref[k].astype(f32) + theirs)
    side = p_ref[...].astype(f32) + q_ref[...].astype(f32)
    out_ref[:, 1792:2304] = low(side[:, :512])
    ln1 = jnp.concatenate([jnp.zeros((4, 128), f32), rows_ref[:2], jnp.zeros((122, 128), f32)], axis=0)
    both = low(ln1.T).astype(f32) + b_ref[:, 1792:].astype(f32)
    out_ref[:, 2304:] = low(side[:, 512:] + both)


def core_add(grads, own_n, sums, theirs, mine_p, theirs_p, rows):
    def tall(cols):
        return pl.BlockSpec((128, cols), lambda i: (i, 0))

    flat = pl.BlockSpec((8, 128), lambda i: (0, i))
    return pl.pallas_call(
        core_add_kernel,
        grid=(4,),
        out_shape=shape(512, 2432),
        in_specs=[
            block_of(grads),
            block_of(own_n),
            block_of(sums),
            tall(1920),
            tall(640),
            tall(640),
            flat,
        ],
        out_specs=tall(2432),
        scratch_shapes=[pltpu.VMEM((512, 256), bf16)],
        compiler_params=ALL,
        cost_estimate=takes(4),
        name="qkv_core_sum",
    )(grads, far(own_n), sums, theirs, far(mine_p), theirs_p, rows)


def end_kernel(inputs_ref, gmid_ref, mine_ref, swapped_ref, vectors_ref, out_ref, order_ref):
    feature_order(order_ref)
    rows = pl.ds(pl.multiple_of(lax.axis_index("tp") * 128, 128), 128)
    norm, inverse = norm_parts(inputs_ref[rows, :].astype(f32))
    grad = mine_ref[...].astype(f32) + swapped_ref[...].astype(f32)
    grad = gmid_ref[rows, :] + norm_back(grad, vectors_ref[0:1, :], norm, inverse)
    out_ref[...] = low(contract(low(grad), order_ref[...], 1, 1))


def join_kernel(mine_ref, theirs_ref, out_ref):
    tp = lax.axis_index("tp")
    out_ref[pl.ds(pl.multiple_of(tp * 128, 128), 128), :] = mine_ref[...]
    out_ref[pl.ds(pl.multiple_of(128 - tp * 128, 128), 128), :] = theirs_ref[...]


def total_qkv_kernel(lengths_ref, got_ref, qkv_ref, proj_ref, bias_ref, fc_ref, roots_ref):
    total = got_ref[0].astype(f32)
    for k in range(1, 32):
        total = total + got_ref[k].astype(f32)
    for c in range(3):
        qkv_ref[:, c, :] = total[:, 512 * c : 512 * (c + 1)]
    for k in range(2):
        for r in range(4):
            row = 8 * k + r
            bias_ref[k : k + 1, 128 * r : 128 * (r + 1)] = total[row : row + 1, 1536:1664]
    count = lengths_ref[0] + lengths_ref[1] + lengths_ref[2] + lengths_ref[3]
    mean = total[12:13, 1536:1664] / (count.astype(f32) * 1024.0)
    roots_ref[...] = jnp.sqrt(mean + ROOT_EPS)
    fc_ref[...] = total[:, 1664:1792]
    proj_ref[...] = total[:, 1792:2304]


def total_cols_kernel(got_ref, cols_ref):
    total = got_ref[0].astype(f32)
    for k in range(1, 32):
        total = total + got_ref[k].astype(f32)
    cols_ref[...] = total.T[:8]


def total_cols(got):
    return pl.pallas_call(
        total_cols_kernel,
        grid=(1,),
        out_shape=shape(8, 16, kind=f32),
        in_specs=[pl.BlockSpec((32, 16, 128), lambda i: (0, 0, 18))],
        out_specs=pl.BlockSpec((8, 16), lambda i: (0, 0)),
        compiler_params=ROOMY,
        cost_estimate=takes(1),
        name="total_cols",
    )(got)


def total_wide_kernel(mine_ref, theirs_ref, fc_ref, out_ref):
    total = mine_ref[...].astype(f32) + theirs_ref[...].astype(f32)
    fc_ref[...] = total[:, :2048]
    out_ref[...] = total[:, 2048:]


def body(
    tokens,
    ln1_gain,
    ln1_bias,
    qkv_weight,
    qv_bias,
    proj_weight,
    proj_bias,
    ln2_gain,
    ln2_bias,
    fc_weight,
    fc_bias,
    out_weight,
    out_bias,
    piece_starts,
    seq_lengths,
    cotangent,
):
    vectors = (ln1_gain, ln1_bias, proj_bias, ln2_gain, ln2_bias, out_bias)
    pay_q = call(
        prepare_kernel,
        "weights_payload",
        shape(32, 16, 1664),
        qkv_weight,
        *[v.reshape(1, 16) for v in vectors],
    )
    own_q = exchange(pay_q, SPREAD).reshape(512, 1664)
    proj_rows = proj_weight.T
    pay_r = call(
        prepare_rest_kernel, "rest_payload", shape(16, 4608), proj_rows, fc_weight, out_weight.T
    )
    pair_r = call(
        pair_kernel,
        "rest_pair",
        shape(32, 5120),
        after(pay_r, pay_q),
        swap(pay_r, "zh"),
        swap(proj_rows, "tp"),
        lax.ppermute(proj_rows, ("zh", "tp"), [(i, 3 - i) for i in range(4)]),
    )
    rest = lax.all_gather(pair_r, ("x", "c", "y"), axis=0, tiled=True)

    inputs, grad_mlp = call(
        inputs_kernel,
        "inputs",
        (shape(256, 1024), shape(256, 1024)),
        seq_lengths,
        tokens[0],
        cotangent[0],
        scalars=1,
        cost=2,
        scratch=[pltpu.VMEM((1024, 1024), bf16)],
    )
    own_q = after(own_q, inputs)
    other_q = swap(own_q, "c")
    heads, own_n, other_n, vectors = call(
        qkv_kernel,
        "qkv",
        (shape(8, 192, 256), shape(256, 512), shape(256, 512), shape(8, 1024, kind=f32)),
        far(inputs),
        own_q,
        other_q,
        qv_bias,
        scratch=[pltpu.VMEM((256, 1024), bf16)],
        cost=3,
    )
    own = exchange(heads, LINE)
    other = swap(own[:, 64:], "c")
    attended, attended_low, log_sum = attn_forward(seq_lengths, piece_starts, own, other)
    heads_all = exchange(attended_low.reshape(16, 64, 256), ("zh", "y", "tp"))
    grad_act = grad_activated(grad_mlp, after(rest, attended_low))
    middle, normed_two, heads_out = attention_end(
        heads_all, after(rest, grad_act), inputs, vectors
    )
    activated, grad_hidden, two_part = feed_forward(
        normed_two, grad_act, fc_bias.reshape(1, 2048), rest
    )
    two_swapped = swap(two_part, "tp")
    wide, mlp_part = wide_grads(normed_two, grad_hidden, grad_mlp, activated, rest)
    wide = lax.psum_scatter(
        after(wide, two_swapped), ("x", "c"), scatter_dimension=0, tiled=True
    )
    two_swapped = after(two_swapped, mlp_part)
    grad_middle, grad_attn, grad_heads, rows = middle_back(
        middle, two_part, two_swapped, vectors, grad_mlp, rest
    )
    grad_mine = exchange(grad_heads, LINE)

    mine_p, theirs_p = call(
        side_kernel,
        "proj_grads",
        (shape(512, 640), shape(512, 640)),
        far(grad_attn),
        far(heads_out),
        rows,
        cost=2,
    )
    grad_mine = after(grad_mine, mine_p)
    theirs_p = swap(after(theirs_p, grad_mine), "c")
    mlp_swapped = swap(after(mlp_part, grad_mine), "tp")

    grad_query, grad_own, grad_other = attn_backward(
        seq_lengths, piece_starts, own, other, grad_mine, attended, log_sum
    )
    grad_other, mlp_swapped = lax.optimization_barrier((grad_other, mlp_swapped))
    grad_back = call(
        merge_kernel, "merge", shape(8, 192, 256), grad_query, grad_own, swap(grad_other, "c")
    )
    grad_back = exchange(grad_back, LINE)
    layer_out, roots = call(
        final_kernel,
        "final",
        (shape(256, 1024), shape(1, 128, kind=f32)),
        seq_lengths,
        far(inputs),
        far(middle),
        after(mlp_part, grad_other),
        mlp_swapped,
        vectors,
        scalars=1,
        cost=3,
        scratch=[pltpu.VMEM((1024, 1024), bf16)],
    )
    one_keep, one_send, rows, theirs_q, grads, sums = call(
        back_kernel,
        "back",
        (
            shape(128, 1024),
            shape(128, 1024),
            shape(8, 512, kind=f32),
            shape(512, 1920),
            shape(1536, 256),
            shape(2, 16, 128),
        ),
        grad_back,
        far(own_q),
        far(other_q),
        far(inputs),
        far(other_n),
        roots,
        far(grad_hidden),
        cost=5,
        scratch=[pltpu.VMEM((256, 1024), f32), pltpu.VMEM((256, 1024), bf16)],
        memory=ALL,
    )
    one_swapped = swap(one_send, "tp")
    wide = lax.psum_scatter(after(wide, roots), "y", scatter_dimension=0, tiled=True)
    both = core_add(
        grads,
        own_n,
        sums,
        after(swap(theirs_q, "c"), one_swapped),
        mine_p,
        theirs_p,
        rows,
    )
    got_q = exchange(both.reshape(32, 16, 2432), SPREAD)
    half_tokens = call(
        end_kernel,
        "end",
        shape(128, 1024),
        far(inputs),
        far(grad_middle),
        one_keep,
        one_swapped,
        vectors,
        cost=2,
        scratch=[pltpu.VMEM((1024, 1024), bf16)],
    )
    grad_tokens = call(
        join_kernel, "join", shape(256, 1024), half_tokens, swap(half_tokens, "tp")
    )
    zh = lax.axis_index("zh")
    keep = lax.dynamic_slice_in_dim(wide, zh * 16, 16, 0)
    send = lax.dynamic_slice_in_dim(wide, 16 - zh * 16, 16, 0)
    grad_fc, grad_out = call(
        total_wide_kernel,
        "total_wide",
        (shape(16, 2048, kind=f32), shape(16, 2048, kind=f32)),
        keep,
        swap(send, "zh"),        cost=14,
    )
    got_q = after(got_q, grad_fc, grad_tokens)
    cols = total_cols(got_q)
    ln1 = cols[4:6]
    grad_qkv, grad_proj, bias_sums, fc_sums, roots = call(
        total_qkv_kernel,
        "total_qkv",
        (
            shape(16, 3, 512, kind=f32),
            shape(16, 512, kind=f32),
            shape(2, 512, kind=f32),
            shape(16, 128, kind=f32),
            shape(1, 128, kind=f32),
        ),
        seq_lengths,
        after(got_q, cols),
        scalars=1,
    )
    ln1 = ln1 + swap(ln1, "tp")
    return (
        layer_out[None],
        grad_tokens[None],
        ln1[0],
        ln1[1],
        grad_qkv,
        bias_sums,
        grad_proj.T,
        cols[0],
        cols[1],
        cols[2],
        grad_fc,
        fc_sums.reshape(2048),
        grad_out.T,
        cols[3],
        roots[0, :4],
    )


def solution(mesh):
    fine = Mesh(mesh.devices.reshape(4, 2, 4, 2, 2), ("x", "zh", "y", "c", "tp"))
    ctx = ("zh", "y", "c")
    every = ("x", "zh", "y", "c")
    in_specs = (
        P("x", ctx, None),
        P(every),
        P(every),
        P(every, None, "tp"),
        P(None, "tp"),
        P("tp", every),
        P(every),
        P(every),
        P(every),
        P(every, "tp"),
        P("tp"),
        P("tp", every),
        P(every),
        P("x", None),
        P(),
        P("x", ctx, None),
    )
    out_specs = (
        P("x", ctx, None),
        P("x", ctx, None),
        P(every),
        P(every),
        P(every, None, "tp"),
        P(None, "tp"),
        P("tp", every),
        P(every),
        P(every),
        P(every),
        P(every, "tp"),
        P("tp"),
        P("tp", every),
        P(every),
        P(),
    )
    return jax.shard_map(body, mesh=fine, in_specs=in_specs, out_specs=out_specs, check_vma=False)
```

profile of v0, /device:TPU:0, one launch (start us, length us, event | category | flops | bytes accessed | tf_op | source)
XLA Modules:
  0.0 283.7 jit_solution(15769485337684305622)
XLA Ops:
  8.1 0.8 copy-done.18
  9.8 4.0 %collective-permute-start.2 = (bf16[16,4608]{1,0:T(8,128)(2,1)S(1)}, bf16[16,4608]{1,0:T(8,128)(2,1)S(1)}, u32[]{:S(2)}, u32[]{:S(2)}) collective-permute-start(bf16[16,4608]{1,0:T(8,128)(2,1)S(1)} %rest_payload.1.mine_ref), channel_id=1, source_target_pairs={{0,16},{16,0},{1,17},{17,1},{2,18},{18,2},{3,19},{19,3},{4,20},{20... | collective-permute-start | bytes 442376 | tf_op jit(solution)/shard_map/ppermute | solution.py:290
  13.8 1.0 collective-permute-start.3
  14.9 4.3 %weights_payload.1 = bf16[32,16,1664]{2,1,0:T(8,128)(2,1)} custom-call(bf16[16,3,512]{2,1,0:T(4,128)(2,1)S(1)} %copy.31.qkv_ref, bf16[1,16]{1,0:T(2,128)(2,1)S(1)} %bitcast.38, bf16[1,16]{1,0:T(2,128)(2,1)S(1)} %bitcast.39, bf16[1,16]{1,0:T(2,128)(2,1)S(1)} %bitcast.40, bf16[1,16]{1,0:T(2,128)(2,1)S(1)} %bitcast.41, bf16[1,16]{1,0:T(2,128)(2,1)S(1)} %bitcast.42, ...), custom_call_target="tpu_custom_call" | custom-call | flops 1150000000 | bytes 1048576 | tf_op jit(solution)/shard_map/weights_payload/pallas_call | solution.py:319
  20.8 9.3 %all-to-all-start = ((bf16[32,16,1664]{2,1,0:T(8,128)(2,1)}), bf16[32,16,1664]{2,1,0:T(8,128)(2,1)S(1)}, u32[]{:S(2)}, u32[]{:S(2)}) async-start(bf16[32,16,1664]{2,1,0:T(8,128)(2,1)} %weights_payload.1), calls=%async_computation | async-start | bytes 3407872 | tf_op jit(solution)/shard_map/all_to_all | solution.py:294
  30.1 1.9 inputs.1
  33.6 26.1 %all-to-all-done = bf16[32,16,1664]{2,1,0:T(8,128)(2,1)S(1)} async-done(((bf16[32,16,1664]{2,1,0:T(8,128)(2,1)}), bf16[32,16,1664]{2,1,0:T(8,128)(2,1)S(1)}, u32[]{:S(2)}, u32[]{:S(2)}) %all-to-all-start) | async-done | bytes 1703968 | tf_op jit(solution)/shard_map/all_to_all | solution.py:294
  59.7 3.6 %collective-permute-done.other_ref = bf16[512,1664]{1,0:T(8,128)(2,1)S(1)} collective-permute-done((bf16[512,1664]{1,0:T(8,128)(2,1)S(1)}, bf16[512,1664]{1,0:T(8,128)(2,1)S(1)}, u32[]{:S(2)}, u32[]{:S(2)}) %collective-permute-start) | collective-permute-done | bytes 1703968 | tf_op jit(solution)/shard_map/ppermute | solution.py:290
  63.3 3.1 %qkv.1 = (bf16[8,192,256]{2,1,0:T(8,128)(2,1)S(1)}, bf16[256,512]{1,0:T(8,128)(2,1)S(1)}, bf16[256,512]{1,0:T(8,128)(2,1)S(1)}, f32[8,1024]{1,0:T(8,128)S(1)}) custom-call(bf16[256,1024]{1,0:T(8,128)(2,1)} %copy-done.29, bf16[512,1664]{1,0:T(8,128)(2,1)S(1)} %bitcast.33, bf16[512,1664]{1,0:T(8,128)(2,1)S(1)} %collective-permute-done.other_ref, ...), custom_call_target="tpu_custom_call" | custom-call | flops 3449999872 | bytes 1048576 | tf_op jit(solution)/shard_map/qkv/pallas_call | solution.py:319
  66.5 24.9 %all_to_all.30.own_ref = bf16[8,192,256]{2,1,0:T(8,128)(2,1)S(1)} all-to-all(bf16[8,192,256]{2,1,0:T(8,128)(2,1)S(1)} %get-tuple-element.74), channel_id=1, replica_groups=mesh['x'=4,'zh'=2,'y'=4,'c'=2,'tp'=2] {'zh','y'}, dimensions={0} | all-to-all | bytes 1572864 | tf_op jit(solution)/shard_map/all_to_all | solution.py:294
  91.6 2.0 collective-permute-done.1.other_ref
  93.6 8.7 %attention_forward.1 = (f32[8,64,256]{2,1,0:T(8,128)S(1)}, bf16[8,2,64,256]{3,2,1,0:T(8,128)(2,1)}, f32[8,1,256]{2,1,0:T(1,128)S(1)}) custom-call(s32[4]{0:T(128)S(1)} %copy-done.28, s32[1,2]{1,0:T(1,128)S(1)} %copy-done.27, bf16[8,192,256]{2,1,0:T(8,128)(2,1)S(1)} %all_to_all.30.own_ref, bf16[8,128,256]{2,1,0:T(8,128)(2,1)S(1)} %collective-permute-done.1.other_ref), custom_call_target="tpu_custom_call" | custom-call | flops 9200000000 | bytes 1048576 | tf_op jit(solution)/shard_map/attention_forward/pallas_call | solution.py:250
  103.1 5.0 %all-to-all-start.2 = ((bf16[16,64,256]{2,1,0:T(8,128)(2,1)}), bf16[16,64,256]{2,1,0:T(8,128)(2,1)S(1)}, u32[]{:S(2)}, u32[]{:S(2)}) async-start(bf16[16,64,256]{2,1,0:T(8,128)(2,1)} %bitcast.9), calls=%async_computation.2 | async-start | bytes 1048576 | tf_op jit(solution)/shard_map/all_to_all | solution.py:294
  108.2 4.1 %grad_act.1.gact_ref = f32[256,2048]{1,0:T(8,128)S(1)} custom-call(bf16[256,1024]{1,0:T(8,128)(2,1)} %copy-done.2, bf16[1024,5120]{1,0:T(8,128)(2,1)} %all-gather.2.cloned.1.call-done.weight_ref), custom_call_target="tpu_custom_call" | custom-call | flops 3449999872 | bytes 1048576 | tf_op jit(solution)/shard_map/grad_act/pallas_call | solution.py:480
  112.4 1.4 copy-done
  113.8 7.1 %all-to-all-done.2.heads_ref = bf16[16,64,256]{2,1,0:T(8,128)(2,1)S(1)} async-done(((bf16[16,64,256]{2,1,0:T(8,128)(2,1)}), bf16[16,64,256]{2,1,0:T(8,128)(2,1)S(1)}, u32[]{:S(2)}, u32[]{:S(2)}) %all-to-all-start.2) | async-done | bytes 524320 | tf_op jit(solution)/shard_map/all_to_all | solution.py:294
  120.9 2.9 %attn_end.1 = (f32[256,1024]{1,0:T(8,128)S(1)}, bf16[256,1024]{1,0:T(8,128)(2,1)S(1)}, bf16[512,256]{1,0:T(8,128)(2,1)S(1)}) custom-call(bf16[16,64,256]{2,1,0:T(8,128)(2,1)S(1)} %all-to-all-done.2.heads_ref, bf16[1024,5120]{1,0:T(8,128)(2,1)} %all-gather.2.cloned.1.call-done.weight_ref, bf16[256,1024]{1,0:T(8,128)(2,1)} %copy-done.29, ...), custom_call_target="tpu_custom_call" | custom-call | flops 3449999872 | bytes 1048576 | tf_op jit(solution)/shard_map/attn_end/pallas_call | solution.py:457
  123.8 6.4 %feed_forward.1 = (bf16[256,2048]{1,0:T(8,128)(2,1)S(1)}, bf16[256,2048]{1,0:T(8,128)(2,1)S(1)}, bf16[256,1024]{1,0:T(8,128)(2,1)S(1)}) custom-call(bf16[256,1024]{1,0:T(8,128)(2,1)S(1)} %get-tuple-element.82.n_ref, f32[256,2048]{1,0:T(8,128)S(1)} %copy-done.1, bf16[1,2048]{1,0:T(2,128)(2,1)S(1)} %reshape.71.bias_ref, ...), custom_call_target="tpu_custom_call" | custom-call | flops 6899999744 | bytes 1048576 | tf_op jit(solution)/shard_map/feed_forward/pallas_call | solution.py:522
  131.0 10.2 %wide_grads.1 = (bf16[1024,4096]{1,0:T(8,128)(2,1)}, bf16[256,1024]{1,0:T(8,128)(2,1)S(1)}) custom-call(bf16[256,1024]{1,0:T(8,128)(2,1)S(1)} %get-tuple-element.82.n_ref, bf16[256,2048]{1,0:T(8,128)(2,1)S(1)} %get-tuple-element.83.gh_ref, bf16[256,1024]{1,0:T(8,128)(2,1)} %copy-done.2, bf16[256,2048]{1,0:T(8,128)(2,1)S(1)} %get-tuple-element.84.act_ref, ...), custom_call_target="tpu_custom_call" | custom-call | flops 9200000000 | bytes 1048576 | tf_op jit(solution)/shard_map/wide_grads/pallas_call | solution.py:560
  142.0 1.5 collective-permute-done.5.swapped_ref
  144.4 4.7 %middle_back.1 = (f32[256,1024]{1,0:T(8,128)}, bf16[256,1024]{1,0:T(8,128)(2,1)}, bf16[8,64,256]{2,1,0:T(8,128)(2,1)}, f32[8,1024]{1,0:T(8,128)}) custom-call(f32[256,1024]{1,0:T(8,128)} %copy-done.4, bf16[256,1024]{1,0:T(8,128)(2,1)} %copy-done.5, bf16[256,1024]{1,0:T(8,128)(2,1)} %copy-done.39, f32[8,1024]{1,0:T(8,128)} %copy-done.6, ...), custom_call_target="tpu_custom_call" | custom-call | flops 3449999872 | bytes 1048576 | tf_op jit(solution)/shard_map/middle_back/pallas_call | solution.py:603
  149.1 3.5 %all-to-all-start.3 = ((bf16[8,64,256]{2,1,0:T(8,128)(2,1)}), bf16[8,64,256]{2,1,0:T(8,128)(2,1)S(1)}, u32[]{:S(2)}, u32[]{:S(2)}) async-start(bf16[8,64,256]{2,1,0:T(8,128)(2,1)} %get-tuple-element.88), calls=%async_computation.3 | async-start | bytes 524288 | tf_op jit(solution)/shard_map/all_to_all | solution.py:294
  153.4 1.7 proj_grads.1
  155.1 0.9 copy-done.31
  156.0 5.5 %all-to-all-done.3.gout_ref = bf16[8,64,256]{2,1,0:T(8,128)(2,1)S(1)} async-done(((bf16[8,64,256]{2,1,0:T(8,128)(2,1)}), bf16[8,64,256]{2,1,0:T(8,128)(2,1)S(1)}, u32[]{:S(2)}, u32[]{:S(2)}) %all-to-all-start.3) | async-done | bytes 262176 | tf_op jit(solution)/shard_map/all_to_all | solution.py:294
  162.0 18.3 %attention_backward.1 = (bf16[8,64,256]{2,1,0:T(8,128)(2,1)S(1)}, f32[8,128,256]{2,1,0:T(8,128)S(1)}, bf16[8,128,256]{2,1,0:T(8,128)(2,1)S(1)}) custom-call(s32[4]{0:T(128)S(1)} %copy-done.28, s32[1,2]{1,0:T(1,128)S(1)} %copy-done.27, bf16[8,192,256]{2,1,0:T(8,128)(2,1)S(1)} %all_to_all.30.own_ref, bf16[8,128,256]{2,1,0:T(8,128)(2,1)S(1)} %copy-done.12, ...), custom_call_target="tpu_custom_call" | custom-call | flops 29899999232 | bytes 1048576 | tf_op jit(solution)/shard_map/attention_backward/pallas_call | solution.py:260
  181.1 1.9 collective-permute-done.7.other_ref
  183.0 1.0 merge.1
  184.0 3.8 %all-to-all-start.4 = ((bf16[8,192,256]{2,1,0:T(8,128)(2,1)}), bf16[8,192,256]{2,1,0:T(8,128)(2,1)S(1)}, u32[]{:S(2)}, u32[]{:S(2)}) async-start(bf16[8,192,256]{2,1,0:T(8,128)(2,1)} %merge.1), calls=%async_computation.4 | async-start | bytes 1572864 | tf_op jit(solution)/shard_map/all_to_all | solution.py:294
  187.8 3.4 %final.1 = (bf16[256,1024]{1,0:T(8,128)(2,1)}, f32[1,128]{1,0:T(1,128)S(1)}) custom-call(s32[4]{0:T(128)S(1)} %copy-done.28, bf16[256,1024]{1,0:T(8,128)(2,1)} %copy-done.29, f32[256,1024]{1,0:T(8,128)} %copy-done.4, bf16[256,1024]{1,0:T(8,128)(2,1)S(1)} %copy-done.14, bf16[256,1024]{1,0:T(8,128)(2,1)S(1)} %copy-done.16, f32[8,1024]{1,0:T(8,128)S(1)} %copy-done.7), custom_call_target="tpu_custom_call" | custom-call | flops 3449999872 | bytes 1048576 | tf_op jit(solution)/shard_map/final/pallas_call | solution.py:319
  191.8 10.9 %all-to-all-done.4.gback_ref = bf16[8,192,256]{2,1,0:T(8,128)(2,1)S(1)} async-done(((bf16[8,192,256]{2,1,0:T(8,128)(2,1)}), bf16[8,192,256]{2,1,0:T(8,128)(2,1)S(1)}, u32[]{:S(2)}, u32[]{:S(2)}) %all-to-all-start.4) | async-done | bytes 786464 | tf_op jit(solution)/shard_map/all_to_all | solution.py:294
  202.7 0.9 copy-done.38
  203.6 6.4 %back.1 = (bf16[128,1024]{1,0:T(8,128)(2,1)}, bf16[128,1024]{1,0:T(8,128)(2,1)}, f32[8,512]{1,0:T(8,128)}, bf16[512,1920]{1,0:T(8,128)(2,1)}, bf16[1536,256]{1,0:T(8,128)(2,1)}, /*index=5*/bf16[2,16,128]{2,1,0:T(8,128)(2,1)}) custom-call(bf16[8,192,256]{2,1,0:T(8,128)(2,1)} %copy-done.38, bf16[512,1664]{1,0:T(8,128)(2,1)} %bitcast.34, ...), custom_call_target="tpu_custom_call" | custom-call | flops 5750000128 | bytes 1048576 | tf_op jit(solution)/shard_map/back/pallas_call | solution.py:319
  210.7 1.6 collective-permute-start.8
  212.2 7.0 %collective-permute-done.8.swapped_ref = bf16[128,1024]{1,0:T(8,128)(2,1)S(1)} collective-permute-done((bf16[128,1024]{1,0:T(8,128)(2,1)}, bf16[128,1024]{1,0:T(8,128)(2,1)S(1)}, u32[]{:S(2)}, u32[]{:S(2)}) %collective-permute-start.8) | collective-permute-done | bytes 262176 | tf_op jit(solution)/shard_map/ppermute | solution.py:290
  219.2 1.3 copy-done.42
  221.3 5.5 %qkv_core_sum.1 = bf16[512,2432]{1,0:T(8,128)(2,1)} custom-call(bf16[1536,256]{1,0:T(8,128)(2,1)} %get-tuple-element.109.grads_ref, bf16[256,512]{1,0:T(8,128)(2,1)} %copy-done.34, bf16[2,16,128]{2,1,0:T(8,128)(2,1)} %get-tuple-element.111.sums_ref, bf16[512,1920]{1,0:T(8,128)(2,1)} %copy-done.42, bf16[512,640]{1,0:T(8,128)(2,1)} %copy-done.31, ...), custom_call_target="tpu_custom_call" | custom-call | flops 4600000000 | bytes 1048576 | tf_op jit(solution)/shard_map/qkv_core_sum/pallas_call | solution.py:745
  226.8 4.7 %all-to-all-start.5 = ((bf16[32,16,2432]{2,1,0:T(8,128)(2,1)}), bf16[32,16,2432]{2,1,0:T(8,128)(2,1)S(1)}, u32[]{:S(2)}, u32[]{:S(2)}) async-start(bf16[32,16,2432]{2,1,0:T(8,128)(2,1)} %bitcast.44), calls=%async_computation.5 | async-start | bytes 4980736 | tf_op jit(solution)/shard_map/all_to_all | solution.py:294
  231.5 2.5 end.1.mine_ref
  234.1 1.2 collective-permute-start.9
  235.3 1.0 constant_dynamic-slice_fusion
  236.3 4.0 %collective-permute-start.12 = (bf16[16,4096]{1,0:T(8,128)(2,1)S(1)}, bf16[16,4096]{1,0:T(8,128)(2,1)S(1)}, u32[]{:S(2)}, u32[]{:S(2)}) collective-permute-start(bf16[16,4096]{1,0:T(8,128)(2,1)S(1)} %get-tuple-element.144), channel_id=1, source_target_pairs={{0,16},{16,0},{1,17},{17,1},{2,18},{18,2},{3,19},{19,3},{4,20},{20... | collective-permute-start | bytes 393224 | tf_op jit(solution)/shard_map/ppermute | solution.py:290
  240.2 26.1 %collective-permute-done.9.theirs_ref = bf16[128,1024]{1,0:T(8,128)(2,1)S(1)} collective-permute-done((bf16[128,1024]{1,0:T(8,128)(2,1)S(1)}, bf16[128,1024]{1,0:T(8,128)(2,1)S(1)}, u32[]{:S(2)}, u32[]{:S(2)}) %collective-permute-start.9) | collective-permute-done | bytes 262176 | tf_op jit(solution)/shard_map/ppermute | solution.py:290
  266.3 0.8 join.1
  267.1 2.8 collective-permute-done.12.theirs_ref
  271.3 1.3 total_qkv.1
  273.1 1.1 collective-permute-start.13
  274.9 1.8 collective-permute-done.13
  (120 shorter events, 15.3 us)
Async XLA Ops:
  7.2 101.0 %all-gather.2.cloned.1.call-start = ((), (), s32[]{:S(2)}) async-start(), calls=%async_computation.8 | async-start | bytes 10813440 | tf_op jit(solution)/shard_map/all_gather | solution.py:864
  8.9 5.9 %copy-start.40 = (bf16[16,3,512]{2,0,1:T(8,128)(2,1)S(1)}, bf16[16,3,512]{2,0,1:T(8,128)(2,1)}, u32[]{:S(2)}) copy-start(bf16[16,3,512]{2,0,1:T(8,128)(2,1)} %param.19) | copy-start | bytes 147460
  8.9 6.0 %copy-start.21 = (bf16[16]{0:T(256)(128)(2,1)S(1)}, bf16[16]{0:T(256)(128)(2,1)}, u32[]{:S(2)}) copy-start(bf16[16]{0:T(256)(128)(2,1)} %param.17) | copy-start | bytes 100
  8.9 6.0 %copy-start.22 = (bf16[16]{0:T(256)(128)(2,1)S(1)}, bf16[16]{0:T(256)(128)(2,1)}, u32[]{:S(2)}) copy-start(bf16[16]{0:T(256)(128)(2,1)} %param.18) | copy-start | bytes 100
  8.9 6.0 %copy-start.23 = (bf16[16]{0:T(256)(128)(2,1)S(1)}, bf16[16]{0:T(256)(128)(2,1)}, u32[]{:S(2)}) copy-start(bf16[16]{0:T(256)(128)(2,1)} %param.22) | copy-start | bytes 100
  8.9 6.0 %copy-start.24 = (bf16[16]{0:T(256)(128)(2,1)S(1)}, bf16[16]{0:T(256)(128)(2,1)}, u32[]{:S(2)}) copy-start(bf16[16]{0:T(256)(128)(2,1)} %param.23) | copy-start | bytes 100
  8.9 6.0 %copy-start.25 = (bf16[16]{0:T(256)(128)(2,1)S(1)}, bf16[16]{0:T(256)(128)(2,1)}, u32[]{:S(2)}) copy-start(bf16[16]{0:T(256)(128)(2,1)} %param.24) | copy-start | bytes 100
  8.9 6.0 %copy-start.26 = (bf16[16]{0:T(256)(128)(2,1)S(1)}, bf16[16]{0:T(256)(128)(2,1)}, u32[]{:S(2)}) copy-start(bf16[16]{0:T(256)(128)(2,1)} %param.28) | copy-start | bytes 100
  9.8 10.2 %collective-permute-start.2 = (bf16[16,4608]{1,0:T(8,128)(2,1)S(1)}, bf16[16,4608]{1,0:T(8,128)(2,1)S(1)}, u32[]{:S(2)}, u32[]{:S(2)}) collective-permute-start(bf16[16,4608]{1,0:T(8,128)(2,1)S(1)} %rest_payload.1.mine_ref), channel_id=1, source_target_pairs={{0,16},{16,0},{1,17},{17,1},{2,18},{18,2},{3,19},{19,3},{4,20},{20... | collective-permute-start | bytes 442376 | tf_op jit(solution)/shard_map/ppermute | solution.py:290
  13.8 5.5 %collective-permute-start.3 = (bf16[16,512]{1,0:T(8,128)(2,1)}, bf16[16,512]{1,0:T(8,128)(2,1)S(1)}, u32[]{:S(2)}, u32[]{:S(2)}) collective-permute-start(bf16[16,512]{1,0:T(8,128)(2,1)} %bitcast.10.proj_ref), channel_id=1, source_target_pairs={{0,1},{1,0},{2,3},{3,2},{4,5},{5,4},{6,7},{7,6},{8,9},{9,8},{10,11... | collective-permute-start | bytes 49160 | tf_op jit(solution)/shard_map/ppermute | solution.py:290
  14.8 5.2 %collective-permute-start.4 = (bf16[16,512]{1,0:T(8,128)(2,1)}, bf16[16,512]{1,0:T(8,128)(2,1)S(1)}, u32[]{:S(2)}, u32[]{:S(2)}) collective-permute-start(bf16[16,512]{1,0:T(8,128)(2,1)} %bitcast.10.proj_ref), channel_id=1, source_target_pairs={{0,17},{1,16},{16,1},{17,0},{2,19},{3,18},{18,3},{19,2},{4,21},{5,... | collective-permute-start | bytes 49160 | tf_op jit(solution)/shard_map/ppermute | solution.py:862
  20.7 9.3 %copy-start.9 = (bf16[1,256,1024]{2,1,0:T(8,128)(2,1)S(1)}, bf16[1,256,1024]{2,1,0:T(8,128)(2,1)}, u32[]{:S(2)}) copy-start(bf16[1,256,1024]{2,1,0:T(8,128)(2,1)} %param.16) | copy-start | bytes 1572868
  20.8 9.3 %copy-start.10 = (bf16[1,256,1024]{2,1,0:T(8,128)(2,1)S(1)}, bf16[1,256,1024]{2,1,0:T(8,128)(2,1)}, u32[]{:S(2)}) copy-start(bf16[1,256,1024]{2,1,0:T(8,128)(2,1)} %param.31) | copy-start | bytes 1572868
  20.8 9.3 %copy-start.28 = (s32[4]{0:T(128)S(1)}, s32[4]{0:T(128)}, u32[]{:S(2)}) copy-start(s32[4]{0:T(128)} %lengths_ref.9) | copy-start | bytes 52
  20.8 38.9 %all-to-all-start = ((bf16[32,16,1664]{2,1,0:T(8,128)(2,1)}), bf16[32,16,1664]{2,1,0:T(8,128)(2,1)S(1)}, u32[]{:S(2)}, u32[]{:S(2)}) async-start(bf16[32,16,1664]{2,1,0:T(8,128)(2,1)} %weights_payload.1), calls=%async_computation | async-start | bytes 3407872 | tf_op jit(solution)/shard_map/all_to_all | solution.py:294
  30.1 33.2 %copy-start.20 = (bf16[2,512]{1,0:T(2,128)(2,1)S(1)}, bf16[2,512]{1,0:T(2,128)(2,1)}, u32[]{:S(2)}) copy-start(bf16[2,512]{1,0:T(2,128)(2,1)} %bias_ref.1) | copy-start | bytes 6148
  59.7 6.7 %copy-start.3 = (bf16[32,16,1664]{2,1,0:T(8,128)(2,1)}, bf16[32,16,1664]{2,1,0:T(8,128)(2,1)S(1)}, u32[]{:S(2)}) copy-start(bf16[32,16,1664]{2,1,0:T(8,128)(2,1)S(1)} %all-to-all-done) | copy-start | bytes 5111812
  59.7 3.6 %collective-permute-start = (bf16[512,1664]{1,0:T(8,128)(2,1)S(1)}, bf16[512,1664]{1,0:T(8,128)(2,1)S(1)}, u32[]{:S(2)}, u32[]{:S(2)}) collective-permute-start(bf16[512,1664]{1,0:T(8,128)(2,1)S(1)} %bitcast.32), channel_id=1, source_target_pairs={{0,2},{2,0},{1,3},{3,1},{4,6},{6,4},{5,7},{7,5},{8,10},{10,8},{9,1... | collective-permute-start | bytes 5111816 | tf_op jit(solution)/shard_map/ppermute | solution.py:290
  66.5 35.8 %copy-start.34 = (bf16[256,512]{1,0:T(8,128)(2,1)}, bf16[256,512]{1,0:T(8,128)(2,1)S(1)}, u32[]{:S(2)}) copy-start(bf16[256,512]{1,0:T(8,128)(2,1)S(1)} %get-tuple-element.110.own_n_ref) | copy-start | bytes 786436
  66.5 35.8 %copy-start.35 = (bf16[256,512]{1,0:T(8,128)(2,1)}, bf16[256,512]{1,0:T(8,128)(2,1)S(1)}, u32[]{:S(2)}) copy-start(bf16[256,512]{1,0:T(8,128)(2,1)S(1)} %get-tuple-element.105.other_n_ref) | copy-start | bytes 786436
  66.5 54.5 %copy-start.6 = (f32[8,1024]{1,0:T(8,128)}, f32[8,1024]{1,0:T(8,128)S(1)}, u32[]{:S(2)}) copy-start(f32[8,1024]{1,0:T(8,128)S(1)} %get-tuple-element.80.vectors_ref) | copy-start | bytes 98308
  66.5 27.1 %copy-start.27 = (s32[1,2]{1,0:T(1,128)S(1)}, s32[1,2]{1,0:T(1,128)}, u32[]{:S(2)}) copy-start(s32[1,2]{1,0:T(1,128)} %starts_ref.3) | copy-start | bytes 28
  91.5 16.7 %copy-start.41 = (bf16[2048]{0:T(1024)(128)(2,1)S(1)}, bf16[2048]{0:T(1024)(128)(2,1)}, u32[]{:S(2)}) copy-start(bf16[2048]{0:T(1024)(128)(2,1)} %param.26) | copy-start | bytes 12292
  91.5 2.1 collective-permute-start.1
  93.6 8.7 %copy-start.11 = (bf16[8,128,256]{2,1,0:T(8,128)(2,1)}, bf16[8,128,256]{2,1,0:T(8,128)(2,1)S(1)}, u32[]{:S(2)}) copy-start(bf16[8,128,256]{2,1,0:T(8,128)(2,1)S(1)} %collective-permute-done.1.other_ref) | copy-start | bytes 1572868
  103.1 17.9 %all-to-all-start.2 = ((bf16[16,64,256]{2,1,0:T(8,128)(2,1)}), bf16[16,64,256]{2,1,0:T(8,128)(2,1)S(1)}, u32[]{:S(2)}, u32[]{:S(2)}) async-start(bf16[16,64,256]{2,1,0:T(8,128)(2,1)} %bitcast.9), calls=%async_computation.2 | async-start | bytes 1048576 | tf_op jit(solution)/shard_map/all_to_all | solution.py:294
  108.1 101.9 %reduce-scatter.3.cloned.1.call-start = ((), (), s32[]{:S(2)}) async-start(), calls=%async_computation.9 | async-start | bytes 9437184 | tf_op jit(solution)/shard_map/reduce_scatter | solution.py:903
  123.8 6.5 %copy-start.4 = (f32[256,1024]{1,0:T(8,128)}, f32[256,1024]{1,0:T(8,128)S(1)}, u32[]{:S(2)}) copy-start(f32[256,1024]{1,0:T(8,128)S(1)} %get-tuple-element.81.middle_ref) | copy-start | bytes 3145732
  123.8 6.5 %copy-start.30 = (bf16[512,256]{1,0:T(8,128)(2,1)}, bf16[512,256]{1,0:T(8,128)(2,1)S(1)}, u32[]{:S(2)}) copy-start(bf16[512,256]{1,0:T(8,128)(2,1)S(1)} %get-tuple-element.90.heads_ref) | copy-start | bytes 786436
  130.3 10.9 %copy-start.5 = (bf16[256,1024]{1,0:T(8,128)(2,1)}, bf16[256,1024]{1,0:T(8,128)(2,1)S(1)}, u32[]{:S(2)}) copy-start(bf16[256,1024]{1,0:T(8,128)(2,1)S(1)} %get-tuple-element.86.mine_ref) | copy-start | bytes 1572868
  130.3 10.9 %copy-start.33 = (bf16[256,2048]{1,0:T(8,128)(2,1)}, bf16[256,2048]{1,0:T(8,128)(2,1)S(1)}, u32[]{:S(2)}) copy-start(bf16[256,2048]{1,0:T(8,128)(2,1)S(1)} %get-tuple-element.83.gh_ref) | copy-start | bytes 3145732
  130.3 13.2 %collective-permute-start.5 = (bf16[256,1024]{1,0:T(8,128)(2,1)S(1)}, bf16[256,1024]{1,0:T(8,128)(2,1)S(1)}, u32[]{:S(2)}, u32[]{:S(2)}) collective-permute-start(bf16[256,1024]{1,0:T(8,128)(2,1)S(1)} %get-tuple-element.86.mine_ref), channel_id=1, source_target_pairs={{0,1},{1,0},{2,3},{3,2},{4,5},{5,4},{6,7},{7,6},{8,9},{9,8},{10,11... | collective-permute-start | bytes 1572872 | tf_op jit(solution)/shard_map/ppermute | solution.py:290
  149.1 12.4 %all-to-all-start.3 = ((bf16[8,64,256]{2,1,0:T(8,128)(2,1)}), bf16[8,64,256]{2,1,0:T(8,128)(2,1)S(1)}, u32[]{:S(2)}, u32[]{:S(2)}) async-start(bf16[8,64,256]{2,1,0:T(8,128)(2,1)} %get-tuple-element.88), calls=%async_computation.3 | async-start | bytes 524288 | tf_op jit(solution)/shard_map/all_to_all | solution.py:294
  153.4 8.1 %copy-start.14 = (bf16[256,1024]{1,0:T(8,128)(2,1)S(1)}, bf16[256,1024]{1,0:T(8,128)(2,1)}, u32[]{:S(2)}) copy-start(bf16[256,1024]{1,0:T(8,128)(2,1)} %copy-done.13) | copy-start | bytes 1572868
  153.4 8.5 %copy-start.12 = (bf16[8,128,256]{2,1,0:T(8,128)(2,1)S(1)}, bf16[8,128,256]{2,1,0:T(8,128)(2,1)}, u32[]{:S(2)}) copy-start(bf16[8,128,256]{2,1,0:T(8,128)(2,1)} %copy-done.11) | copy-start | bytes 1572868
  161.5 18.8 %collective-permute-start.6 = (bf16[256,1024]{1,0:T(8,128)(2,1)S(1)}, bf16[256,1024]{1,0:T(8,128)(2,1)S(1)}, u32[]{:S(2)}, u32[]{:S(2)}) collective-permute-start(bf16[256,1024]{1,0:T(8,128)(2,1)S(1)} %copy-done.14), channel_id=1, source_target_pairs={{0,1},{1,0},{2,3},{3,2},{4,5},{5,4},{6,7},{7,6},{8,9},{9,8},{10,11... | collective-permute-start | bytes 1572872 | tf_op jit(solution)/shard_map/ppermute | solution.py:290
  181.1 1.9 collective-permute-start.7
  183.0 4.8 %copy-start.7 = (f32[8,1024]{1,0:T(8,128)S(1)}, f32[8,1024]{1,0:T(8,128)}, u32[]{:S(2)}) copy-start(f32[8,1024]{1,0:T(8,128)} %copy-done.6) | copy-start | bytes 98308
  183.0 4.9 %copy-start.16 = (bf16[256,1024]{1,0:T(8,128)(2,1)S(1)}, bf16[256,1024]{1,0:T(8,128)(2,1)}, u32[]{:S(2)}) copy-start(bf16[256,1024]{1,0:T(8,128)(2,1)} %copy-done.15) | copy-start | bytes 1572868
  184.0 18.7 %all-to-all-start.4 = ((bf16[8,192,256]{2,1,0:T(8,128)(2,1)}), bf16[8,192,256]{2,1,0:T(8,128)(2,1)S(1)}, u32[]{:S(2)}, u32[]{:S(2)}) async-start(bf16[8,192,256]{2,1,0:T(8,128)(2,1)} %merge.1), calls=%async_computation.4 | async-start | bytes 1572864 | tf_op jit(solution)/shard_map/all_to_all | solution.py:294
  187.8 47.5 %reduce-scatter.5.cloned.1.call-start = ((), (), s32[]{:S(2)}) async-start(), calls=%async_computation.10 | async-start | bytes 1310720 | tf_op jit(solution)/shard_map/reduce_scatter | solution.py:970
  210.0 9.1 %collective-permute-start.10 = (bf16[512,1920]{1,0:T(8,128)(2,1)}, bf16[512,1920]{1,0:T(8,128)(2,1)S(1)}, u32[]{:S(2)}, u32[]{:S(2)}) collective-permute-start(bf16[512,1920]{1,0:T(8,128)(2,1)} %get-tuple-element.112), channel_id=1, source_target_pairs={{0,2},{2,0},{1,3},{3,1},{4,6},{6,4},{5,7},{7,5},{8,10},{10,8},{9,1... | collective-permute-start | bytes 5898248 | tf_op jit(solution)/shard_map/ppermute | solution.py:290
  210.1 9.1 %collective-permute-start.11 = (bf16[512,640]{1,0:T(8,128)(2,1)S(1)}, bf16[512,640]{1,0:T(8,128)(2,1)S(1)}, u32[]{:S(2)}, u32[]{:S(2)}) collective-permute-start(bf16[512,640]{1,0:T(8,128)(2,1)S(1)} %get-tuple-element.115), channel_id=1, source_target_pairs={{0,2},{2,0},{1,3},{3,1},{4,6},{6,4},{5,7},{7,5},{8,10},{10,8},{9,1... | collective-permute-start | bytes 1966088 | tf_op jit(solution)/shard_map/ppermute | solution.py:290
  210.7 8.5 %collective-permute-start.8 = (bf16[128,1024]{1,0:T(8,128)(2,1)}, bf16[128,1024]{1,0:T(8,128)(2,1)S(1)}, u32[]{:S(2)}, u32[]{:S(2)}) collective-permute-start(bf16[128,1024]{1,0:T(8,128)(2,1)} %get-tuple-element.108), channel_id=1, source_target_pairs={{0,1},{1,0},{2,3},{3,2},{4,5},{5,4},{6,7},{7,6},{8,9},{9,8},{10,11... | collective-permute-start | bytes 786440 | tf_op jit(solution)/shard_map/ppermute | solution.py:290
  226.8 43.9 %all-to-all-start.5 = ((bf16[32,16,2432]{2,1,0:T(8,128)(2,1)}), bf16[32,16,2432]{2,1,0:T(8,128)(2,1)S(1)}, u32[]{:S(2)}, u32[]{:S(2)}) async-start(bf16[32,16,2432]{2,1,0:T(8,128)(2,1)} %bitcast.44), calls=%async_computation.5 | async-start | bytes 4980736 | tf_op jit(solution)/shard_map/all_to_all | solution.py:294
  234.1 32.2 %collective-permute-start.9 = (bf16[128,1024]{1,0:T(8,128)(2,1)S(1)}, bf16[128,1024]{1,0:T(8,128)(2,1)S(1)}, u32[]{:S(2)}, u32[]{:S(2)}) collective-permute-start(bf16[128,1024]{1,0:T(8,128)(2,1)S(1)} %end.1.mine_ref), channel_id=1, source_target_pairs={{0,1},{1,0},{2,3},{3,2},{4,5},{5,4},{6,7},{7,6},{8,9},{9,8},{10,11... | collective-permute-start | bytes 786440 | tf_op jit(solution)/shard_map/ppermute | solution.py:290
  236.3 33.7 %collective-permute-start.12 = (bf16[16,4096]{1,0:T(8,128)(2,1)S(1)}, bf16[16,4096]{1,0:T(8,128)(2,1)S(1)}, u32[]{:S(2)}, u32[]{:S(2)}) collective-permute-start(bf16[16,4096]{1,0:T(8,128)(2,1)S(1)} %get-tuple-element.144), channel_id=1, source_target_pairs={{0,16},{16,0},{1,17},{17,1},{2,18},{18,2},{3,19},{19,3},{4,20},{20... | collective-permute-start | bytes 393224 | tf_op jit(solution)/shard_map/ppermute | solution.py:290
  273.1 3.6 %collective-permute-start.13 = (f32[2,16]{1,0:T(2,128)S(1)}, f32[2,16]{1,0:T(2,128)S(1)}, u32[]{:S(2)}, u32[]{:S(2)}) collective-permute-start(f32[2,16]{1,0:T(2,128)S(1)} %slice.28), channel_id=1, source_target_pairs={{0,1},{1,0},{2,3},{3,2},{4,5},{5,4},{6,7},{7,6},{8,9},{9,8},{10,11... | collective-permute-start | bytes 392 | tf_op jit(solution)/shard_map/ppermute | solution.py:290
  (18 other events, 23.8 us)
Sparse Core Ops, SparseCore 0:
  20.9 78.9 all-gather.1
  144.5 48.9 reduce-scatter.2
  210.2 20.1 reduce-scatter.4
where the time goes:
time: 285 us; the launch traced here: 284 us
  waiting for transfers between devices  97 us (34%)
  Pallas kernels  89.9 us (32%)
  starting transfers between devices  41.1 us (14%)
  blocking collectives  24.9 us (9%)
  local copies, waits for them, and re-layouts  16.4 us (6%)
  between operations  14.3 us (5%)
    all_to_all x5, waiting for transfers between devices, exchange(): return lax.all_to_all(field, axes, split_axis=0, concat_axis=0, tiled=True)  49.7 us
    ppermute x13, waiting for transfers between devices, swap(): return lax.ppermute(field, axis, [(0, 1), (1, 0)])  46.6 us
    pallas_call x13, Pallas kernels, call(): pl.pallas_call(kernel, grid=(1,), out_shape=outs, in_specs=[SM] * scalars...  28.9 us
    all_to_all x5, starting transfers between devices, exchange(): return lax.all_to_all(field, axes, split_axis=0, concat_axis=0, tiled=True)  26.3 us
    all_to_all x1, blocking collectives, exchange(): return lax.all_to_all(field, axes, split_axis=0, concat_axis=0, tiled=True)  24.9 us
    pallas_call x1, Pallas kernels, attn_backward(): pl.pallas_call(backward_kernel, grid=(1,), out_shape=(jax.ShapeDtypeStruc...  18.3 us
    ppermute x13, starting transfers between devices, swap(): return lax.ppermute(field, axis, [(0, 1), (1, 0)])  14.7 us
    unnamed x90, local copies, waits for them, and re-layouts  13.8 us
  transfers between devices with their start and end apart: 22, of which 13 were waited for; matrix products, arithmetic and copies ran while one was open for 1% of the time, Pallas kernels for 27%

commit v1 on v0

--- a/solution.py
+++ b/solution.py
@@ -50,7 +50,7 @@
 def split3(row):
     top = row.astype(bf16).astype(f32)
     mid = (row - top).astype(bf16).astype(f32)
-    rows = jnp.concatenate([top, mid, row - top - mid, jnp.zeros((13, B), f32)], axis=0)
+    rows = jnp.concatenate([top, mid, row - top - mid, jnp.zeros((13, row.shape[1]), f32)], axis=0)
     return rows.astype(bf16)
 
 
@@ -59,17 +59,36 @@
     return jnp.concatenate([block, jnp.where(lane < 3, 1.0, 0.0).astype(bf16)], axis=1)
 
 
-CHUNK = 1024
-
-
-def walk(m, odd, extra, step, carry):
+CHUNK = 4 * B
+
+
+def pair_allowed(m, info_ref):
+    key = m * CHUNK + lax.broadcasted_iota(jnp.int32, (CHUNK, 1), 0)
+    lane = lax.broadcasted_iota(jnp.int32, (1, 2 * B), 1)
+    query = (4 * m + info_ref[0]) * B + lane + jnp.where(lane >= B, B, 0)
+    key_piece, query_piece = piece_of(key, info_ref), piece_of(query, info_ref)
+    query_piece = jnp.where(query_piece == 0, -1, query_piece)
+    valid = key < info_ref[1]
+    key_piece = jnp.where(valid, key_piece, -2)
+    key = jnp.where(valid, key, 1 << 20)
+    return (key <= query) | (key_piece == query_piece)
+
+
+def pair_of(ref, m):
+    return jnp.concatenate([ref[2 * m], ref[2 * m + 1]], axis=1)
+
+
+def walk(m, extra, step, beyond, carry):
+    def chunk(i, c):
+        return step(pl.multiple_of(i * CHUNK, CHUNK), None, c)
+
+    carry = lax.fori_loop(0, m, chunk, carry)
     first = pl.multiple_of(m * CHUNK, CHUNK)
-    carry = lax.fori_loop(
-        0, m, lambda i, c: step(pl.multiple_of(i * CHUNK, CHUNK), CHUNK, 0, c), carry
-    )
-    carry = step(first, 2 * B * (1 + odd), 2, carry)
-    end = pl.multiple_of(first + 2 * B * (1 + odd), B)
-    return lax.fori_loop(0, extra, lambda i, c: step(end, B, 1, c), carry)
+    carry = step(first, m, carry)
+    second = lax.fori_loop(
+        0, extra, lambda i, c: beyond(pl.multiple_of(first + CHUNK, B), c), carry[:, B:]
+    )
+    return carry[:, :B], second
 
 
 def masked_from(e, first, count, masked, query_block, info_ref):
@@ -78,7 +97,7 @@
     keep = count - masked * B
     parts = [e[:keep]] if keep else []
     for at in range(keep, count, B):
-        allowed = allowed_block((first + at) // B, query_block, info_ref)
+        allowed = allowed_block((first >> 8) + at // B, query_block, info_ref)
         parts.append(jnp.where(allowed, e[at : at + B], 0.0))
     return jnp.concatenate(parts, axis=0)
 
@@ -130,17 +149,30 @@
 
     @pl.when(bound <= (8.0 * SAFE) ** 2)
     def _():
-        for p in range(NB // 2):
-            query = own_ref[p, :E, :] * jnp.asarray(0.125, bf16)
-            qb = 2 * p + core
-
-            def step(first, count, masked, acc):
-                e = jnp.exp(dot(key_ref[first : first + count, :], query))
-                e = masked_from(e, first, count, masked, qb, info_ref)
-                return acc + dot(value_ref[:, first : first + count], e.astype(bf16))
-
-            acc = walk_all(p, extra_blocks(p, info_ref), step, jnp.zeros((E + 16, B), f32), CHUNK)
-            finish(p, 0.0, acc)
+        def both(m, _):
+            query = pair_of(own_ref.at[:, :E, :], m) * jnp.asarray(0.125, bf16)
+
+            def step(first, masked, acc):
+                at = pl.ds(first, CHUNK)
+                e = jnp.exp(dot(key_ref[at, :], query))
+                if masked is not None:
+                    e = jnp.where(pair_allowed(masked, info_ref), e, 0.0)
+                return acc + dot(value_ref[:, at], e.astype(bf16))
+
+            def beyond(first, acc):
+                at = pl.ds(first, B)
+                e = jnp.exp(dot(key_ref[at, :], query[:, B:]))
+                e = jnp.where(allowed_block(4 * m + 4, 4 * m + 2 + core, info_ref), e, 0.0)
+                return acc + dot(value_ref[:, at], e.astype(bf16))
+
+            accs = walk(
+                m, extra_blocks(2 * m + 1, info_ref), step, beyond, jnp.zeros((E + 16, 2 * B), f32)
+            )
+            for odd in range(2):
+                finish(2 * m + odd, 0.0, accs[odd])
+            return 0
+
+        lax.fori_loop(0, NB // 4, both, 0)
 
     @pl.when(bound > (8.0 * SAFE) ** 2)
     def _():
@@ -176,24 +208,9 @@
         lax.fori_loop(0, NB // 2, one, 0)
 
 
-def backward_kernel(
-    lengths_ref,
-    starts_ref,
-    own_ref,
-    other_ref,
-    gout_ref,
-    out_ref,
-    lse_ref,
-    gq_ref,
-    gown_ref,
-    gother_ref,
-    key_ref,
-    keyt_ref,
-    value_ref,
-    grad_ref,
-):
-    info_ref = Facts(lengths_ref, starts_ref)
-    core = info_ref[0]
+def stage_kernel(own_ref, other_ref, lse_ref, key_ref, keyt_ref, value_ref, query_ref, rows_ref):
+    core = lax.axis_index("c")
+    blank = jnp.zeros((B, E), bf16)
     for p in range(NB // 2):
         mine, theirs = own_ref[p, E : 2 * E, :], other_ref[p, :E, :]
         here, there = place(2 * p + core), place(2 * p + 1 - core)
@@ -203,37 +220,72 @@
         key_ref[there, :] = ones_beside(theirs.T)
         value_ref[here, :] = ones_beside(own_ref[p, 2 * E :, :].T)
         value_ref[there, :] = ones_beside(other_ref[p, E:, :].T)
+        query = own_ref[p, :E, :] * jnp.asarray(0.125, bf16)
+        query_ref[p, :E, :] = query
+        query_ref[p, E:, :] = split3(-lse_ref[p])
+        rows_ref[p] = jnp.concatenate([blank, query.T], axis=1)
+
+
+def backward_kernel(
+    lengths_ref,
+    starts_ref,
+    key_ref,
+    keyt_ref,
+    value_ref,
+    query_ref,
+    rows_ref,
+    gout_ref,
+    out_ref,
+    gq_ref,
+    gown_ref,
+    gother_ref,
+    grad_ref,
+    gouts_ref,
+    grows_ref,
+    sum_ref,
+):
+    info_ref = Facts(lengths_ref, starts_ref)
+    core = info_ref[0]
     grad_ref[...] = jnp.zeros_like(grad_ref)
     blank = jnp.zeros((B, E), bf16)
-
-    def one(m, odd):
-        p = 2 * m + odd
-        query = own_ref[p, :E, :] * jnp.asarray(0.125, bf16)
+    for p in range(NB // 2):
         gout = gout_ref[p]
         delta = jnp.sum(gout.astype(f32) * out_ref[p], axis=0, keepdims=True)
-        rows = jnp.concatenate([blank, query.T], axis=1)
-        gout_rows = jnp.concatenate([gout.T, blank], axis=1)
-        query = jnp.concatenate([query, split3(-lse_ref[p])], axis=0)
-        gout = jnp.concatenate([gout, split3(-delta)], axis=0)
-        qb = 2 * p + core
-
-        def step(first, count, masked, acc):
-            at = pl.ds(first, count)
-            e = jnp.exp(dot(key_ref[at, :], query))
-            e = masked_from(e, first, count, masked, qb, info_ref)
-            gs = (e * dot(value_ref[at, :], gout)).astype(bf16)
-            grad_ref[at, :] += dot(e.astype(bf16), gout_rows) + dot(gs, rows)
-            return acc + dot(keyt_ref[:, at], gs)
-
-        acc = walk(m, odd, extra_blocks(p, info_ref), step, jnp.zeros((E, B), f32))
-        gq_ref[p] = (acc * 0.125).astype(bf16)
+        gouts_ref[p, :E, :] = gout
+        gouts_ref[p, E:, :] = split3(-delta)
+        grows_ref[p] = jnp.concatenate([gout.T, blank], axis=1)
+    sum_ref[...] = jnp.zeros_like(sum_ref)
+
+    def chunk(p, first, count, masked):
+        at = pl.ds(pl.multiple_of(first, B), count)
+        e = jnp.exp(dot(key_ref[at, :], query_ref[p]))
+        if masked:
+            e = masked_from(e, first, count, masked, 2 * p + core, info_ref)
+        gs = (e * dot(value_ref[at, :], gouts_ref[p])).astype(bf16)
+        grad_ref[at, :] += dot(e.astype(bf16), grows_ref[p]) + dot(gs, rows_ref[p])
+        sum_ref[p] += dot(keyt_ref[:, at], gs)
 
     def both(m, _):
-        one(m, 0)
-        one(m, 1)
+        top = NB // 2 - 1 - m
+        for k in range(NB // 2 - 1):
+            late = k < top
+            chunk(jnp.where(late, top, m), 2 * B * jnp.where(late, k, k - top), 2 * B, 0)
+        chunk(top, 2 * B * top, 2 * B, 2)
+        chunk(m, 2 * B * m, 2 * B, 2)
         return 0
 
     lax.fori_loop(0, NB // 4, both, 0)
+
+    def beyond(p, _):
+        def add(i, _):
+            chunk(p, 2 * B * (p + 1), B, 1)
+            return 0
+
+        return lax.fori_loop(0, extra_blocks(p, info_ref), add, 0)
+
+    lax.fori_loop(0, NB // 2 - 1, beyond, 0)
+    for p in range(NB // 2):
+        gq_ref[p] = (sum_ref[p] * 0.125).astype(bf16)
     for p in range(NB // 2):
         mine = grad_ref[place(2 * p + core), :].T
         theirs = grad_ref[place(2 * p + 1 - core), :].T.astype(bf16)
@@ -254,16 +306,53 @@
         compiler_params=pltpu.CompilerParams(vmem_limit_bytes=LIMIT),
         cost_estimate=takes(8),
         name="attention_forward")(lengths,starts,own,other)
-def attn_backward(lengths,starts,own,other,gout,out,lse):
-    H=NB//2
-    def full(*dims): return pl.BlockSpec(dims,lambda i:(0,)*len(dims))
-    return pl.pallas_call(backward_kernel,grid=(1,),
-        out_shape=(jax.ShapeDtypeStruct((H,E,B),bf16),jax.ShapeDtypeStruct((H,2*E,B),f32),jax.ShapeDtypeStruct((H,2*E,B),bf16)),
-        in_specs=[SM,SM,full(H,192,B),full(H,128,B),full(H,E,B),full(H,E,B),full(H,1,B)],out_specs=(full(H,E,B),full(H,128,B),full(H,128,B)),
-        scratch_shapes=[pltpu.VMEM((NB*B,E+16),bf16),pltpu.VMEM((E,NB*B),bf16),pltpu.VMEM((NB*B,E+16),bf16),pltpu.VMEM((NB*B,2*E),f32)],
+def attn_stage(own, other, lse):
+    half = NB // 2
+    outs = (
+        jax.ShapeDtypeStruct((NB * B, E + 16), bf16),
+        jax.ShapeDtypeStruct((E, NB * B), bf16),
+        jax.ShapeDtypeStruct((NB * B, E + 16), bf16),
+        jax.ShapeDtypeStruct((half, E + 16, B), bf16),
+        jax.ShapeDtypeStruct((half, B, 2 * E), bf16),
+    )
+    return pl.pallas_call(
+        stage_kernel,
+        out_shape=outs,
+        in_specs=[VM] * 3,
+        out_specs=(VM,) * 5,
+        compiler_params=pltpu.CompilerParams(vmem_limit_bytes=LIMIT),
+        cost_estimate=takes(1),
+        name="attention_stage",
+    )(own, other, lse)
+
+
+def attn_backward(lengths, starts, staged, gout, out):
+    half = NB // 2
+
+    def full(array):
+        return pl.BlockSpec(array.shape, lambda i: (0,) * len(array.shape))
+
+    outs = (
+        jax.ShapeDtypeStruct((half, E, B), bf16),
+        jax.ShapeDtypeStruct((half, 2 * E, B), f32),
+        jax.ShapeDtypeStruct((half, 2 * E, B), bf16),
+    )
+    return pl.pallas_call(
+        backward_kernel,
+        grid=(1,),
+        out_shape=outs,
+        in_specs=[SM, SM] + [full(x) for x in (*staged, gout, out)],
+        out_specs=tuple(full(x) for x in outs),
+        scratch_shapes=[
+            pltpu.VMEM((NB * B, 2 * E), f32),
+            pltpu.VMEM((half, E + 16, B), bf16),
+            pltpu.VMEM((half, B, 2 * E), bf16),
+            pltpu.VMEM((half, E, B), f32),
+        ],
         compiler_params=pltpu.CompilerParams(vmem_limit_bytes=LIMIT),
         cost_estimate=takes(26),
-        name="attention_backward")(lengths,starts,own,other,gout,far(out),lse)
+        name="attention_backward",
+    )(lengths, starts, *[far(x) for x in staged], gout, far(out))
 
 
 SPREAD = ("x", "y", "zh")
@@ -757,7 +846,7 @@
         ],
         out_specs=tall(2432),
         scratch_shapes=[pltpu.VMEM((512, 256), bf16)],
-        compiler_params=ALL,
+        compiler_params=ROOMY,
         cost_estimate=takes(4),
         name="qkv_core_sum",
     )(grads, far(own_n), sums, theirs, far(mine_p), theirs_p, rows)
@@ -871,7 +960,7 @@
         tokens[0],
         cotangent[0],
         scalars=1,
-        cost=2,
+        cost=300,
         scratch=[pltpu.VMEM((1024, 1024), bf16)],
     )
     own_q = after(own_q, inputs)
@@ -880,7 +969,7 @@
         qkv_kernel,
         "qkv",
         (shape(8, 192, 256), shape(256, 512), shape(256, 512), shape(8, 1024, kind=f32)),
-        far(inputs),
+        inputs,
         own_q,
         other_q,
         qv_bias,
@@ -891,9 +980,10 @@
     other = swap(own[:, 64:], "c")
     attended, attended_low, log_sum = attn_forward(seq_lengths, piece_starts, own, other)
     heads_all = exchange(attended_low.reshape(16, 64, 256), ("zh", "y", "tp"))
+    staged = attn_stage(own, other, log_sum)
     grad_act = grad_activated(grad_mlp, after(rest, attended_low))
     middle, normed_two, heads_out = attention_end(
-        heads_all, after(rest, grad_act), inputs, vectors
+        after(heads_all, staged[0], grad_act), rest, inputs, vectors
     )
     activated, grad_hidden, two_part = feed_forward(
         normed_two, grad_act, fc_bias.reshape(1, 2048), rest
@@ -923,7 +1013,7 @@
     mlp_swapped = swap(after(mlp_part, grad_mine), "tp")
 
     grad_query, grad_own, grad_other = attn_backward(
-        seq_lengths, piece_starts, own, other, grad_mine, attended, log_sum
+        seq_lengths, piece_starts, staged, grad_mine, attended
     )
     grad_other, mlp_swapped = lax.optimization_barrier((grad_other, mlp_swapped))
     grad_back = call(

time: 285 us -> 280 us (0.982)
  waiting for transfers between devices: 97 us -> 89.5 us
  starting transfers between devices: 41.1 us -> 44.3 us
    all_to_all x5, waiting for transfers between devices: 49.7 us -> 42.3 us  [exchange(): return lax.all_to_all(field, axes, split_axis=0, concat_axis=0, tiled=True)]
    pallas_call x1 -> x2, Pallas kernels: 18.3 us -> 16.8 us  [the longest x1 15.7 us: attn_backward(): pl.pallas_call(backward_kernel, grid=(1,), out_shape=outs, in_specs=[SM,...]
    unnamed x90 -> x84, local copies, waits for them, and re-layouts: 13.8 us -> 14.4 us
  transfers between devices with their start and end apart: 22 -> 22, of which waited for: 13 -> 12; matrix products, arithmetic and copies ran while one was open for 1% -> 1% of each run, Pallas kernels for 27% -> 27%
where the time goes in v1:
time: 280 us; the launch traced here: 278 us
  waiting for transfers between devices  89.5 us (32%)
  Pallas kernels  87.4 us (31%)
  starting transfers between devices  44.3 us (16%)
  blocking collectives  25.4 us (9%)
  local copies, waits for them, and re-layouts  17 us (6%)
  between operations  14.3 us (5%)
    ppermute x13, waiting for transfers between devices, swap(): return lax.ppermute(field, axis, [(0, 1), (1, 0)])  47.1 us
    all_to_all x5, waiting for transfers between devices, exchange(): return lax.all_to_all(field, axes, split_axis=0, concat_axis=0, tiled=True)  42.3 us
    pallas_call x13, Pallas kernels, call(): pl.pallas_call(kernel, grid=(1,), out_shape=outs, in_specs=[SM] * scalars...  29.5 us
    all_to_all x5, starting transfers between devices, exchange(): return lax.all_to_all(field, axes, split_axis=0, concat_axis=0, tiled=True)  28.7 us
    all_to_all x1, blocking collectives, exchange(): return lax.all_to_all(field, axes, split_axis=0, concat_axis=0, tiled=True)  25.4 us
    pallas_call x1, Pallas kernels, attn_backward(): pl.pallas_call(backward_kernel, grid=(1,), out_shape=outs, in_specs=[SM,...  15.7 us
    ppermute x13, starting transfers between devices, swap(): return lax.ppermute(field, axis, [(0, 1), (1, 0)])  15.5 us
    unnamed x84, local copies, waits for them, and re-layouts  14.4 us
  transfers between devices with their start and end apart: 22, of which 12 were waited for; matrix products, arithmetic and copies ran while one was open for 1% of the time, Pallas kernels for 27%

profile of v1, /device:TPU:0, one launch (start us, length us, event | category | flops | bytes accessed | tf_op | source)
XLA Modules:
  0.0 277.9 jit_solution(1581280987801855204)
XLA Ops:
  9.7 4.0 %collective-permute-start.2 = (bf16[16,4608]{1,0:T(8,128)(2,1)S(1)}, bf16[16,4608]{1,0:T(8,128)(2,1)S(1)}, u32[]{:S(2)}, u32[]{:S(2)}) collective-permute-start(bf16[16,4608]{1,0:T(8,128)(2,1)S(1)} %rest_payload.1.mine_ref), channel_id=1, source_target_pairs={{0,16},{16,0},{1,17},{17,1},{2,18},{18,2},{3,19},{19,3},{4,20},{20... | collective-permute-start | bytes 442376 | tf_op jit(solution)/shard_map/ppermute | solution.py:379
  13.8 1.0 collective-permute-start.3
  14.9 4.3 %weights_payload.1 = bf16[32,16,1664]{2,1,0:T(8,128)(2,1)} custom-call(bf16[16,3,512]{2,1,0:T(4,128)(2,1)S(1)} %copy.31.qkv_ref, bf16[1,16]{1,0:T(2,128)(2,1)S(1)} %bitcast.36, bf16[1,16]{1,0:T(2,128)(2,1)S(1)} %bitcast.37, bf16[1,16]{1,0:T(2,128)(2,1)S(1)} %bitcast.38, bf16[1,16]{1,0:T(2,128)(2,1)S(1)} %bitcast.39, bf16[1,16]{1,0:T(2,128)(2,1)S(1)} %bitcast.40, ...), custom_call_target="tpu_custom_call" | custom-call | flops 1150000000 | bytes 1048576 | tf_op jit(solution)/shard_map/weights_payload/pallas_call | solution.py:408
  19.2 9.9 %all-to-all-start = ((bf16[32,16,1664]{2,1,0:T(8,128)(2,1)}), bf16[32,16,1664]{2,1,0:T(8,128)(2,1)}, u32[]{:S(2)}, u32[]{:S(2)}) async-start(bf16[32,16,1664]{2,1,0:T(8,128)(2,1)} %weights_payload.1), calls=%async_computation | async-start | bytes 3407872 | tf_op jit(solution)/shard_map/all_to_all | solution.py:383
  30.5 1.9 inputs.1
  33.2 22.3 %all-to-all-done = bf16[32,16,1664]{2,1,0:T(8,128)(2,1)} async-done(((bf16[32,16,1664]{2,1,0:T(8,128)(2,1)}), bf16[32,16,1664]{2,1,0:T(8,128)(2,1)}, u32[]{:S(2)}, u32[]{:S(2)}) %all-to-all-start) | async-done | bytes 1703968 | tf_op jit(solution)/shard_map/all_to_all | solution.py:383
  55.6 3.8 %collective-permute-done.other_ref = bf16[512,1664]{1,0:T(8,128)(2,1)S(1)} collective-permute-done((bf16[512,1664]{1,0:T(8,128)(2,1)}, bf16[512,1664]{1,0:T(8,128)(2,1)S(1)}, u32[]{:S(2)}, u32[]{:S(2)}) %collective-permute-start) | collective-permute-done | bytes 1703968 | tf_op jit(solution)/shard_map/ppermute | solution.py:379
  59.4 3.8 %qkv.1 = (bf16[8,192,256]{2,1,0:T(8,128)(2,1)S(1)}, bf16[256,512]{1,0:T(8,128)(2,1)S(1)}, bf16[256,512]{1,0:T(8,128)(2,1)S(1)}, f32[8,1024]{1,0:T(8,128)S(1)}) custom-call(bf16[256,1024]{1,0:T(8,128)(2,1)S(1)} %get-tuple-element.77.inputs_ref, bf16[512,1664]{1,0:T(8,128)(2,1)} %bitcast.8.own_ref, bf16[512,1664]{1,0:T(8,128)(2,1)S(1)} %collective-permute-done.other_ref, ...), custom_call_target="tpu_custom_call" | custom-call | flops 3449999872 | bytes 1048576 | tf_op jit(solution)/shard_map/qkv/pallas_call | solution.py:408
  63.9 25.4 %all_to_all.30.own_ref = bf16[8,192,256]{2,1,0:T(8,128)(2,1)S(1)} all-to-all(bf16[8,192,256]{2,1,0:T(8,128)(2,1)S(1)} %get-tuple-element.79), channel_id=1, replica_groups=mesh['x'=4,'zh'=2,'y'=4,'c'=2,'tp'=2] {'zh','y'}, dimensions={0} | all-to-all | bytes 1572864 | tf_op jit(solution)/shard_map/all_to_all | solution.py:383
  89.4 2.0 collective-permute-done.1.other_ref
  91.4 9.2 %attention_forward.1 = (f32[8,64,256]{2,1,0:T(8,128)S(1)}, bf16[8,2,64,256]{3,2,1,0:T(8,128)(2,1)}, f32[8,1,256]{2,1,0:T(1,128)S(1)}) custom-call(s32[4]{0:T(128)S(1)} %copy-done.20, s32[1,2]{1,0:T(1,128)S(1)} %copy-done.19, bf16[8,192,256]{2,1,0:T(8,128)(2,1)S(1)} %all_to_all.30.own_ref, bf16[8,128,256]{2,1,0:T(8,128)(2,1)S(1)} %collective-permute-done.1.other_ref), custom_call_target="tpu_custom_call" | custom-call | flops 9200000000 | bytes 1048576 | tf_op jit(solution)/shard_map/attention_forward/pallas_call | solution.py:302
  100.7 5.2 %all-to-all-start.2 = ((bf16[16,64,256]{2,1,0:T(8,128)(2,1)}), bf16[16,64,256]{2,1,0:T(8,128)(2,1)S(1)}, u32[]{:S(2)}, u32[]{:S(2)}) async-start(bf16[16,64,256]{2,1,0:T(8,128)(2,1)} %bitcast.9), calls=%async_computation.2 | async-start | bytes 1048576 | tf_op jit(solution)/shard_map/all_to_all | solution.py:383
  106.0 1.1 attention_stage.1
  107.1 1.0 copy-done.23
  108.1 1.0 copy-done.24
  110.7 4.2 %grad_act.1.gact_ref = f32[256,2048]{1,0:T(8,128)S(1)} custom-call(bf16[256,1024]{1,0:T(8,128)(2,1)} %copy-done.1, bf16[1024,5120]{1,0:T(8,128)(2,1)} %all-gather.2.cloned.1.call-done.weight_ref), custom_call_target="tpu_custom_call" | custom-call | flops 3449999872 | bytes 1048576 | tf_op jit(solution)/shard_map/grad_act/pallas_call | solution.py:569
  114.9 2.9 %all-to-all-done.2.heads_ref = bf16[16,64,256]{2,1,0:T(8,128)(2,1)S(1)} async-done(((bf16[16,64,256]{2,1,0:T(8,128)(2,1)}), bf16[16,64,256]{2,1,0:T(8,128)(2,1)S(1)}, u32[]{:S(2)}, u32[]{:S(2)}) %all-to-all-start.2) | async-done | bytes 524320 | tf_op jit(solution)/shard_map/all_to_all | solution.py:383
  117.8 2.7 attn_end.1
  120.6 6.5 %feed_forward.1 = (bf16[256,2048]{1,0:T(8,128)(2,1)S(1)}, bf16[256,2048]{1,0:T(8,128)(2,1)S(1)}, bf16[256,1024]{1,0:T(8,128)(2,1)S(1)}) custom-call(bf16[256,1024]{1,0:T(8,128)(2,1)S(1)} %get-tuple-element.89.n_ref, f32[256,2048]{1,0:T(8,128)S(1)} %grad_act.1.gact_ref, bf16[1,2048]{1,0:T(2,128)(2,1)S(1)} %reshape.71.bias_ref, ...), custom_call_target="tpu_custom_call" | custom-call | flops 6899999744 | bytes 1048576 | tf_op jit(solution)/shard_map/feed_forward/pallas_call | solution.py:611
  127.1 0.8 collective-permute-start.5
  127.9 10.2 %wide_grads.1 = (bf16[1024,4096]{1,0:T(8,128)(2,1)}, bf16[256,1024]{1,0:T(8,128)(2,1)S(1)}) custom-call(bf16[256,1024]{1,0:T(8,128)(2,1)S(1)} %get-tuple-element.89.n_ref, bf16[256,2048]{1,0:T(8,128)(2,1)S(1)} %get-tuple-element.90.gh_ref, bf16[256,1024]{1,0:T(8,128)(2,1)} %copy-done.1, bf16[256,2048]{1,0:T(8,128)(2,1)S(1)} %get-tuple-element.91.act_ref, ...), custom_call_target="tpu_custom_call" | custom-call | flops 9200000000 | bytes 1048576 | tf_op jit(solution)/shard_map/wide_grads/pallas_call | solution.py:649
  138.1 2.0 collective-permute-done.5.swapped_ref
  140.9 4.8 %middle_back.1 = (f32[256,1024]{1,0:T(8,128)}, bf16[256,1024]{1,0:T(8,128)(2,1)}, bf16[8,64,256]{2,1,0:T(8,128)(2,1)}, f32[8,1024]{1,0:T(8,128)}) custom-call(f32[256,1024]{1,0:T(8,128)} %copy-done.2, bf16[256,1024]{1,0:T(8,128)(2,1)} %copy-done.3, bf16[256,1024]{1,0:T(8,128)(2,1)} %copy-done.38, f32[8,1024]{1,0:T(8,128)} %copy-done.4, ...), custom_call_target="tpu_custom_call" | custom-call | flops 3449999872 | bytes 1048576 | tf_op jit(solution)/shard_map/middle_back/pallas_call | solution.py:692
  145.7 5.0 %all-to-all-start.3 = ((bf16[8,64,256]{2,1,0:T(8,128)(2,1)}), bf16[8,64,256]{2,1,0:T(8,128)(2,1)S(1)}, u32[]{:S(2)}, u32[]{:S(2)}) async-start(bf16[8,64,256]{2,1,0:T(8,128)(2,1)} %get-tuple-element.99), calls=%async_computation.3 | async-start | bytes 524288 | tf_op jit(solution)/shard_map/all_to_all | solution.py:383
  151.5 1.6 proj_grads.1
  153.9 5.6 %all-to-all-done.3.gout_ref = bf16[8,64,256]{2,1,0:T(8,128)(2,1)S(1)} async-done(((bf16[8,64,256]{2,1,0:T(8,128)(2,1)}), bf16[8,64,256]{2,1,0:T(8,128)(2,1)S(1)}, u32[]{:S(2)}, u32[]{:S(2)}) %all-to-all-start.3) | async-done | bytes 262176 | tf_op jit(solution)/shard_map/all_to_all | solution.py:383
  160.2 15.7 %attention_backward.1 = (bf16[8,64,256]{2,1,0:T(8,128)(2,1)S(1)}, f32[8,128,256]{2,1,0:T(8,128)S(1)}, bf16[8,128,256]{2,1,0:T(8,128)(2,1)S(1)}) custom-call(s32[4]{0:T(128)S(1)} %copy-done.20, s32[1,2]{1,0:T(1,128)S(1)} %copy-done.19, bf16[4096,80]{1,0:T(8,128)(2,1)} %copy-done.23, bf16[64,4096]{1,0:T(8,128)(2,1)} %copy-done.25, ...), custom_call_target="tpu_custom_call" | custom-call | flops 29899999232 | bytes 1048576 | tf_op jit(solution)/shard_map/attention_backward/pallas_call | solution.py:340
  176.0 1.9 collective-permute-done.7.other_ref
  177.9 1.0 merge.1
  178.9 4.2 %all-to-all-start.4 = ((bf16[8,192,256]{2,1,0:T(8,128)(2,1)}), bf16[8,192,256]{2,1,0:T(8,128)(2,1)}, u32[]{:S(2)}, u32[]{:S(2)}) async-start(bf16[8,192,256]{2,1,0:T(8,128)(2,1)} %merge.1), calls=%async_computation.4 | async-start | bytes 1572864 | tf_op jit(solution)/shard_map/all_to_all | solution.py:383
  183.2 3.4 %final.1 = (bf16[256,1024]{1,0:T(8,128)(2,1)}, f32[1,128]{1,0:T(1,128)S(1)}) custom-call(s32[4]{0:T(128)S(1)} %copy-done.20, bf16[256,1024]{1,0:T(8,128)(2,1)} %copy-done.21, f32[256,1024]{1,0:T(8,128)} %copy-done.2, bf16[256,1024]{1,0:T(8,128)(2,1)S(1)} %get-tuple-element.109.mine_ref, bf16[256,1024]{1,0:T(8,128)(2,1)S(1)} %collective-permute-done.6.swapped_ref, ...), custom_call_target="tpu_custom_call" | custom-call | flops 3449999872 | bytes 1048576 | tf_op jit(solution)/shard_map/final/pallas_call | solution.py:408
  186.6 11.5 %all-to-all-done.4.gback_ref = bf16[8,192,256]{2,1,0:T(8,128)(2,1)} async-done(((bf16[8,192,256]{2,1,0:T(8,128)(2,1)}), bf16[8,192,256]{2,1,0:T(8,128)(2,1)}, u32[]{:S(2)}, u32[]{:S(2)}) %all-to-all-start.4) | async-done | bytes 786464 | tf_op jit(solution)/shard_map/all_to_all | solution.py:383
  198.1 6.4 %back.1 = (bf16[128,1024]{1,0:T(8,128)(2,1)}, bf16[128,1024]{1,0:T(8,128)(2,1)}, f32[8,512]{1,0:T(8,128)}, bf16[512,1920]{1,0:T(8,128)(2,1)}, bf16[1536,256]{1,0:T(8,128)(2,1)}, /*index=5*/bf16[2,16,128]{2,1,0:T(8,128)(2,1)}) custom-call(bf16[8,192,256]{2,1,0:T(8,128)(2,1)} %all-to-all-done.4.gback_ref, bf16[512,1664]{1,0:T(8,128)(2,1)} %bitcast.8.own_ref, ...), custom_call_target="tpu_custom_call" | custom-call | flops 5750000128 | bytes 1048576 | tf_op jit(solution)/shard_map/back/pallas_call | solution.py:408
  205.4 1.4 collective-permute-start.8
  206.8 7.1 %collective-permute-done.8.swapped_ref = bf16[128,1024]{1,0:T(8,128)(2,1)S(1)} collective-permute-done((bf16[128,1024]{1,0:T(8,128)(2,1)}, bf16[128,1024]{1,0:T(8,128)(2,1)S(1)}, u32[]{:S(2)}, u32[]{:S(2)}) %collective-permute-start.8) | collective-permute-done | bytes 262176 | tf_op jit(solution)/shard_map/ppermute | solution.py:379
  213.9 1.1 copy-done.29
  216.4 3.5 %qkv_core_sum.1 = bf16[512,2432]{1,0:T(8,128)(2,1)S(1)} custom-call(bf16[1536,256]{1,0:T(8,128)(2,1)S(1)} %copy-done.29, bf16[256,512]{1,0:T(8,128)(2,1)} %copy-done.32, bf16[2,16,128]{2,1,0:T(8,128)(2,1)S(1)} %copy-done.36, bf16[512,1920]{1,0:T(8,128)(2,1)S(1)} %collective-permute-done.10.b_ref, bf16[512,640]{1,0:T(8,128)(2,1)} %copy-done.28, ...), custom_call_target="tpu_custom_call" | custom-call | flops 4600000000 | bytes 1048576 | tf_op jit(solution)/shard_map/qkv_core_sum/pallas_call | solution.py:834
  219.9 1.4 copy-done
  221.3 4.3 %all-to-all-start.5 = ((bf16[32,16,2432]{2,1,0:T(8,128)(2,1)}), bf16[32,16,2432]{2,1,0:T(8,128)(2,1)S(1)}, u32[]{:S(2)}, u32[]{:S(2)}) async-start(bf16[32,16,2432]{2,1,0:T(8,128)(2,1)} %bitcast.32), calls=%async_computation.5 | async-start | bytes 4980736 | tf_op jit(solution)/shard_map/all_to_all | solution.py:383
  225.6 2.5 end.1.mine_ref
  228.2 1.4 collective-permute-start.9
  229.6 1.0 constant_dynamic-slice_fusion
  230.6 3.9 %collective-permute-start.12 = (bf16[16,4096]{1,0:T(8,128)(2,1)S(1)}, bf16[16,4096]{1,0:T(8,128)(2,1)S(1)}, u32[]{:S(2)}, u32[]{:S(2)}) collective-permute-start(bf16[16,4096]{1,0:T(8,128)(2,1)S(1)} %get-tuple-element.154), channel_id=1, source_target_pairs={{0,16},{16,0},{1,17},{17,1},{2,18},{18,2},{3,19},{19,3},{4,20},{20... | collective-permute-start | bytes 393224 | tf_op jit(solution)/shard_map/ppermute | solution.py:379
  234.5 26.0 %collective-permute-done.9.theirs_ref = bf16[128,1024]{1,0:T(8,128)(2,1)S(1)} collective-permute-done((bf16[128,1024]{1,0:T(8,128)(2,1)S(1)}, bf16[128,1024]{1,0:T(8,128)(2,1)S(1)}, u32[]{:S(2)}, u32[]{:S(2)}) %collective-permute-start.9) | collective-permute-done | bytes 262176 | tf_op jit(solution)/shard_map/ppermute | solution.py:379
  261.3 2.8 collective-permute-done.12.theirs_ref
  265.4 1.3 total_qkv.1
  267.2 1.3 collective-permute-start.13
  269.2 1.6 collective-permute-done.13
  (115 shorter events, 16.5 us)
Async XLA Ops:
  8.9 5.9 %copy-start.39 = (bf16[16,3,512]{2,0,1:T(8,128)(2,1)S(1)}, bf16[16,3,512]{2,0,1:T(8,128)(2,1)}, u32[]{:S(2)}) copy-start(bf16[16,3,512]{2,0,1:T(8,128)(2,1)} %param.19) | copy-start | bytes 147460
  8.9 6.0 %copy-start.13 = (bf16[16]{0:T(256)(128)(2,1)S(1)}, bf16[16]{0:T(256)(128)(2,1)}, u32[]{:S(2)}) copy-start(bf16[16]{0:T(256)(128)(2,1)} %param.17) | copy-start | bytes 100
  8.9 6.0 %copy-start.14 = (bf16[16]{0:T(256)(128)(2,1)S(1)}, bf16[16]{0:T(256)(128)(2,1)}, u32[]{:S(2)}) copy-start(bf16[16]{0:T(256)(128)(2,1)} %param.18) | copy-start | bytes 100
  8.9 6.0 %copy-start.15 = (bf16[16]{0:T(256)(128)(2,1)S(1)}, bf16[16]{0:T(256)(128)(2,1)}, u32[]{:S(2)}) copy-start(bf16[16]{0:T(256)(128)(2,1)} %param.22) | copy-start | bytes 100
  8.9 6.0 %copy-start.16 = (bf16[16]{0:T(256)(128)(2,1)S(1)}, bf16[16]{0:T(256)(128)(2,1)}, u32[]{:S(2)}) copy-start(bf16[16]{0:T(256)(128)(2,1)} %param.23) | copy-start | bytes 100
  8.9 6.0 %copy-start.17 = (bf16[16]{0:T(256)(128)(2,1)S(1)}, bf16[16]{0:T(256)(128)(2,1)}, u32[]{:S(2)}) copy-start(bf16[16]{0:T(256)(128)(2,1)} %param.24) | copy-start | bytes 100
  8.9 6.0 %copy-start.18 = (bf16[16]{0:T(256)(128)(2,1)S(1)}, bf16[16]{0:T(256)(128)(2,1)}, u32[]{:S(2)}) copy-start(bf16[16]{0:T(256)(128)(2,1)} %param.28) | copy-start | bytes 100
  9.7 19.6 %collective-permute-start.2 = (bf16[16,4608]{1,0:T(8,128)(2,1)S(1)}, bf16[16,4608]{1,0:T(8,128)(2,1)S(1)}, u32[]{:S(2)}, u32[]{:S(2)}) collective-permute-start(bf16[16,4608]{1,0:T(8,128)(2,1)S(1)} %rest_payload.1.mine_ref), channel_id=1, source_target_pairs={{0,16},{16,0},{1,17},{17,1},{2,18},{18,2},{3,19},{19,3},{4,20},{20... | collective-permute-start | bytes 442376 | tf_op jit(solution)/shard_map/ppermute | solution.py:379
  13.8 15.5 %collective-permute-start.3 = (bf16[16,512]{1,0:T(8,128)(2,1)}, bf16[16,512]{1,0:T(8,128)(2,1)S(1)}, u32[]{:S(2)}, u32[]{:S(2)}) collective-permute-start(bf16[16,512]{1,0:T(8,128)(2,1)} %bitcast.10.proj_ref), channel_id=1, source_target_pairs={{0,1},{1,0},{2,3},{3,2},{4,5},{5,4},{6,7},{7,6},{8,9},{9,8},{10,11... | collective-permute-start | bytes 49160 | tf_op jit(solution)/shard_map/ppermute | solution.py:379
  14.8 14.5 %collective-permute-start.4 = (bf16[16,512]{1,0:T(8,128)(2,1)}, bf16[16,512]{1,0:T(8,128)(2,1)S(1)}, u32[]{:S(2)}, u32[]{:S(2)}) collective-permute-start(bf16[16,512]{1,0:T(8,128)(2,1)} %bitcast.10.proj_ref), channel_id=1, source_target_pairs={{0,17},{1,16},{16,1},{17,0},{2,19},{3,18},{18,3},{19,2},{4,21},{5,... | collective-permute-start | bytes 49160 | tf_op jit(solution)/shard_map/ppermute | solution.py:951
  19.2 36.4 %all-to-all-start = ((bf16[32,16,1664]{2,1,0:T(8,128)(2,1)}), bf16[32,16,1664]{2,1,0:T(8,128)(2,1)}, u32[]{:S(2)}, u32[]{:S(2)}) async-start(bf16[32,16,1664]{2,1,0:T(8,128)(2,1)} %weights_payload.1), calls=%async_computation | async-start | bytes 3407872 | tf_op jit(solution)/shard_map/all_to_all | solution.py:383
  29.2 1.3 copy-start.8
  29.2 1.3 copy-start.20
  29.2 81.5 %all-gather.2.cloned.1.call-start = ((), (), s32[]{:S(2)}) async-start(), calls=%async_computation.8 | async-start | bytes 10813440 | tf_op jit(solution)/shard_map/all_gather | solution.py:953
  30.5 28.9 %copy-start.12 = (bf16[2,512]{1,0:T(2,128)(2,1)S(1)}, bf16[2,512]{1,0:T(2,128)(2,1)}, u32[]{:S(2)}) copy-start(bf16[2,512]{1,0:T(2,128)(2,1)} %bias_ref.1) | copy-start | bytes 6148
  33.2 30.0 %copy-start.21 = (bf16[256,1024]{1,0:T(8,128)(2,1)}, bf16[256,1024]{1,0:T(8,128)(2,1)S(1)}, u32[]{:S(2)}) copy-start(bf16[256,1024]{1,0:T(8,128)(2,1)S(1)} %get-tuple-element.77.inputs_ref) | copy-start | bytes 1572868
  55.6 3.8 %collective-permute-start = (bf16[512,1664]{1,0:T(8,128)(2,1)}, bf16[512,1664]{1,0:T(8,128)(2,1)S(1)}, u32[]{:S(2)}, u32[]{:S(2)}) collective-permute-start(bf16[512,1664]{1,0:T(8,128)(2,1)} %bitcast.8.own_ref), channel_id=1, source_target_pairs={{0,2},{2,0},{1,3},{3,1},{4,6},{6,4},{5,7},{7,5},{8,10},{10,8},{9,1... | collective-permute-start | bytes 5111816 | tf_op jit(solution)/shard_map/ppermute | solution.py:379
  59.4 3.8 %copy-start.6 = (bf16[512,1664]{1,0:T(8,128)(2,1)}, bf16[512,1664]{1,0:T(8,128)(2,1)S(1)}, u32[]{:S(2)}) copy-start(bf16[512,1664]{1,0:T(8,128)(2,1)S(1)} %collective-permute-done.other_ref) | copy-start | bytes 5111812
  63.9 36.7 %copy-start.33 = (bf16[256,512]{1,0:T(8,128)(2,1)}, bf16[256,512]{1,0:T(8,128)(2,1)S(1)}, u32[]{:S(2)}) copy-start(bf16[256,512]{1,0:T(8,128)(2,1)S(1)} %get-tuple-element.115.other_n_ref) | copy-start | bytes 786436
  63.9 53.9 %copy-start.4 = (f32[8,1024]{1,0:T(8,128)}, f32[8,1024]{1,0:T(8,128)S(1)}, u32[]{:S(2)}) copy-start(f32[8,1024]{1,0:T(8,128)S(1)} %get-tuple-element.87.vectors_ref) | copy-start | bytes 98308
  63.9 27.5 %copy-start.19 = (s32[1,2]{1,0:T(1,128)S(1)}, s32[1,2]{1,0:T(1,128)}, u32[]{:S(2)}) copy-start(s32[1,2]{1,0:T(1,128)} %starts_ref.3) | copy-start | bytes 28
  89.3 16.6 %copy-start.40 = (bf16[2048]{0:T(1024)(128)(2,1)S(1)}, bf16[2048]{0:T(1024)(128)(2,1)}, u32[]{:S(2)}) copy-start(bf16[2048]{0:T(1024)(128)(2,1)} %param.26) | copy-start | bytes 12292
  89.3 2.1 collective-permute-start.1
  100.7 5.3 %copy-start.34 = (f32[8,64,256]{2,1,0:T(8,128)}, f32[8,64,256]{2,1,0:T(8,128)S(1)}, u32[]{:S(2)}) copy-start(f32[8,64,256]{2,1,0:T(8,128)S(1)} %get-tuple-element.105.out_ref) | copy-start | bytes 1572868
  100.7 17.2 %all-to-all-start.2 = ((bf16[16,64,256]{2,1,0:T(8,128)(2,1)}), bf16[16,64,256]{2,1,0:T(8,128)(2,1)S(1)}, u32[]{:S(2)}, u32[]{:S(2)}) async-start(bf16[16,64,256]{2,1,0:T(8,128)(2,1)} %bitcast.9), calls=%async_computation.2 | async-start | bytes 1048576 | tf_op jit(solution)/shard_map/all_to_all | solution.py:383
  105.9 98.6 %reduce-scatter.3.cloned.1.call-start = ((), (), s32[]{:S(2)}) async-start(), calls=%async_computation.9 | async-start | bytes 9437184 | tf_op jit(solution)/shard_map/reduce_scatter | solution.py:993
  110.7 4.3 %copy-start.27 = (bf16[8,80,256]{2,1,0:T(8,128)(2,1)}, bf16[8,80,256]{2,1,0:T(8,128)(2,1)S(1)}, u32[]{:S(2)}) copy-start(bf16[8,80,256]{2,1,0:T(8,128)(2,1)S(1)} %get-tuple-element.95.query_ref) | copy-start | bytes 983044
  120.5 6.5 %copy-start.2 = (f32[256,1024]{1,0:T(8,128)}, f32[256,1024]{1,0:T(8,128)S(1)}, u32[]{:S(2)}) copy-start(f32[256,1024]{1,0:T(8,128)S(1)} %get-tuple-element.88.middle_ref) | copy-start | bytes 3145732
  120.6 6.5 %copy-start.22 = (bf16[512,256]{1,0:T(8,128)(2,1)}, bf16[512,256]{1,0:T(8,128)(2,1)S(1)}, u32[]{:S(2)}) copy-start(bf16[512,256]{1,0:T(8,128)(2,1)S(1)} %get-tuple-element.101.heads_ref) | copy-start | bytes 786436
  127.0 11.0 %copy-start.3 = (bf16[256,1024]{1,0:T(8,128)(2,1)}, bf16[256,1024]{1,0:T(8,128)(2,1)S(1)}, u32[]{:S(2)}) copy-start(bf16[256,1024]{1,0:T(8,128)(2,1)S(1)} %get-tuple-element.97.mine_ref) | copy-start | bytes 1572868
  127.1 11.0 %copy-start.31 = (bf16[256,2048]{1,0:T(8,128)(2,1)}, bf16[256,2048]{1,0:T(8,128)(2,1)S(1)}, u32[]{:S(2)}) copy-start(bf16[256,2048]{1,0:T(8,128)(2,1)S(1)} %get-tuple-element.90.gh_ref) | copy-start | bytes 3145732
  127.1 13.0 %collective-permute-start.5 = (bf16[256,1024]{1,0:T(8,128)(2,1)S(1)}, bf16[256,1024]{1,0:T(8,128)(2,1)S(1)}, u32[]{:S(2)}, u32[]{:S(2)}) collective-permute-start(bf16[256,1024]{1,0:T(8,128)(2,1)S(1)} %get-tuple-element.97.mine_ref), channel_id=1, source_target_pairs={{0,1},{1,0},{2,3},{3,2},{4,5},{5,4},{6,7},{7,6},{8,9},{9,8},{10,11... | collective-permute-start | bytes 1572872 | tf_op jit(solution)/shard_map/ppermute | solution.py:379
  145.7 13.8 %all-to-all-start.3 = ((bf16[8,64,256]{2,1,0:T(8,128)(2,1)}), bf16[8,64,256]{2,1,0:T(8,128)(2,1)S(1)}, u32[]{:S(2)}, u32[]{:S(2)}) async-start(bf16[8,64,256]{2,1,0:T(8,128)(2,1)} %get-tuple-element.99), calls=%async_computation.3 | async-start | bytes 524288 | tf_op jit(solution)/shard_map/all_to_all | solution.py:383
  159.5 16.3 %collective-permute-start.6 = (bf16[256,1024]{1,0:T(8,128)(2,1)S(1)}, bf16[256,1024]{1,0:T(8,128)(2,1)S(1)}, u32[]{:S(2)}, u32[]{:S(2)}) collective-permute-start(bf16[256,1024]{1,0:T(8,128)(2,1)S(1)} %get-tuple-element.109.mine_ref), channel_id=1, source_target_pairs={{0,1},{1,0},{2,3},{3,2},{4,5},{5,4},{6,7},{7,6},{8,9},{9,8},{10,11... | collective-permute-start | bytes 1572872 | tf_op jit(solution)/shard_map/ppermute | solution.py:379
  175.9 2.0 collective-permute-start.7
  177.9 5.3 %copy-start.5 = (f32[8,1024]{1,0:T(8,128)S(1)}, f32[8,1024]{1,0:T(8,128)}, u32[]{:S(2)}) copy-start(f32[8,1024]{1,0:T(8,128)} %copy-done.4) | copy-start | bytes 98308
  178.9 19.2 %all-to-all-start.4 = ((bf16[8,192,256]{2,1,0:T(8,128)(2,1)}), bf16[8,192,256]{2,1,0:T(8,128)(2,1)}, u32[]{:S(2)}, u32[]{:S(2)}) async-start(bf16[8,192,256]{2,1,0:T(8,128)(2,1)} %merge.1), calls=%async_computation.4 | async-start | bytes 1572864 | tf_op jit(solution)/shard_map/all_to_all | solution.py:383
  183.1 46.5 %reduce-scatter.5.cloned.1.call-start = ((), (), s32[]{:S(2)}) async-start(), calls=%async_computation.10 | async-start | bytes 1310720 | tf_op jit(solution)/shard_map/reduce_scatter | solution.py:1060
  186.6 11.5 %copy-start.37 = (f32[1,128]{1,0:T(1,128)}, f32[1,128]{1,0:T(1,128)S(1)}, u32[]{:S(2)}) copy-start(f32[1,128]{1,0:T(1,128)S(1)} %get-tuple-element.116.roots_ref) | copy-start | bytes 1540
  204.5 9.4 %collective-permute-start.10 = (bf16[512,1920]{1,0:T(8,128)(2,1)}, bf16[512,1920]{1,0:T(8,128)(2,1)S(1)}, u32[]{:S(2)}, u32[]{:S(2)}) collective-permute-start(bf16[512,1920]{1,0:T(8,128)(2,1)} %get-tuple-element.122), channel_id=1, source_target_pairs={{0,2},{2,0},{1,3},{3,1},{4,6},{6,4},{5,7},{7,5},{8,10},{10,8},{9,1... | collective-permute-start | bytes 5898248 | tf_op jit(solution)/shard_map/ppermute | solution.py:379
  204.6 9.3 %collective-permute-start.11 = (bf16[512,640]{1,0:T(8,128)(2,1)S(1)}, bf16[512,640]{1,0:T(8,128)(2,1)S(1)}, u32[]{:S(2)}, u32[]{:S(2)}) collective-permute-start(bf16[512,640]{1,0:T(8,128)(2,1)S(1)} %get-tuple-element.125), channel_id=1, source_target_pairs={{0,2},{2,0},{1,3},{3,1},{4,6},{6,4},{5,7},{7,5},{8,10},{10,8},{9,1... | collective-permute-start | bytes 1966088 | tf_op jit(solution)/shard_map/ppermute | solution.py:379
  205.4 8.5 %collective-permute-start.8 = (bf16[128,1024]{1,0:T(8,128)(2,1)}, bf16[128,1024]{1,0:T(8,128)(2,1)S(1)}, u32[]{:S(2)}, u32[]{:S(2)}) collective-permute-start(bf16[128,1024]{1,0:T(8,128)(2,1)} %get-tuple-element.118), channel_id=1, source_target_pairs={{0,1},{1,0},{2,3},{3,2},{4,5},{5,4},{6,7},{7,6},{8,9},{9,8},{10,11... | collective-permute-start | bytes 786440 | tf_op jit(solution)/shard_map/ppermute | solution.py:379
  219.9 1.4 copy-start
  221.3 4.3 %copy-start.30 = (bf16[128,1024]{1,0:T(8,128)(2,1)S(1)}, bf16[128,1024]{1,0:T(8,128)(2,1)}, u32[]{:S(2)}) copy-start(bf16[128,1024]{1,0:T(8,128)(2,1)} %get-tuple-element.117.mine_ref) | copy-start | bytes 786436
  221.3 43.4 %all-to-all-start.5 = ((bf16[32,16,2432]{2,1,0:T(8,128)(2,1)}), bf16[32,16,2432]{2,1,0:T(8,128)(2,1)S(1)}, u32[]{:S(2)}, u32[]{:S(2)}) async-start(bf16[32,16,2432]{2,1,0:T(8,128)(2,1)} %bitcast.32), calls=%async_computation.5 | async-start | bytes 4980736 | tf_op jit(solution)/shard_map/all_to_all | solution.py:383
  228.2 32.3 %collective-permute-start.9 = (bf16[128,1024]{1,0:T(8,128)(2,1)S(1)}, bf16[128,1024]{1,0:T(8,128)(2,1)S(1)}, u32[]{:S(2)}, u32[]{:S(2)}) collective-permute-start(bf16[128,1024]{1,0:T(8,128)(2,1)S(1)} %end.1.mine_ref), channel_id=1, source_target_pairs={{0,1},{1,0},{2,3},{3,2},{4,5},{5,4},{6,7},{7,6},{8,9},{9,8},{10,11... | collective-permute-start | bytes 786440 | tf_op jit(solution)/shard_map/ppermute | solution.py:379
  230.6 33.4 %collective-permute-start.12 = (bf16[16,4096]{1,0:T(8,128)(2,1)S(1)}, bf16[16,4096]{1,0:T(8,128)(2,1)S(1)}, u32[]{:S(2)}, u32[]{:S(2)}) collective-permute-start(bf16[16,4096]{1,0:T(8,128)(2,1)S(1)} %get-tuple-element.154), channel_id=1, source_target_pairs={{0,16},{16,0},{1,17},{17,1},{2,18},{18,2},{3,19},{19,3},{4,20},{20... | collective-permute-start | bytes 393224 | tf_op jit(solution)/shard_map/ppermute | solution.py:379
  267.2 3.6 %collective-permute-start.13 = (f32[2,16]{1,0:T(2,128)S(1)}, f32[2,16]{1,0:T(2,128)S(1)}, u32[]{:S(2)}, u32[]{:S(2)}) collective-permute-start(f32[2,16]{1,0:T(2,128)S(1)} %slice.28), channel_id=1, source_target_pairs={{0,1},{1,0},{2,3},{3,2},{4,5},{5,4},{6,7},{7,6},{8,9},{9,8},{10,11... | collective-permute-start | bytes 392 | tf_op jit(solution)/shard_map/ppermute | solution.py:379
  (15 other events, 12.8 us)
Sparse Core Ops, SparseCore 0:
  32.3 69.3 all-gather.1
  140.3 49.9 reduce-scatter.2
  204.7 19.6 reduce-scatter.4

commit v2 on v1

--- a/solution.py
+++ b/solution.py
@@ -558,7 +558,7 @@
         compiler_params=ROOMY,
         cost_estimate=takes(3),
         name="attn_end",
-    )(heads_all, far(rest), far(inputs), vectors)
+    )(heads_all, far(rest), far(inputs), far(vectors))
 
 
 def grad_act_kernel(gm_ref, weight_ref, out_ref):
@@ -703,7 +703,7 @@
         compiler_params=ALL,
         cost_estimate=takes(3),
         name="middle_back",
-    )(far(middle), mine, swapped, vectors, far(grad_mlp), far(rest))
+    )(*[far(x) for x in (middle, mine, swapped, vectors, grad_mlp, rest)])
 
 
 def put_block(ref, at, block):
@@ -846,10 +846,10 @@
         ],
         out_specs=tall(2432),
         scratch_shapes=[pltpu.VMEM((512, 256), bf16)],
-        compiler_params=ROOMY,
+        compiler_params=ALL,
         cost_estimate=takes(4),
         name="qkv_core_sum",
-    )(grads, far(own_n), sums, theirs, far(mine_p), theirs_p, rows)
+    )(*[far(x) for x in (grads, own_n, sums, theirs, mine_p, theirs_p, rows)])
 
 
 def end_kernel(inputs_ref, gmid_ref, mine_ref, swapped_ref, vectors_ref, out_ref, order_ref):
@@ -872,7 +872,7 @@
     for k in range(1, 32):
         total = total + got_ref[k].astype(f32)
     for c in range(3):
-        qkv_ref[:, c, :] = total[:, 512 * c : 512 * (c + 1)]
+        qkv_ref[c] = total[:, 512 * c : 512 * (c + 1)]
     for k in range(2):
         for r in range(4):
             row = 8 * k + r
@@ -1080,9 +1080,7 @@
         cost=2,
         scratch=[pltpu.VMEM((1024, 1024), bf16)],
     )
-    grad_tokens = call(
-        join_kernel, "join", shape(256, 1024), half_tokens, swap(half_tokens, "tp")
-    )
+    half_swapped = swap(half_tokens, "tp")
     zh = lax.axis_index("zh")
     keep = lax.dynamic_slice_in_dim(wide, zh * 16, 16, 0)
     send = lax.dynamic_slice_in_dim(wide, 16 - zh * 16, 16, 0)
@@ -1093,14 +1091,14 @@
         keep,
         swap(send, "zh"),        cost=14,
     )
-    got_q = after(got_q, grad_fc, grad_tokens)
+    got_q = after(got_q, grad_fc, half_swapped)
     cols = total_cols(got_q)
     ln1 = cols[4:6]
     grad_qkv, grad_proj, bias_sums, fc_sums, roots = call(
         total_qkv_kernel,
         "total_qkv",
         (
-            shape(16, 3, 512, kind=f32),
+            shape(3, 16, 512, kind=f32),
             shape(16, 512, kind=f32),
             shape(2, 512, kind=f32),
             shape(16, 128, kind=f32),
@@ -1110,13 +1108,18 @@
         after(got_q, cols),
         scalars=1,
     )
-    ln1 = ln1 + swap(ln1, "tp")
+    ln1_swapped = swap(ln1, "tp")
+    half_swapped = after(half_swapped, grad_qkv)
+    grad_tokens = call(
+        join_kernel, "join", shape(256, 1024), half_tokens, half_swapped
+    )
+    ln1 = ln1 + ln1_swapped
     return (
         layer_out[None],
         grad_tokens[None],
         ln1[0],
         ln1[1],
-        grad_qkv,
+        grad_qkv.transpose(1, 0, 2),
         bias_sums,
         grad_proj.T,
         cols[0],

time: 280 us -> 274 us (0.979)
  local copies, waits for them, and re-layouts: 17 us -> 12.5 us
    unnamed x84 -> x77, local copies, waits for them, and re-layouts: 14.4 us -> 9.87 us
  transfers between devices with their start and end apart: 22 -> 22, of which waited for: 12 -> 12; matrix products, arithmetic and copies ran while one was open for 1% -> 1% of each run, Pallas kernels for 27% -> 29%
where the time goes in v2:
time: 274 us; the launch traced here: 273 us
  Pallas kernels  89.9 us (33%)
  waiting for transfers between devices  87.8 us (32%)
  starting transfers between devices  43 us (16%)
  blocking collectives  25.1 us (9%)
  between operations  14.3 us (5%)
  local copies, waits for them, and re-layouts  12.5 us (5%)
    ppermute x13, waiting for transfers between devices, swap(): return lax.ppermute(field, axis, [(0, 1), (1, 0)])  45.1 us
    all_to_all x5, waiting for transfers between devices, exchange(): return lax.all_to_all(field, axes, split_axis=0, concat_axis=0, tiled=True)  42.6 us
    pallas_call x13, Pallas kernels, call(): pl.pallas_call(kernel, grid=(1,), out_shape=outs, in_specs=[SM] * scalars...  29.7 us
    all_to_all x5, starting transfers between devices, exchange(): return lax.all_to_all(field, axes, split_axis=0, concat_axis=0, tiled=True)  28.6 us
    all_to_all x1, blocking collectives, exchange(): return lax.all_to_all(field, axes, split_axis=0, concat_axis=0, tiled=True)  25.1 us
    pallas_call x1, Pallas kernels, attn_backward(): pl.pallas_call(backward_kernel, grid=(1,), out_shape=outs, in_specs=[SM,...  15.7 us
    ppermute x13, starting transfers between devices, swap(): return lax.ppermute(field, axis, [(0, 1), (1, 0)])  14.2 us
    pallas_call x1, Pallas kernels, wide_grads(): pl.pallas_call(wide_kernel, grid=(8,), out_shape=(shape(1024, 4096), shap...  10.3 us
  transfers between devices with their start and end apart: 22, of which 12 were waited for; matrix products, arithmetic and copies ran while one was open for 1% of the time, Pallas kernels for 29%

profile of v2, /device:TPU:0, one launch (start us, length us, event | category | flops | bytes accessed | tf_op | source)
XLA Modules:
  0.0 272.6 jit_solution(15380680783436172083)
XLA Ops:
  7.2 0.8 copy-done.8
  8.0 0.8 copy-done.9
  9.7 4.0 %collective-permute-start.2 = (bf16[16,4608]{1,0:T(8,128)(2,1)S(1)}, bf16[16,4608]{1,0:T(8,128)(2,1)S(1)}, u32[]{:S(2)}, u32[]{:S(2)}) collective-permute-start(bf16[16,4608]{1,0:T(8,128)(2,1)S(1)} %rest_payload.1.mine_ref), channel_id=1, source_target_pairs={{0,16},{16,0},{1,17},{17,1},{2,18},{18,2},{3,19},{19,3},{4,20},{20... | collective-permute-start | bytes 442376 | tf_op jit(solution)/shard_map/ppermute | solution.py:379
  13.8 1.0 collective-permute-start.3
  14.9 4.3 %weights_payload.1 = bf16[32,16,1664]{2,1,0:T(8,128)(2,1)} custom-call(bf16[16,3,512]{2,1,0:T(4,128)(2,1)S(1)} %copy.31.qkv_ref, bf16[1,16]{1,0:T(2,128)(2,1)S(1)} %bitcast.36, bf16[1,16]{1,0:T(2,128)(2,1)S(1)} %bitcast.37, bf16[1,16]{1,0:T(2,128)(2,1)S(1)} %bitcast.38, bf16[1,16]{1,0:T(2,128)(2,1)S(1)} %bitcast.39, bf16[1,16]{1,0:T(2,128)(2,1)S(1)} %bitcast.40, ...), custom_call_target="tpu_custom_call" | custom-call | flops 1150000000 | bytes 1048576 | tf_op jit(solution)/shard_map/weights_payload/pallas_call | solution.py:408
  19.2 9.9 %all-to-all-start = ((bf16[32,16,1664]{2,1,0:T(8,128)(2,1)}), bf16[32,16,1664]{2,1,0:T(8,128)(2,1)}, u32[]{:S(2)}, u32[]{:S(2)}) async-start(bf16[32,16,1664]{2,1,0:T(8,128)(2,1)} %weights_payload.1), calls=%async_computation | async-start | bytes 3407872 | tf_op jit(solution)/shard_map/all_to_all | solution.py:383
  30.5 1.9 inputs.1
  33.2 22.4 %all-to-all-done = bf16[32,16,1664]{2,1,0:T(8,128)(2,1)} async-done(((bf16[32,16,1664]{2,1,0:T(8,128)(2,1)}), bf16[32,16,1664]{2,1,0:T(8,128)(2,1)}, u32[]{:S(2)}, u32[]{:S(2)}) %all-to-all-start) | async-done | bytes 1703968 | tf_op jit(solution)/shard_map/all_to_all | solution.py:383
  55.6 3.8 %collective-permute-done.other_ref = bf16[512,1664]{1,0:T(8,128)(2,1)S(1)} collective-permute-done((bf16[512,1664]{1,0:T(8,128)(2,1)}, bf16[512,1664]{1,0:T(8,128)(2,1)S(1)}, u32[]{:S(2)}, u32[]{:S(2)}) %collective-permute-start) | collective-permute-done | bytes 1703968 | tf_op jit(solution)/shard_map/ppermute | solution.py:379
  59.4 3.8 %qkv.1 = (bf16[8,192,256]{2,1,0:T(8,128)(2,1)S(1)}, bf16[256,512]{1,0:T(8,128)(2,1)S(1)}, bf16[256,512]{1,0:T(8,128)(2,1)S(1)}, f32[8,1024]{1,0:T(8,128)S(1)}) custom-call(bf16[256,1024]{1,0:T(8,128)(2,1)S(1)} %get-tuple-element.78.inputs_ref, bf16[512,1664]{1,0:T(8,128)(2,1)} %bitcast.8.own_ref, bf16[512,1664]{1,0:T(8,128)(2,1)S(1)} %collective-permute-done.other_ref, ...), custom_call_target="tpu_custom_call" | custom-call | flops 3449999872 | bytes 1048576 | tf_op jit(solution)/shard_map/qkv/pallas_call | solution.py:408
  63.3 25.1 %all_to_all.30.own_ref = bf16[8,192,256]{2,1,0:T(8,128)(2,1)S(1)} all-to-all(bf16[8,192,256]{2,1,0:T(8,128)(2,1)S(1)} %get-tuple-element.80), channel_id=1, replica_groups=mesh['x'=4,'zh'=2,'y'=4,'c'=2,'tp'=2] {'zh','y'}, dimensions={0} | all-to-all | bytes 1572864 | tf_op jit(solution)/shard_map/all_to_all | solution.py:383
  88.5 1.9 collective-permute-done.1.other_ref
  90.4 9.2 %attention_forward.1 = (f32[8,64,256]{2,1,0:T(8,128)S(1)}, bf16[8,2,64,256]{3,2,1,0:T(8,128)(2,1)}, f32[8,1,256]{2,1,0:T(1,128)S(1)}) custom-call(s32[4]{0:T(128)S(1)} %copy-done.19, s32[1,2]{1,0:T(1,128)S(1)} %copy-done.18, bf16[8,192,256]{2,1,0:T(8,128)(2,1)S(1)} %all_to_all.30.own_ref, bf16[8,128,256]{2,1,0:T(8,128)(2,1)S(1)} %collective-permute-done.1.other_ref), custom_call_target="tpu_custom_call" | custom-call | flops 9200000000 | bytes 1048576 | tf_op jit(solution)/shard_map/attention_forward/pallas_call | solution.py:302
  99.7 5.5 %all-to-all-start.2 = ((bf16[16,64,256]{2,1,0:T(8,128)(2,1)}), bf16[16,64,256]{2,1,0:T(8,128)(2,1)S(1)}, u32[]{:S(2)}, u32[]{:S(2)}) async-start(bf16[16,64,256]{2,1,0:T(8,128)(2,1)} %bitcast.9), calls=%async_computation.2 | async-start | bytes 1048576 | tf_op jit(solution)/shard_map/all_to_all | solution.py:383
  105.3 1.1 attention_stage.1
  106.4 1.0 copy-done.22
  107.4 1.0 copy-done.23
  108.4 0.8 copy-done.24
  110.0 4.2 %grad_act.1.gact_ref = f32[256,2048]{1,0:T(8,128)S(1)} custom-call(bf16[256,1024]{1,0:T(8,128)(2,1)} %copy-done, bf16[1024,5120]{1,0:T(8,128)(2,1)} %all-gather.2.cloned.1.call-done.weight_ref), custom_call_target="tpu_custom_call" | custom-call | flops 3449999872 | bytes 1048576 | tf_op jit(solution)/shard_map/grad_act/pallas_call | solution.py:569
  114.3 3.2 %all-to-all-done.2.heads_ref = bf16[16,64,256]{2,1,0:T(8,128)(2,1)S(1)} async-done(((bf16[16,64,256]{2,1,0:T(8,128)(2,1)}), bf16[16,64,256]{2,1,0:T(8,128)(2,1)S(1)}, u32[]{:S(2)}, u32[]{:S(2)}) %all-to-all-start.2) | async-done | bytes 524320 | tf_op jit(solution)/shard_map/all_to_all | solution.py:383
  117.5 2.8 %attn_end.1 = (f32[256,1024]{1,0:T(8,128)S(1)}, bf16[256,1024]{1,0:T(8,128)(2,1)S(1)}, bf16[512,256]{1,0:T(8,128)(2,1)S(1)}) custom-call(bf16[16,64,256]{2,1,0:T(8,128)(2,1)S(1)} %all-to-all-done.2.heads_ref, bf16[1024,5120]{1,0:T(8,128)(2,1)} %all-gather.2.cloned.1.call-done.weight_ref, bf16[256,1024]{1,0:T(8,128)(2,1)} %copy-done.20, f32[8,1024]{1,0:T(8,128)} %copy-done.3), custom_call_target="tpu_custom_call" | custom-call | flops 3449999872 | bytes 1048576 | tf_op jit(solution)/shard_map/attn_end/pallas_call | solution.py:546
  120.3 6.5 %feed_forward.1 = (bf16[256,2048]{1,0:T(8,128)(2,1)S(1)}, bf16[256,2048]{1,0:T(8,128)(2,1)S(1)}, bf16[256,1024]{1,0:T(8,128)(2,1)S(1)}) custom-call(bf16[256,1024]{1,0:T(8,128)(2,1)S(1)} %get-tuple-element.90.n_ref, f32[256,2048]{1,0:T(8,128)S(1)} %grad_act.1.gact_ref, bf16[1,2048]{1,0:T(2,128)(2,1)S(1)} %reshape.71.bias_ref, ...), custom_call_target="tpu_custom_call" | custom-call | flops 6899999744 | bytes 1048576 | tf_op jit(solution)/shard_map/feed_forward/pallas_call | solution.py:611
  127.7 10.3 %wide_grads.1 = (bf16[1024,4096]{1,0:T(8,128)(2,1)}, bf16[256,1024]{1,0:T(8,128)(2,1)S(1)}) custom-call(bf16[256,1024]{1,0:T(8,128)(2,1)S(1)} %get-tuple-element.90.n_ref, bf16[256,2048]{1,0:T(8,128)(2,1)S(1)} %get-tuple-element.91.gh_ref, bf16[256,1024]{1,0:T(8,128)(2,1)} %copy-done, bf16[256,2048]{1,0:T(8,128)(2,1)S(1)} %get-tuple-element.92.act_ref, ...), custom_call_target="tpu_custom_call" | custom-call | flops 9200000000 | bytes 1048576 | tf_op jit(solution)/shard_map/wide_grads/pallas_call | solution.py:649
  137.9 2.1 collective-permute-done.5.swapped_ref
  140.8 4.8 %middle_back.1 = (f32[256,1024]{1,0:T(8,128)}, bf16[256,1024]{1,0:T(8,128)(2,1)}, bf16[8,64,256]{2,1,0:T(8,128)(2,1)}, f32[8,1024]{1,0:T(8,128)}) custom-call(f32[256,1024]{1,0:T(8,128)} %copy-done.1, bf16[256,1024]{1,0:T(8,128)(2,1)} %copy-done.2, bf16[256,1024]{1,0:T(8,128)(2,1)} %copy-done.34, f32[8,1024]{1,0:T(8,128)} %copy-done.3, ...), custom_call_target="tpu_custom_call" | custom-call | flops 3449999872 | bytes 1048576 | tf_op jit(solution)/shard_map/middle_back/pallas_call | solution.py:692
  145.6 4.8 %all-to-all-start.3 = ((bf16[8,64,256]{2,1,0:T(8,128)(2,1)}), bf16[8,64,256]{2,1,0:T(8,128)(2,1)S(1)}, u32[]{:S(2)}, u32[]{:S(2)}) async-start(bf16[8,64,256]{2,1,0:T(8,128)(2,1)} %get-tuple-element.100), calls=%async_computation.3 | async-start | bytes 524288 | tf_op jit(solution)/shard_map/all_to_all | solution.py:383
  151.1 1.6 proj_grads.1
  152.8 0.8 copy-done.27
  153.6 5.5 %all-to-all-done.3.gout_ref = bf16[8,64,256]{2,1,0:T(8,128)(2,1)S(1)} async-done(((bf16[8,64,256]{2,1,0:T(8,128)(2,1)}), bf16[8,64,256]{2,1,0:T(8,128)(2,1)S(1)}, u32[]{:S(2)}, u32[]{:S(2)}) %all-to-all-start.3) | async-done | bytes 262176 | tf_op jit(solution)/shard_map/all_to_all | solution.py:383
  159.8 15.7 %attention_backward.1 = (bf16[8,64,256]{2,1,0:T(8,128)(2,1)S(1)}, f32[8,128,256]{2,1,0:T(8,128)S(1)}, bf16[8,128,256]{2,1,0:T(8,128)(2,1)S(1)}) custom-call(s32[4]{0:T(128)S(1)} %copy-done.19, s32[1,2]{1,0:T(1,128)S(1)} %copy-done.18, bf16[4096,80]{1,0:T(8,128)(2,1)} %copy-done.22, bf16[64,4096]{1,0:T(8,128)(2,1)} %copy-done.24, ...), custom_call_target="tpu_custom_call" | custom-call | flops 29899999232 | bytes 1048576 | tf_op jit(solution)/shard_map/attention_backward/pallas_call | solution.py:340
  175.6 1.9 collective-permute-done.7.other_ref
  177.5 1.1 merge.1
  178.6 4.2 %all-to-all-start.4 = ((bf16[8,192,256]{2,1,0:T(8,128)(2,1)}), bf16[8,192,256]{2,1,0:T(8,128)(2,1)}, u32[]{:S(2)}, u32[]{:S(2)}) async-start(bf16[8,192,256]{2,1,0:T(8,128)(2,1)} %merge.1), calls=%async_computation.4 | async-start | bytes 1572864 | tf_op jit(solution)/shard_map/all_to_all | solution.py:383
  182.9 3.4 %final.1 = (bf16[256,1024]{1,0:T(8,128)(2,1)}, f32[1,128]{1,0:T(1,128)S(1)}) custom-call(s32[4]{0:T(128)S(1)} %copy-done.19, bf16[256,1024]{1,0:T(8,128)(2,1)} %copy-done.20, f32[256,1024]{1,0:T(8,128)} %copy-done.1, bf16[256,1024]{1,0:T(8,128)(2,1)S(1)} %get-tuple-element.110.mine_ref, bf16[256,1024]{1,0:T(8,128)(2,1)S(1)} %collective-permute-done.6.swapped_ref, ...), custom_call_target="tpu_custom_call" | custom-call | flops 3449999872 | bytes 1048576 | tf_op jit(solution)/shard_map/final/pallas_call | solution.py:408
  186.3 11.5 %all-to-all-done.4.gback_ref = bf16[8,192,256]{2,1,0:T(8,128)(2,1)} async-done(((bf16[8,192,256]{2,1,0:T(8,128)(2,1)}), bf16[8,192,256]{2,1,0:T(8,128)(2,1)}, u32[]{:S(2)}, u32[]{:S(2)}) %all-to-all-start.4) | async-done | bytes 786464 | tf_op jit(solution)/shard_map/all_to_all | solution.py:383
  197.8 6.4 %back.1 = (bf16[128,1024]{1,0:T(8,128)(2,1)}, bf16[128,1024]{1,0:T(8,128)(2,1)}, f32[8,512]{1,0:T(8,128)}, bf16[512,1920]{1,0:T(8,128)(2,1)}, bf16[1536,256]{1,0:T(8,128)(2,1)}, /*index=5*/bf16[2,16,128]{2,1,0:T(8,128)(2,1)}) custom-call(bf16[8,192,256]{2,1,0:T(8,128)(2,1)} %all-to-all-done.4.gback_ref, bf16[512,1664]{1,0:T(8,128)(2,1)} %bitcast.8.own_ref, ...), custom_call_target="tpu_custom_call" | custom-call | flops 5750000128 | bytes 1048576 | tf_op jit(solution)/shard_map/back/pallas_call | solution.py:408
  205.1 1.4 collective-permute-start.8
  206.5 7.1 %collective-permute-done.8.swapped_ref = bf16[128,1024]{1,0:T(8,128)(2,1)S(1)} collective-permute-done((bf16[128,1024]{1,0:T(8,128)(2,1)}, bf16[128,1024]{1,0:T(8,128)(2,1)S(1)}, u32[]{:S(2)}, u32[]{:S(2)}) %collective-permute-start.8) | collective-permute-done | bytes 262176 | tf_op jit(solution)/shard_map/ppermute | solution.py:379
  214.4 5.5 %qkv_core_sum.1 = bf16[512,2432]{1,0:T(8,128)(2,1)} custom-call(bf16[1536,256]{1,0:T(8,128)(2,1)} %get-tuple-element.120.grads_ref, bf16[256,512]{1,0:T(8,128)(2,1)} %copy-done.30, bf16[2,16,128]{2,1,0:T(8,128)(2,1)} %get-tuple-element.122.sums_ref, bf16[512,1920]{1,0:T(8,128)(2,1)} %collective-permute-done.10.b_ref, bf16[512,640]{1,0:T(8,128)(2,1)} %copy-done.27, ...), custom_call_target="tpu_custom_call" | custom-call | flops 4600000000 | bytes 1048576 | tf_op jit(solution)/shard_map/qkv_core_sum/pallas_call | solution.py:834
  219.9 4.2 %all-to-all-start.5 = ((bf16[32,16,2432]{2,1,0:T(8,128)(2,1)}), bf16[32,16,2432]{2,1,0:T(8,128)(2,1)S(1)}, u32[]{:S(2)}, u32[]{:S(2)}) async-start(bf16[32,16,2432]{2,1,0:T(8,128)(2,1)} %bitcast.42), calls=%async_computation.5 | async-start | bytes 4980736 | tf_op jit(solution)/shard_map/all_to_all | solution.py:383
  224.1 1.0 constant_dynamic-slice_fusion
  225.1 3.3 %collective-permute-start.12 = (bf16[16,4096]{1,0:T(8,128)(2,1)S(1)}, bf16[16,4096]{1,0:T(8,128)(2,1)S(1)}, u32[]{:S(2)}, u32[]{:S(2)}) collective-permute-start(bf16[16,4096]{1,0:T(8,128)(2,1)S(1)} %get-tuple-element.141), channel_id=1, source_target_pairs={{0,16},{16,0},{1,17},{17,1},{2,18},{18,2},{3,19},{19,3},{4,20},{20... | collective-permute-start | bytes 393224 | tf_op jit(solution)/shard_map/ppermute | solution.py:379
  228.4 2.5 end.1.mine_ref
  230.9 1.5 collective-permute-start.9
  232.4 22.3 %collective-permute-done.12.theirs_ref = bf16[16,4096]{1,0:T(8,128)(2,1)S(1)} collective-permute-done((bf16[16,4096]{1,0:T(8,128)(2,1)S(1)}, bf16[16,4096]{1,0:T(8,128)(2,1)S(1)}, u32[]{:S(2)}, u32[]{:S(2)}) %collective-permute-start.12) | collective-permute-done | bytes 131104 | tf_op jit(solution)/shard_map/ppermute | solution.py:379
  255.4 5.9 %collective-permute-done.9.theirs_ref = bf16[128,1024]{1,0:T(8,128)(2,1)S(1)} collective-permute-done((bf16[128,1024]{1,0:T(8,128)(2,1)S(1)}, bf16[128,1024]{1,0:T(8,128)(2,1)S(1)}, u32[]{:S(2)}, u32[]{:S(2)}) %collective-permute-start.9) | collective-permute-done | bytes 262176 | tf_op jit(solution)/shard_map/ppermute | solution.py:379
  262.6 1.5 total_qkv.1
  264.6 0.8 join.1
  (108 shorter events, 12.0 us)
Async XLA Ops:
  8.9 5.9 %copy-start.35 = (bf16[16,3,512]{2,0,1:T(8,128)(2,1)S(1)}, bf16[16,3,512]{2,0,1:T(8,128)(2,1)}, u32[]{:S(2)}) copy-start(bf16[16,3,512]{2,0,1:T(8,128)(2,1)} %param.19) | copy-start | bytes 147460
  8.9 6.0 %copy-start.12 = (bf16[16]{0:T(256)(128)(2,1)S(1)}, bf16[16]{0:T(256)(128)(2,1)}, u32[]{:S(2)}) copy-start(bf16[16]{0:T(256)(128)(2,1)} %param.17) | copy-start | bytes 100
  8.9 6.0 %copy-start.13 = (bf16[16]{0:T(256)(128)(2,1)S(1)}, bf16[16]{0:T(256)(128)(2,1)}, u32[]{:S(2)}) copy-start(bf16[16]{0:T(256)(128)(2,1)} %param.18) | copy-start | bytes 100
  8.9 6.0 %copy-start.14 = (bf16[16]{0:T(256)(128)(2,1)S(1)}, bf16[16]{0:T(256)(128)(2,1)}, u32[]{:S(2)}) copy-start(bf16[16]{0:T(256)(128)(2,1)} %param.22) | copy-start | bytes 100
  8.9 6.0 %copy-start.15 = (bf16[16]{0:T(256)(128)(2,1)S(1)}, bf16[16]{0:T(256)(128)(2,1)}, u32[]{:S(2)}) copy-start(bf16[16]{0:T(256)(128)(2,1)} %param.23) | copy-start | bytes 100
  8.9 6.0 %copy-start.16 = (bf16[16]{0:T(256)(128)(2,1)S(1)}, bf16[16]{0:T(256)(128)(2,1)}, u32[]{:S(2)}) copy-start(bf16[16]{0:T(256)(128)(2,1)} %param.24) | copy-start | bytes 100
  8.9 6.0 %copy-start.17 = (bf16[16]{0:T(256)(128)(2,1)S(1)}, bf16[16]{0:T(256)(128)(2,1)}, u32[]{:S(2)}) copy-start(bf16[16]{0:T(256)(128)(2,1)} %param.28) | copy-start | bytes 100
  9.7 19.6 %collective-permute-start.2 = (bf16[16,4608]{1,0:T(8,128)(2,1)S(1)}, bf16[16,4608]{1,0:T(8,128)(2,1)S(1)}, u32[]{:S(2)}, u32[]{:S(2)}) collective-permute-start(bf16[16,4608]{1,0:T(8,128)(2,1)S(1)} %rest_payload.1.mine_ref), channel_id=1, source_target_pairs={{0,16},{16,0},{1,17},{17,1},{2,18},{18,2},{3,19},{19,3},{4,20},{20... | collective-permute-start | bytes 442376 | tf_op jit(solution)/shard_map/ppermute | solution.py:379
  13.8 15.5 %collective-permute-start.3 = (bf16[16,512]{1,0:T(8,128)(2,1)}, bf16[16,512]{1,0:T(8,128)(2,1)S(1)}, u32[]{:S(2)}, u32[]{:S(2)}) collective-permute-start(bf16[16,512]{1,0:T(8,128)(2,1)} %bitcast.10.proj_ref), channel_id=1, source_target_pairs={{0,1},{1,0},{2,3},{3,2},{4,5},{5,4},{6,7},{7,6},{8,9},{9,8},{10,11... | collective-permute-start | bytes 49160 | tf_op jit(solution)/shard_map/ppermute | solution.py:379
  14.8 14.5 %collective-permute-start.4 = (bf16[16,512]{1,0:T(8,128)(2,1)}, bf16[16,512]{1,0:T(8,128)(2,1)S(1)}, u32[]{:S(2)}, u32[]{:S(2)}) collective-permute-start(bf16[16,512]{1,0:T(8,128)(2,1)} %bitcast.10.proj_ref), channel_id=1, source_target_pairs={{0,17},{1,16},{16,1},{17,0},{2,19},{3,18},{18,3},{19,2},{4,21},{5,... | collective-permute-start | bytes 49160 | tf_op jit(solution)/shard_map/ppermute | solution.py:951
  19.2 36.4 %all-to-all-start = ((bf16[32,16,1664]{2,1,0:T(8,128)(2,1)}), bf16[32,16,1664]{2,1,0:T(8,128)(2,1)}, u32[]{:S(2)}, u32[]{:S(2)}) async-start(bf16[32,16,1664]{2,1,0:T(8,128)(2,1)} %weights_payload.1), calls=%async_computation | async-start | bytes 3407872 | tf_op jit(solution)/shard_map/all_to_all | solution.py:383
  29.2 1.3 copy-start.7
  29.2 1.3 copy-start.19
  29.2 80.8 %all-gather.2.cloned.1.call-start = ((), (), s32[]{:S(2)}) async-start(), calls=%async_computation.8 | async-start | bytes 10813440 | tf_op jit(solution)/shard_map/all_gather | solution.py:953
  30.5 28.9 %copy-start.11 = (bf16[2,512]{1,0:T(2,128)(2,1)S(1)}, bf16[2,512]{1,0:T(2,128)(2,1)}, u32[]{:S(2)}) copy-start(bf16[2,512]{1,0:T(2,128)(2,1)} %bias_ref.1) | copy-start | bytes 6148
  33.2 30.0 %copy-start.20 = (bf16[256,1024]{1,0:T(8,128)(2,1)}, bf16[256,1024]{1,0:T(8,128)(2,1)S(1)}, u32[]{:S(2)}) copy-start(bf16[256,1024]{1,0:T(8,128)(2,1)S(1)} %get-tuple-element.78.inputs_ref) | copy-start | bytes 1572868
  55.6 3.8 %collective-permute-start = (bf16[512,1664]{1,0:T(8,128)(2,1)}, bf16[512,1664]{1,0:T(8,128)(2,1)S(1)}, u32[]{:S(2)}, u32[]{:S(2)}) collective-permute-start(bf16[512,1664]{1,0:T(8,128)(2,1)} %bitcast.8.own_ref), channel_id=1, source_target_pairs={{0,2},{2,0},{1,3},{3,1},{4,6},{6,4},{5,7},{7,5},{8,10},{10,8},{9,1... | collective-permute-start | bytes 5111816 | tf_op jit(solution)/shard_map/ppermute | solution.py:379
  59.4 3.8 %copy-start.5 = (bf16[512,1664]{1,0:T(8,128)(2,1)}, bf16[512,1664]{1,0:T(8,128)(2,1)S(1)}, u32[]{:S(2)}) copy-start(bf16[512,1664]{1,0:T(8,128)(2,1)S(1)} %collective-permute-done.other_ref) | copy-start | bytes 5111812
  63.2 36.5 %copy-start.3 = (f32[8,1024]{1,0:T(8,128)}, f32[8,1024]{1,0:T(8,128)S(1)}, u32[]{:S(2)}) copy-start(f32[8,1024]{1,0:T(8,128)S(1)} %get-tuple-element.88.vectors_ref) | copy-start | bytes 98308
  63.2 36.4 %copy-start.30 = (bf16[256,512]{1,0:T(8,128)(2,1)}, bf16[256,512]{1,0:T(8,128)(2,1)S(1)}, u32[]{:S(2)}) copy-start(bf16[256,512]{1,0:T(8,128)(2,1)S(1)} %get-tuple-element.121.own_n_ref) | copy-start | bytes 786436
  63.2 36.4 %copy-start.31 = (bf16[256,512]{1,0:T(8,128)(2,1)}, bf16[256,512]{1,0:T(8,128)(2,1)S(1)}, u32[]{:S(2)}) copy-start(bf16[256,512]{1,0:T(8,128)(2,1)S(1)} %get-tuple-element.116.other_n_ref) | copy-start | bytes 786436
  63.3 27.2 %copy-start.18 = (s32[1,2]{1,0:T(1,128)S(1)}, s32[1,2]{1,0:T(1,128)}, u32[]{:S(2)}) copy-start(s32[1,2]{1,0:T(1,128)} %starts_ref.3) | copy-start | bytes 28
  88.4 16.9 %copy-start.36 = (bf16[2048]{0:T(1024)(128)(2,1)S(1)}, bf16[2048]{0:T(1024)(128)(2,1)}, u32[]{:S(2)}) copy-start(bf16[2048]{0:T(1024)(128)(2,1)} %param.26) | copy-start | bytes 12292
  88.4 2.0 collective-permute-start.1
  99.7 5.6 %copy-start.32 = (f32[8,64,256]{2,1,0:T(8,128)}, f32[8,64,256]{2,1,0:T(8,128)S(1)}, u32[]{:S(2)}) copy-start(f32[8,64,256]{2,1,0:T(8,128)S(1)} %get-tuple-element.106.out_ref) | copy-start | bytes 1572868
  99.7 17.8 %all-to-all-start.2 = ((bf16[16,64,256]{2,1,0:T(8,128)(2,1)}), bf16[16,64,256]{2,1,0:T(8,128)(2,1)S(1)}, u32[]{:S(2)}, u32[]{:S(2)}) async-start(bf16[16,64,256]{2,1,0:T(8,128)(2,1)} %bitcast.9), calls=%async_computation.2 | async-start | bytes 1048576 | tf_op jit(solution)/shard_map/all_to_all | solution.py:383
  105.2 99.0 %reduce-scatter.3.cloned.1.call-start = ((), (), s32[]{:S(2)}) async-start(), calls=%async_computation.9 | async-start | bytes 9437184 | tf_op jit(solution)/shard_map/reduce_scatter | solution.py:993
  110.0 4.3 %copy-start.26 = (bf16[8,80,256]{2,1,0:T(8,128)(2,1)}, bf16[8,80,256]{2,1,0:T(8,128)(2,1)S(1)}, u32[]{:S(2)}) copy-start(bf16[8,80,256]{2,1,0:T(8,128)(2,1)S(1)} %get-tuple-element.96.query_ref) | copy-start | bytes 983044
  120.3 6.5 %copy-start.1 = (f32[256,1024]{1,0:T(8,128)}, f32[256,1024]{1,0:T(8,128)S(1)}, u32[]{:S(2)}) copy-start(f32[256,1024]{1,0:T(8,128)S(1)} %get-tuple-element.89.middle_ref) | copy-start | bytes 3145732
  120.3 6.5 %copy-start.21 = (bf16[512,256]{1,0:T(8,128)(2,1)}, bf16[512,256]{1,0:T(8,128)(2,1)S(1)}, u32[]{:S(2)}) copy-start(bf16[512,256]{1,0:T(8,128)(2,1)S(1)} %get-tuple-element.102.heads_ref) | copy-start | bytes 786436
  126.8 11.1 %copy-start.2 = (bf16[256,1024]{1,0:T(8,128)(2,1)}, bf16[256,1024]{1,0:T(8,128)(2,1)S(1)}, u32[]{:S(2)}) copy-start(bf16[256,1024]{1,0:T(8,128)(2,1)S(1)} %get-tuple-element.98.mine_ref) | copy-start | bytes 1572868
  126.8 11.1 %copy-start.29 = (bf16[256,2048]{1,0:T(8,128)(2,1)}, bf16[256,2048]{1,0:T(8,128)(2,1)S(1)}, u32[]{:S(2)}) copy-start(bf16[256,2048]{1,0:T(8,128)(2,1)S(1)} %get-tuple-element.91.gh_ref) | copy-start | bytes 3145732
  126.8 13.2 %collective-permute-start.5 = (bf16[256,1024]{1,0:T(8,128)(2,1)S(1)}, bf16[256,1024]{1,0:T(8,128)(2,1)S(1)}, u32[]{:S(2)}, u32[]{:S(2)}) collective-permute-start(bf16[256,1024]{1,0:T(8,128)(2,1)S(1)} %get-tuple-element.98.mine_ref), channel_id=1, source_target_pairs={{0,1},{1,0},{2,3},{3,2},{4,5},{5,4},{6,7},{7,6},{8,9},{9,8},{10,11... | collective-permute-start | bytes 1572872 | tf_op jit(solution)/shard_map/ppermute | solution.py:379
  145.6 13.5 %all-to-all-start.3 = ((bf16[8,64,256]{2,1,0:T(8,128)(2,1)}), bf16[8,64,256]{2,1,0:T(8,128)(2,1)S(1)}, u32[]{:S(2)}, u32[]{:S(2)}) async-start(bf16[8,64,256]{2,1,0:T(8,128)(2,1)} %get-tuple-element.100), calls=%async_computation.3 | async-start | bytes 524288 | tf_op jit(solution)/shard_map/all_to_all | solution.py:383
  159.2 16.4 %collective-permute-start.6 = (bf16[256,1024]{1,0:T(8,128)(2,1)S(1)}, bf16[256,1024]{1,0:T(8,128)(2,1)S(1)}, u32[]{:S(2)}, u32[]{:S(2)}) collective-permute-start(bf16[256,1024]{1,0:T(8,128)(2,1)S(1)} %get-tuple-element.110.mine_ref), channel_id=1, source_target_pairs={{0,1},{1,0},{2,3},{3,2},{4,5},{5,4},{6,7},{7,6},{8,9},{9,8},{10,11... | collective-permute-start | bytes 1572872 | tf_op jit(solution)/shard_map/ppermute | solution.py:379
  175.5 2.0 collective-permute-start.7
  177.5 5.3 %copy-start.4 = (f32[8,1024]{1,0:T(8,128)S(1)}, f32[8,1024]{1,0:T(8,128)}, u32[]{:S(2)}) copy-start(f32[8,1024]{1,0:T(8,128)} %copy-done.3) | copy-start | bytes 98308
  178.6 19.2 %all-to-all-start.4 = ((bf16[8,192,256]{2,1,0:T(8,128)(2,1)}), bf16[8,192,256]{2,1,0:T(8,128)(2,1)}, u32[]{:S(2)}, u32[]{:S(2)}) async-start(bf16[8,192,256]{2,1,0:T(8,128)(2,1)} %merge.1), calls=%async_computation.4 | async-start | bytes 1572864 | tf_op jit(solution)/shard_map/all_to_all | solution.py:383
  182.8 41.3 %reduce-scatter.5.cloned.1.call-start = ((), (), s32[]{:S(2)}) async-start(), calls=%async_computation.10 | async-start | bytes 1310720 | tf_op jit(solution)/shard_map/reduce_scatter | solution.py:1060
  186.3 11.5 %copy-start.33 = (f32[1,128]{1,0:T(1,128)}, f32[1,128]{1,0:T(1,128)S(1)}, u32[]{:S(2)}) copy-start(f32[1,128]{1,0:T(1,128)S(1)} %get-tuple-element.117.roots_ref) | copy-start | bytes 1540
  204.2 9.4 %collective-permute-start.10 = (bf16[512,1920]{1,0:T(8,128)(2,1)}, bf16[512,1920]{1,0:T(8,128)(2,1)}, u32[]{:S(2)}, u32[]{:S(2)}) collective-permute-start(bf16[512,1920]{1,0:T(8,128)(2,1)} %get-tuple-element.123), channel_id=1, source_target_pairs={{0,2},{2,0},{1,3},{3,1},{4,6},{6,4},{5,7},{7,5},{8,10},{10,8},{9,1... | collective-permute-start | bytes 5898248 | tf_op jit(solution)/shard_map/ppermute | solution.py:379
  204.3 9.3 %collective-permute-start.11 = (bf16[512,640]{1,0:T(8,128)(2,1)S(1)}, bf16[512,640]{1,0:T(8,128)(2,1)S(1)}, u32[]{:S(2)}, u32[]{:S(2)}) collective-permute-start(bf16[512,640]{1,0:T(8,128)(2,1)S(1)} %get-tuple-element.126), channel_id=1, source_target_pairs={{0,2},{2,0},{1,3},{3,1},{4,6},{6,4},{5,7},{7,5},{8,10},{10,8},{9,1... | collective-permute-start | bytes 1966088 | tf_op jit(solution)/shard_map/ppermute | solution.py:379
  205.1 8.5 %collective-permute-start.8 = (bf16[128,1024]{1,0:T(8,128)(2,1)}, bf16[128,1024]{1,0:T(8,128)(2,1)S(1)}, u32[]{:S(2)}, u32[]{:S(2)}) collective-permute-start(bf16[128,1024]{1,0:T(8,128)(2,1)} %get-tuple-element.119), channel_id=1, source_target_pairs={{0,1},{1,0},{2,3},{3,2},{4,5},{5,4},{6,7},{7,6},{8,9},{9,8},{10,11... | collective-permute-start | bytes 786440 | tf_op jit(solution)/shard_map/ppermute | solution.py:379
  219.9 8.5 %copy-start.28 = (bf16[128,1024]{1,0:T(8,128)(2,1)S(1)}, bf16[128,1024]{1,0:T(8,128)(2,1)}, u32[]{:S(2)}) copy-start(bf16[128,1024]{1,0:T(8,128)(2,1)} %get-tuple-element.118.mine_ref) | copy-start | bytes 786436
  219.9 41.4 %all-to-all-start.5 = ((bf16[32,16,2432]{2,1,0:T(8,128)(2,1)}), bf16[32,16,2432]{2,1,0:T(8,128)(2,1)S(1)}, u32[]{:S(2)}, u32[]{:S(2)}) async-start(bf16[32,16,2432]{2,1,0:T(8,128)(2,1)} %bitcast.42), calls=%async_computation.5 | async-start | bytes 4980736 | tf_op jit(solution)/shard_map/all_to_all | solution.py:383
  225.1 29.6 %collective-permute-start.12 = (bf16[16,4096]{1,0:T(8,128)(2,1)S(1)}, bf16[16,4096]{1,0:T(8,128)(2,1)S(1)}, u32[]{:S(2)}, u32[]{:S(2)}) collective-permute-start(bf16[16,4096]{1,0:T(8,128)(2,1)S(1)} %get-tuple-element.141), channel_id=1, source_target_pairs={{0,16},{16,0},{1,17},{17,1},{2,18},{18,2},{3,19},{19,3},{4,20},{20... | collective-permute-start | bytes 393224 | tf_op jit(solution)/shard_map/ppermute | solution.py:379
  230.9 30.4 %collective-permute-start.9 = (bf16[128,1024]{1,0:T(8,128)(2,1)S(1)}, bf16[128,1024]{1,0:T(8,128)(2,1)S(1)}, u32[]{:S(2)}, u32[]{:S(2)}) collective-permute-start(bf16[128,1024]{1,0:T(8,128)(2,1)S(1)} %end.1.mine_ref), channel_id=1, source_target_pairs={{0,1},{1,0},{2,3},{3,2},{4,5},{5,4},{6,7},{7,6},{8,9},{9,8},{10,11... | collective-permute-start | bytes 786440 | tf_op jit(solution)/shard_map/ppermute | solution.py:379
  262.0 3.6 %collective-permute-start.13 = (f32[2,16]{1,0:T(2,128)S(1)}, f32[2,16]{1,0:T(2,128)S(1)}, u32[]{:S(2)}, u32[]{:S(2)}) collective-permute-start(f32[2,16]{1,0:T(2,128)S(1)} %slice.28), channel_id=1, source_target_pairs={{0,1},{1,0},{2,3},{3,2},{4,5},{5,4},{6,7},{7,6},{8,9},{9,8},{10,11... | collective-permute-start | bytes 392 | tf_op jit(solution)/shard_map/ppermute | solution.py:379
  (12 other events, 10.4 us)
Sparse Core Ops, SparseCore 0:
  32.3 69.3 all-gather.1
  140.2 49.1 reduce-scatter.2
  204.4 19.0 reduce-scatter.4

commit v3 on v2

--- a/solution.py
+++ b/solution.py
@@ -588,7 +588,7 @@
     def _():
         total_ref[...] = jnp.zeros_like(total_ref)
 
-    halves = (slice(0, 256), slice(256, 512))
+    halves = [slice(at, at + 256) for at in range(0, 1024, 256)]
     hidden = [
         dot(n_ref[...], weight_ref[:, cols]) + bias_ref[:, cols].astype(f32) for cols in halves
     ]
@@ -598,21 +598,21 @@
         gh_ref[:, cols] = low(gact_ref[:, cols] * slope)
     total_ref[...] += contract(gh_ref[...], weight_ref[...], 1, 1)
 
-    @pl.when(i == 3)
+    @pl.when(i == 1)
     def _():
         part_ref[...] = low(total_ref[...])
 
 
 def feed_forward(normed_two, grad_act, fc_bias, rest):
     def tile(rows, first):
-        return pl.BlockSpec((rows, 512), lambda i: (0, first + i))
+        return pl.BlockSpec((rows, 1024), lambda i: (0, first + i))
 
     wide = pl.BlockSpec((256, 1024), lambda i: (0, 0))
     return pl.pallas_call(
         feed_kernel,
-        grid=(4,),
+        grid=(2,),
         out_shape=(shape(256, 2048), shape(256, 2048), shape(256, 1024)),
-        in_specs=[wide, tile(256, 0), tile(1, 0), tile(1024, 2)],
+        in_specs=[wide, tile(256, 0), tile(1, 0), tile(1024, 1)],
         out_specs=(tile(256, 0), tile(256, 0), wide),
         scratch_shapes=[pltpu.VMEM((256, 1024), f32)],
         compiler_params=ROOMY,
@@ -1054,7 +1054,6 @@
         far(grad_hidden),
         cost=5,
         scratch=[pltpu.VMEM((256, 1024), f32), pltpu.VMEM((256, 1024), bf16)],
-        memory=ALL,
     )
     one_swapped = swap(one_send, "tp")
     wide = lax.psum_scatter(after(wide, roots), "y", scatter_dimension=0, tiled=True)

time: 274 us -> 273 us (level)
    unnamed x77 -> x79, local copies, waits for them, and re-layouts: 9.87 us -> 10.8 us
where the time goes in v3:
time: 273 us; the launch traced here: 271 us
  Pallas kernels  88.9 us (33%)
  waiting for transfers between devices  87.4 us (32%)
  starting transfers between devices  42.3 us (15%)
  blocking collectives  25.1 us (9%)
  between operations  14.3 us (5%)
  local copies, waits for them, and re-layouts  13.4 us (5%)
    ppermute x13, waiting for transfers between devices, swap(): return lax.ppermute(field, axis, [(0, 1), (1, 0)])  45 us
    all_to_all x5, waiting for transfers between devices, exchange(): return lax.all_to_all(field, axes, split_axis=0, concat_axis=0, tiled=True)  42.3 us
    pallas_call x13, Pallas kernels, call(): pl.pallas_call(kernel, grid=(1,), out_shape=outs, in_specs=[SM] * scalars...  29.1 us
    all_to_all x5, starting transfers between devices, exchange(): return lax.all_to_all(field, axes, split_axis=0, concat_axis=0, tiled=True)  28 us
    all_to_all x1, blocking collectives, exchange(): return lax.all_to_all(field, axes, split_axis=0, concat_axis=0, tiled=True)  25.1 us
    pallas_call x1, Pallas kernels, attn_backward(): pl.pallas_call(backward_kernel, grid=(1,), out_shape=outs, in_specs=[SM,...  15.7 us
    ppermute x13, starting transfers between devices, swap(): return lax.ppermute(field, axis, [(0, 1), (1, 0)])  13.9 us
    unnamed x79, local copies, waits for them, and re-layouts  10.8 us
  transfers between devices with their start and end apart: 22, of which 12 were waited for; matrix products, arithmetic and copies ran while one was open for 1% of the time, Pallas kernels for 29%

profile of v3, /device:TPU:0, one launch (start us, length us, event | category | flops | bytes accessed | tf_op | source)
XLA Modules:
  0.0 271.4 jit_solution(4954000585469227805)
XLA Ops:
  8.0 0.8 copy-done.9
  9.7 4.0 %collective-permute-start.2 = (bf16[16,4608]{1,0:T(8,128)(2,1)S(1)}, bf16[16,4608]{1,0:T(8,128)(2,1)S(1)}, u32[]{:S(2)}, u32[]{:S(2)}) collective-permute-start(bf16[16,4608]{1,0:T(8,128)(2,1)S(1)} %rest_payload.1.mine_ref), channel_id=1, source_target_pairs={{0,16},{16,0},{1,17},{17,1},{2,18},{18,2},{3,19},{19,3},{4,20},{20... | collective-permute-start | bytes 442376 | tf_op jit(solution)/shard_map/ppermute | solution.py:379
  13.8 1.0 collective-permute-start.3
  14.9 4.3 %weights_payload.1 = bf16[32,16,1664]{2,1,0:T(8,128)(2,1)} custom-call(bf16[16,3,512]{2,1,0:T(4,128)(2,1)S(1)} %copy.31.qkv_ref, bf16[1,16]{1,0:T(2,128)(2,1)S(1)} %bitcast.36, bf16[1,16]{1,0:T(2,128)(2,1)S(1)} %bitcast.37, bf16[1,16]{1,0:T(2,128)(2,1)S(1)} %bitcast.38, bf16[1,16]{1,0:T(2,128)(2,1)S(1)} %bitcast.39, bf16[1,16]{1,0:T(2,128)(2,1)S(1)} %bitcast.40, ...), custom_call_target="tpu_custom_call" | custom-call | flops 1150000000 | bytes 1048576 | tf_op jit(solution)/shard_map/weights_payload/pallas_call | solution.py:408
  19.2 9.9 %all-to-all-start = ((bf16[32,16,1664]{2,1,0:T(8,128)(2,1)}), bf16[32,16,1664]{2,1,0:T(8,128)(2,1)}, u32[]{:S(2)}, u32[]{:S(2)}) async-start(bf16[32,16,1664]{2,1,0:T(8,128)(2,1)} %weights_payload.1), calls=%async_computation | async-start | bytes 3407872 | tf_op jit(solution)/shard_map/all_to_all | solution.py:383
  30.5 1.9 inputs.1
  33.2 22.4 %all-to-all-done = bf16[32,16,1664]{2,1,0:T(8,128)(2,1)} async-done(((bf16[32,16,1664]{2,1,0:T(8,128)(2,1)}), bf16[32,16,1664]{2,1,0:T(8,128)(2,1)}, u32[]{:S(2)}, u32[]{:S(2)}) %all-to-all-start) | async-done | bytes 1703968 | tf_op jit(solution)/shard_map/all_to_all | solution.py:383
  55.6 3.8 %collective-permute-done.other_ref = bf16[512,1664]{1,0:T(8,128)(2,1)S(1)} collective-permute-done((bf16[512,1664]{1,0:T(8,128)(2,1)}, bf16[512,1664]{1,0:T(8,128)(2,1)S(1)}, u32[]{:S(2)}, u32[]{:S(2)}) %collective-permute-start) | collective-permute-done | bytes 1703968 | tf_op jit(solution)/shard_map/ppermute | solution.py:379
  59.4 3.8 %qkv.1 = (bf16[8,192,256]{2,1,0:T(8,128)(2,1)S(1)}, bf16[256,512]{1,0:T(8,128)(2,1)S(1)}, bf16[256,512]{1,0:T(8,128)(2,1)S(1)}, f32[8,1024]{1,0:T(8,128)S(1)}) custom-call(bf16[256,1024]{1,0:T(8,128)(2,1)S(1)} %get-tuple-element.78.inputs_ref, bf16[512,1664]{1,0:T(8,128)(2,1)} %bitcast.8.own_ref, bf16[512,1664]{1,0:T(8,128)(2,1)S(1)} %collective-permute-done.other_ref, ...), custom_call_target="tpu_custom_call" | custom-call | flops 3449999872 | bytes 1048576 | tf_op jit(solution)/shard_map/qkv/pallas_call | solution.py:408
  63.3 25.1 %all_to_all.30.own_ref = bf16[8,192,256]{2,1,0:T(8,128)(2,1)S(1)} all-to-all(bf16[8,192,256]{2,1,0:T(8,128)(2,1)S(1)} %get-tuple-element.80), channel_id=1, replica_groups=mesh['x'=4,'zh'=2,'y'=4,'c'=2,'tp'=2] {'zh','y'}, dimensions={0} | all-to-all | bytes 1572864 | tf_op jit(solution)/shard_map/all_to_all | solution.py:383
  88.5 1.9 collective-permute-done.1.other_ref
  90.4 9.2 %attention_forward.1 = (f32[8,64,256]{2,1,0:T(8,128)S(1)}, bf16[8,2,64,256]{3,2,1,0:T(8,128)(2,1)}, f32[8,1,256]{2,1,0:T(1,128)S(1)}) custom-call(s32[4]{0:T(128)S(1)} %copy-done.19, s32[1,2]{1,0:T(1,128)S(1)} %copy-done.18, bf16[8,192,256]{2,1,0:T(8,128)(2,1)S(1)} %all_to_all.30.own_ref, bf16[8,128,256]{2,1,0:T(8,128)(2,1)S(1)} %collective-permute-done.1.other_ref), custom_call_target="tpu_custom_call" | custom-call | flops 9200000000 | bytes 1048576 | tf_op jit(solution)/shard_map/attention_forward/pallas_call | solution.py:302
  99.7 5.5 %all-to-all-start.2 = ((bf16[16,64,256]{2,1,0:T(8,128)(2,1)}), bf16[16,64,256]{2,1,0:T(8,128)(2,1)S(1)}, u32[]{:S(2)}, u32[]{:S(2)}) async-start(bf16[16,64,256]{2,1,0:T(8,128)(2,1)} %bitcast.9), calls=%async_computation.2 | async-start | bytes 1048576 | tf_op jit(solution)/shard_map/all_to_all | solution.py:383
  105.5 1.1 attention_stage.1
  106.6 1.0 copy-done.22
  107.6 1.0 copy-done.23
  110.2 4.2 %grad_act.1.gact_ref = f32[256,2048]{1,0:T(8,128)S(1)} custom-call(bf16[256,1024]{1,0:T(8,128)(2,1)} %copy-done, bf16[1024,5120]{1,0:T(8,128)(2,1)} %all-gather.2.cloned.1.call-done.weight_ref), custom_call_target="tpu_custom_call" | custom-call | flops 3449999872 | bytes 1048576 | tf_op jit(solution)/shard_map/grad_act/pallas_call | solution.py:569
  114.5 3.0 %all-to-all-done.2.heads_ref = bf16[16,64,256]{2,1,0:T(8,128)(2,1)S(1)} async-done(((bf16[16,64,256]{2,1,0:T(8,128)(2,1)}), bf16[16,64,256]{2,1,0:T(8,128)(2,1)S(1)}, u32[]{:S(2)}, u32[]{:S(2)}) %all-to-all-start.2) | async-done | bytes 524320 | tf_op jit(solution)/shard_map/all_to_all | solution.py:383
  117.5 2.8 %attn_end.1 = (f32[256,1024]{1,0:T(8,128)S(1)}, bf16[256,1024]{1,0:T(8,128)(2,1)S(1)}, bf16[512,256]{1,0:T(8,128)(2,1)S(1)}) custom-call(bf16[16,64,256]{2,1,0:T(8,128)(2,1)S(1)} %all-to-all-done.2.heads_ref, bf16[1024,5120]{1,0:T(8,128)(2,1)} %all-gather.2.cloned.1.call-done.weight_ref, bf16[256,1024]{1,0:T(8,128)(2,1)} %copy-done.20, f32[8,1024]{1,0:T(8,128)} %copy-done.3), custom_call_target="tpu_custom_call" | custom-call | flops 3449999872 | bytes 1048576 | tf_op jit(solution)/shard_map/attn_end/pallas_call | solution.py:546
  120.3 6.1 %feed_forward.1 = (bf16[256,2048]{1,0:T(8,128)(2,1)S(1)}, bf16[256,2048]{1,0:T(8,128)(2,1)S(1)}, bf16[256,1024]{1,0:T(8,128)(2,1)S(1)}) custom-call(bf16[256,1024]{1,0:T(8,128)(2,1)S(1)} %get-tuple-element.90.n_ref, f32[256,2048]{1,0:T(8,128)S(1)} %grad_act.1.gact_ref, bf16[1,2048]{1,0:T(2,128)(2,1)S(1)} %reshape.71.bias_ref, ...), custom_call_target="tpu_custom_call" | custom-call | flops 6899999744 | bytes 1048576 | tf_op jit(solution)/shard_map/feed_forward/pallas_call | solution.py:611
  127.1 10.2 %wide_grads.1 = (bf16[1024,4096]{1,0:T(8,128)(2,1)}, bf16[256,1024]{1,0:T(8,128)(2,1)S(1)}) custom-call(bf16[256,1024]{1,0:T(8,128)(2,1)S(1)} %get-tuple-element.90.n_ref, bf16[256,2048]{1,0:T(8,128)(2,1)S(1)} %get-tuple-element.91.gh_ref, bf16[256,1024]{1,0:T(8,128)(2,1)} %copy-done, bf16[256,2048]{1,0:T(8,128)(2,1)S(1)} %get-tuple-element.92.act_ref, ...), custom_call_target="tpu_custom_call" | custom-call | flops 9200000000 | bytes 1048576 | tf_op jit(solution)/shard_map/wide_grads/pallas_call | solution.py:649
  137.4 2.1 collective-permute-done.5.swapped_ref
  140.3 4.8 %middle_back.1 = (f32[256,1024]{1,0:T(8,128)}, bf16[256,1024]{1,0:T(8,128)(2,1)}, bf16[8,64,256]{2,1,0:T(8,128)(2,1)}, f32[8,1024]{1,0:T(8,128)}) custom-call(f32[256,1024]{1,0:T(8,128)} %copy-done.1, bf16[256,1024]{1,0:T(8,128)(2,1)} %copy-done.2, bf16[256,1024]{1,0:T(8,128)(2,1)} %copy-done.35, f32[8,1024]{1,0:T(8,128)} %copy-done.3, ...), custom_call_target="tpu_custom_call" | custom-call | flops 3449999872 | bytes 1048576 | tf_op jit(solution)/shard_map/middle_back/pallas_call | solution.py:692
  145.1 4.9 %all-to-all-start.3 = ((bf16[8,64,256]{2,1,0:T(8,128)(2,1)}), bf16[8,64,256]{2,1,0:T(8,128)(2,1)S(1)}, u32[]{:S(2)}, u32[]{:S(2)}) async-start(bf16[8,64,256]{2,1,0:T(8,128)(2,1)} %get-tuple-element.100), calls=%async_computation.3 | async-start | bytes 524288 | tf_op jit(solution)/shard_map/all_to_all | solution.py:383
  150.7 1.6 proj_grads.1
  152.4 0.8 copy-done.27
  153.2 5.6 %all-to-all-done.3.gout_ref = bf16[8,64,256]{2,1,0:T(8,128)(2,1)S(1)} async-done(((bf16[8,64,256]{2,1,0:T(8,128)(2,1)}), bf16[8,64,256]{2,1,0:T(8,128)(2,1)S(1)}, u32[]{:S(2)}, u32[]{:S(2)}) %all-to-all-start.3) | async-done | bytes 262176 | tf_op jit(solution)/shard_map/all_to_all | solution.py:383
  159.4 15.7 %attention_backward.1 = (bf16[8,64,256]{2,1,0:T(8,128)(2,1)S(1)}, f32[8,128,256]{2,1,0:T(8,128)S(1)}, bf16[8,128,256]{2,1,0:T(8,128)(2,1)S(1)}) custom-call(s32[4]{0:T(128)S(1)} %copy-done.19, s32[1,2]{1,0:T(1,128)S(1)} %copy-done.18, bf16[4096,80]{1,0:T(8,128)(2,1)} %copy-done.22, bf16[64,4096]{1,0:T(8,128)(2,1)} %copy-done.24, ...), custom_call_target="tpu_custom_call" | custom-call | flops 29899999232 | bytes 1048576 | tf_op jit(solution)/shard_map/attention_backward/pallas_call | solution.py:340
  175.2 1.9 collective-permute-done.7.other_ref
  177.1 1.0 merge.1
  178.2 3.5 %all-to-all-start.4 = ((bf16[8,192,256]{2,1,0:T(8,128)(2,1)}), bf16[8,192,256]{2,1,0:T(8,128)(2,1)S(1)}, u32[]{:S(2)}, u32[]{:S(2)}) async-start(bf16[8,192,256]{2,1,0:T(8,128)(2,1)} %merge.1), calls=%async_computation.4 | async-start | bytes 1572864 | tf_op jit(solution)/shard_map/all_to_all | solution.py:383
  181.8 3.5 %final.1 = (bf16[256,1024]{1,0:T(8,128)(2,1)}, f32[1,128]{1,0:T(1,128)S(1)}) custom-call(s32[4]{0:T(128)S(1)} %copy-done.19, bf16[256,1024]{1,0:T(8,128)(2,1)} %copy-done.20, f32[256,1024]{1,0:T(8,128)} %copy-done.1, bf16[256,1024]{1,0:T(8,128)(2,1)S(1)} %get-tuple-element.110.mine_ref, bf16[256,1024]{1,0:T(8,128)(2,1)S(1)} %collective-permute-done.6.swapped_ref, ...), custom_call_target="tpu_custom_call" | custom-call | flops 3449999872 | bytes 1048576 | tf_op jit(solution)/shard_map/final/pallas_call | solution.py:408
  185.3 11.4 %all-to-all-done.4.gback_ref = bf16[8,192,256]{2,1,0:T(8,128)(2,1)S(1)} async-done(((bf16[8,192,256]{2,1,0:T(8,128)(2,1)}), bf16[8,192,256]{2,1,0:T(8,128)(2,1)S(1)}, u32[]{:S(2)}, u32[]{:S(2)}) %all-to-all-start.4) | async-done | bytes 786464 | tf_op jit(solution)/shard_map/all_to_all | solution.py:383
  196.7 5.9 %back.1 = (bf16[128,1024]{1,0:T(8,128)(2,1)S(1)}, bf16[128,1024]{1,0:T(8,128)(2,1)S(1)}, f32[8,512]{1,0:T(8,128)S(1)}, bf16[512,1920]{1,0:T(8,128)(2,1)}, bf16[1...) custom-call(bf16[8,192,256]{2,1,0:T(8,128)(2,1)S(1)} %all-to-all-done.4.gback_ref, ...), custom_call_target="tpu_custom_call" | custom-call | flops 5750000128 | bytes 1048576 | tf_op jit(solution)/shard_map/back/pallas_call | solution.py:408
  202.5 0.9 copy-done.28
  204.1 1.5 collective-permute-start.8
  205.5 6.8 %collective-permute-done.8.swapped_ref = bf16[128,1024]{1,0:T(8,128)(2,1)S(1)} collective-permute-done((bf16[128,1024]{1,0:T(8,128)(2,1)S(1)}, bf16[128,1024]{1,0:T(8,128)(2,1)S(1)}, u32[]{:S(2)}, u32[]{:S(2)}) %collective-permute-start.8) | collective-permute-done | bytes 262176 | tf_op jit(solution)/shard_map/ppermute | solution.py:379
  212.4 0.8 copy-done.38
  213.2 5.5 %qkv_core_sum.1 = bf16[512,2432]{1,0:T(8,128)(2,1)} custom-call(bf16[1536,256]{1,0:T(8,128)(2,1)} %copy-done.28, bf16[256,512]{1,0:T(8,128)(2,1)} %copy-done.30, bf16[2,16,128]{2,1,0:T(8,128)(2,1)} %copy-done.34, bf16[512,1920]{1,0:T(8,128)(2,1)} %collective-permute-done.10.b_ref, bf16[512,640]{1,0:T(8,128)(2,1)} %copy-done.27, bf16[512,640]{1,0:T(8,128)(2,1)} %copy-done.38, ...), custom_call_target="tpu_custom_call" | custom-call | flops 4600000000 | bytes 1048576 | tf_op jit(solution)/shard_map/qkv_core_sum/pallas_call | solution.py:834
  218.7 4.1 %all-to-all-start.5 = ((bf16[32,16,2432]{2,1,0:T(8,128)(2,1)}), bf16[32,16,2432]{2,1,0:T(8,128)(2,1)S(1)}, u32[]{:S(2)}, u32[]{:S(2)}) async-start(bf16[32,16,2432]{2,1,0:T(8,128)(2,1)} %bitcast.42), calls=%async_computation.5 | async-start | bytes 4980736 | tf_op jit(solution)/shard_map/all_to_all | solution.py:383
  222.8 1.0 constant_dynamic-slice_fusion
  223.8 3.3 %collective-permute-start.12 = (bf16[16,4096]{1,0:T(8,128)(2,1)S(1)}, bf16[16,4096]{1,0:T(8,128)(2,1)S(1)}, u32[]{:S(2)}, u32[]{:S(2)}) collective-permute-start(bf16[16,4096]{1,0:T(8,128)(2,1)S(1)} %get-tuple-element.141), channel_id=1, source_target_pairs={{0,16},{16,0},{1,17},{17,1},{2,18},{18,2},{3,19},{19,3},{4,20},{20... | collective-permute-start | bytes 393224 | tf_op jit(solution)/shard_map/ppermute | solution.py:379
  227.1 2.5 end.1.mine_ref
  229.6 1.6 collective-permute-start.9
  231.2 22.2 %collective-permute-done.12.theirs_ref = bf16[16,4096]{1,0:T(8,128)(2,1)S(1)} collective-permute-done((bf16[16,4096]{1,0:T(8,128)(2,1)S(1)}, bf16[16,4096]{1,0:T(8,128)(2,1)S(1)}, u32[]{:S(2)}, u32[]{:S(2)}) %collective-permute-start.12) | collective-permute-done | bytes 131104 | tf_op jit(solution)/shard_map/ppermute | solution.py:379
  254.1 6.0 %collective-permute-done.9.theirs_ref = bf16[128,1024]{1,0:T(8,128)(2,1)S(1)} collective-permute-done((bf16[128,1024]{1,0:T(8,128)(2,1)S(1)}, bf16[128,1024]{1,0:T(8,128)(2,1)S(1)}, u32[]{:S(2)}, u32[]{:S(2)}) %collective-permute-start.9) | collective-permute-done | bytes 262176 | tf_op jit(solution)/shard_map/ppermute | solution.py:379
  261.3 1.5 total_qkv.1
  263.3 0.8 join.1
  (110 shorter events, 12.6 us)
Async XLA Ops:
  8.9 5.9 %copy-start.36 = (bf16[16,3,512]{2,0,1:T(8,128)(2,1)S(1)}, bf16[16,3,512]{2,0,1:T(8,128)(2,1)}, u32[]{:S(2)}) copy-start(bf16[16,3,512]{2,0,1:T(8,128)(2,1)} %param.19) | copy-start | bytes 147460
  8.9 6.0 %copy-start.12 = (bf16[16]{0:T(256)(128)(2,1)S(1)}, bf16[16]{0:T(256)(128)(2,1)}, u32[]{:S(2)}) copy-start(bf16[16]{0:T(256)(128)(2,1)} %param.17) | copy-start | bytes 100
  8.9 6.0 %copy-start.13 = (bf16[16]{0:T(256)(128)(2,1)S(1)}, bf16[16]{0:T(256)(128)(2,1)}, u32[]{:S(2)}) copy-start(bf16[16]{0:T(256)(128)(2,1)} %param.18) | copy-start | bytes 100
  8.9 6.0 %copy-start.14 = (bf16[16]{0:T(256)(128)(2,1)S(1)}, bf16[16]{0:T(256)(128)(2,1)}, u32[]{:S(2)}) copy-start(bf16[16]{0:T(256)(128)(2,1)} %param.22) | copy-start | bytes 100
  8.9 6.0 %copy-start.15 = (bf16[16]{0:T(256)(128)(2,1)S(1)}, bf16[16]{0:T(256)(128)(2,1)}, u32[]{:S(2)}) copy-start(bf16[16]{0:T(256)(128)(2,1)} %param.23) | copy-start | bytes 100
  8.9 6.0 %copy-start.16 = (bf16[16]{0:T(256)(128)(2,1)S(1)}, bf16[16]{0:T(256)(128)(2,1)}, u32[]{:S(2)}) copy-start(bf16[16]{0:T(256)(128)(2,1)} %param.24) | copy-start | bytes 100
  8.9 6.0 %copy-start.17 = (bf16[16]{0:T(256)(128)(2,1)S(1)}, bf16[16]{0:T(256)(128)(2,1)}, u32[]{:S(2)}) copy-start(bf16[16]{0:T(256)(128)(2,1)} %param.28) | copy-start | bytes 100
  9.7 19.6 %collective-permute-start.2 = (bf16[16,4608]{1,0:T(8,128)(2,1)S(1)}, bf16[16,4608]{1,0:T(8,128)(2,1)S(1)}, u32[]{:S(2)}, u32[]{:S(2)}) collective-permute-start(bf16[16,4608]{1,0:T(8,128)(2,1)S(1)} %rest_payload.1.mine_ref), channel_id=1, source_target_pairs={{0,16},{16,0},{1,17},{17,1},{2,18},{18,2},{3,19},{19,3},{4,20},{20... | collective-permute-start | bytes 442376 | tf_op jit(solution)/shard_map/ppermute | solution.py:379
  13.8 15.5 %collective-permute-start.3 = (bf16[16,512]{1,0:T(8,128)(2,1)}, bf16[16,512]{1,0:T(8,128)(2,1)S(1)}, u32[]{:S(2)}, u32[]{:S(2)}) collective-permute-start(bf16[16,512]{1,0:T(8,128)(2,1)} %bitcast.10.proj_ref), channel_id=1, source_target_pairs={{0,1},{1,0},{2,3},{3,2},{4,5},{5,4},{6,7},{7,6},{8,9},{9,8},{10,11... | collective-permute-start | bytes 49160 | tf_op jit(solution)/shard_map/ppermute | solution.py:379
  14.8 14.5 %collective-permute-start.4 = (bf16[16,512]{1,0:T(8,128)(2,1)}, bf16[16,512]{1,0:T(8,128)(2,1)S(1)}, u32[]{:S(2)}, u32[]{:S(2)}) collective-permute-start(bf16[16,512]{1,0:T(8,128)(2,1)} %bitcast.10.proj_ref), channel_id=1, source_target_pairs={{0,17},{1,16},{16,1},{17,0},{2,19},{3,18},{18,3},{19,2},{4,21},{5,... | collective-permute-start | bytes 49160 | tf_op jit(solution)/shard_map/ppermute | solution.py:951
  19.2 36.4 %all-to-all-start = ((bf16[32,16,1664]{2,1,0:T(8,128)(2,1)}), bf16[32,16,1664]{2,1,0:T(8,128)(2,1)}, u32[]{:S(2)}, u32[]{:S(2)}) async-start(bf16[32,16,1664]{2,1,0:T(8,128)(2,1)} %weights_payload.1), calls=%async_computation | async-start | bytes 3407872 | tf_op jit(solution)/shard_map/all_to_all | solution.py:383
  29.2 1.0 copy-start.6
  29.2 1.3 copy-start.7
  29.2 1.3 copy-start.19
  29.2 81.0 %all-gather.2.cloned.1.call-start = ((), (), s32[]{:S(2)}) async-start(), calls=%async_computation.8 | async-start | bytes 10813440 | tf_op jit(solution)/shard_map/all_gather | solution.py:953
  30.5 28.9 %copy-start.11 = (bf16[2,512]{1,0:T(2,128)(2,1)S(1)}, bf16[2,512]{1,0:T(2,128)(2,1)}, u32[]{:S(2)}) copy-start(bf16[2,512]{1,0:T(2,128)(2,1)} %bias_ref.1) | copy-start | bytes 6148
  33.2 30.0 %copy-start.20 = (bf16[256,1024]{1,0:T(8,128)(2,1)}, bf16[256,1024]{1,0:T(8,128)(2,1)S(1)}, u32[]{:S(2)}) copy-start(bf16[256,1024]{1,0:T(8,128)(2,1)S(1)} %get-tuple-element.78.inputs_ref) | copy-start | bytes 1572868
  55.6 3.8 %collective-permute-start = (bf16[512,1664]{1,0:T(8,128)(2,1)}, bf16[512,1664]{1,0:T(8,128)(2,1)S(1)}, u32[]{:S(2)}, u32[]{:S(2)}) collective-permute-start(bf16[512,1664]{1,0:T(8,128)(2,1)} %bitcast.8.own_ref), channel_id=1, source_target_pairs={{0,2},{2,0},{1,3},{3,1},{4,6},{6,4},{5,7},{7,5},{8,10},{10,8},{9,1... | collective-permute-start | bytes 5111816 | tf_op jit(solution)/shard_map/ppermute | solution.py:379
  59.4 3.8 %copy-start.5 = (bf16[512,1664]{1,0:T(8,128)(2,1)}, bf16[512,1664]{1,0:T(8,128)(2,1)S(1)}, u32[]{:S(2)}) copy-start(bf16[512,1664]{1,0:T(8,128)(2,1)S(1)} %collective-permute-done.other_ref) | copy-start | bytes 5111812
  63.2 36.5 %copy-start.3 = (f32[8,1024]{1,0:T(8,128)}, f32[8,1024]{1,0:T(8,128)S(1)}, u32[]{:S(2)}) copy-start(f32[8,1024]{1,0:T(8,128)S(1)} %get-tuple-element.88.vectors_ref) | copy-start | bytes 98308
  63.2 36.4 %copy-start.30 = (bf16[256,512]{1,0:T(8,128)(2,1)}, bf16[256,512]{1,0:T(8,128)(2,1)S(1)}, u32[]{:S(2)}) copy-start(bf16[256,512]{1,0:T(8,128)(2,1)S(1)} %get-tuple-element.121.own_n_ref) | copy-start | bytes 786436
  63.2 36.4 %copy-start.31 = (bf16[256,512]{1,0:T(8,128)(2,1)}, bf16[256,512]{1,0:T(8,128)(2,1)S(1)}, u32[]{:S(2)}) copy-start(bf16[256,512]{1,0:T(8,128)(2,1)S(1)} %get-tuple-element.116.other_n_ref) | copy-start | bytes 786436
  63.2 27.2 %copy-start.18 = (s32[1,2]{1,0:T(1,128)S(1)}, s32[1,2]{1,0:T(1,128)}, u32[]{:S(2)}) copy-start(s32[1,2]{1,0:T(1,128)} %starts_ref.3) | copy-start | bytes 28
  88.4 17.1 %copy-start.37 = (bf16[2048]{0:T(1024)(128)(2,1)S(1)}, bf16[2048]{0:T(1024)(128)(2,1)}, u32[]{:S(2)}) copy-start(bf16[2048]{0:T(1024)(128)(2,1)} %param.26) | copy-start | bytes 12292
  88.4 2.0 collective-permute-start.1
  99.7 5.8 %copy-start.32 = (f32[8,64,256]{2,1,0:T(8,128)}, f32[8,64,256]{2,1,0:T(8,128)S(1)}, u32[]{:S(2)}) copy-start(f32[8,64,256]{2,1,0:T(8,128)S(1)} %get-tuple-element.106.out_ref) | copy-start | bytes 1572868
  99.7 17.8 %all-to-all-start.2 = ((bf16[16,64,256]{2,1,0:T(8,128)(2,1)}), bf16[16,64,256]{2,1,0:T(8,128)(2,1)S(1)}, u32[]{:S(2)}, u32[]{:S(2)}) async-start(bf16[16,64,256]{2,1,0:T(8,128)(2,1)} %bitcast.9), calls=%async_computation.2 | async-start | bytes 1048576 | tf_op jit(solution)/shard_map/all_to_all | solution.py:383
  105.2 98.2 %reduce-scatter.3.cloned.1.call-start = ((), (), s32[]{:S(2)}) async-start(), calls=%async_computation.9 | async-start | bytes 9437184 | tf_op jit(solution)/shard_map/reduce_scatter | solution.py:993
  107.6 1.0 copy-start.23
  110.2 4.3 %copy-start.26 = (bf16[8,80,256]{2,1,0:T(8,128)(2,1)}, bf16[8,80,256]{2,1,0:T(8,128)(2,1)S(1)}, u32[]{:S(2)}) copy-start(bf16[8,80,256]{2,1,0:T(8,128)(2,1)S(1)} %get-tuple-element.96.query_ref) | copy-start | bytes 983044
  120.3 6.1 %copy-start.1 = (f32[256,1024]{1,0:T(8,128)}, f32[256,1024]{1,0:T(8,128)S(1)}, u32[]{:S(2)}) copy-start(f32[256,1024]{1,0:T(8,128)S(1)} %get-tuple-element.89.middle_ref) | copy-start | bytes 3145732
  120.3 6.1 %copy-start.21 = (bf16[512,256]{1,0:T(8,128)(2,1)}, bf16[512,256]{1,0:T(8,128)(2,1)S(1)}, u32[]{:S(2)}) copy-start(bf16[512,256]{1,0:T(8,128)(2,1)S(1)} %get-tuple-element.102.heads_ref) | copy-start | bytes 786436
  126.4 10.9 %copy-start.2 = (bf16[256,1024]{1,0:T(8,128)(2,1)}, bf16[256,1024]{1,0:T(8,128)(2,1)S(1)}, u32[]{:S(2)}) copy-start(bf16[256,1024]{1,0:T(8,128)(2,1)S(1)} %get-tuple-element.98.mine_ref) | copy-start | bytes 1572868
  126.4 10.9 %copy-start.29 = (bf16[256,2048]{1,0:T(8,128)(2,1)}, bf16[256,2048]{1,0:T(8,128)(2,1)S(1)}, u32[]{:S(2)}) copy-start(bf16[256,2048]{1,0:T(8,128)(2,1)S(1)} %get-tuple-element.91.gh_ref) | copy-start | bytes 3145732
  126.4 13.0 %collective-permute-start.5 = (bf16[256,1024]{1,0:T(8,128)(2,1)S(1)}, bf16[256,1024]{1,0:T(8,128)(2,1)S(1)}, u32[]{:S(2)}, u32[]{:S(2)}) collective-permute-start(bf16[256,1024]{1,0:T(8,128)(2,1)S(1)} %get-tuple-element.98.mine_ref), channel_id=1, source_target_pairs={{0,1},{1,0},{2,3},{3,2},{4,5},{5,4},{6,7},{7,6},{8,9},{9,8},{10,11... | collective-permute-start | bytes 1572872 | tf_op jit(solution)/shard_map/ppermute | solution.py:379
  145.1 13.7 %all-to-all-start.3 = ((bf16[8,64,256]{2,1,0:T(8,128)(2,1)}), bf16[8,64,256]{2,1,0:T(8,128)(2,1)S(1)}, u32[]{:S(2)}, u32[]{:S(2)}) async-start(bf16[8,64,256]{2,1,0:T(8,128)(2,1)} %get-tuple-element.100), calls=%async_computation.3 | async-start | bytes 524288 | tf_op jit(solution)/shard_map/all_to_all | solution.py:383
  158.8 16.4 %collective-permute-start.6 = (bf16[256,1024]{1,0:T(8,128)(2,1)S(1)}, bf16[256,1024]{1,0:T(8,128)(2,1)S(1)}, u32[]{:S(2)}, u32[]{:S(2)}) collective-permute-start(bf16[256,1024]{1,0:T(8,128)(2,1)S(1)} %get-tuple-element.110.mine_ref), channel_id=1, source_target_pairs={{0,1},{1,0},{2,3},{3,2},{4,5},{5,4},{6,7},{7,6},{8,9},{9,8},{10,11... | collective-permute-start | bytes 1572872 | tf_op jit(solution)/shard_map/ppermute | solution.py:379
  175.2 2.0 collective-permute-start.7
  177.1 4.7 %copy-start.4 = (f32[8,1024]{1,0:T(8,128)S(1)}, f32[8,1024]{1,0:T(8,128)}, u32[]{:S(2)}) copy-start(f32[8,1024]{1,0:T(8,128)} %copy-done.3) | copy-start | bytes 98308
  178.2 18.5 %all-to-all-start.4 = ((bf16[8,192,256]{2,1,0:T(8,128)(2,1)}), bf16[8,192,256]{2,1,0:T(8,128)(2,1)S(1)}, u32[]{:S(2)}, u32[]{:S(2)}) async-start(bf16[8,192,256]{2,1,0:T(8,128)(2,1)} %merge.1), calls=%async_computation.4 | async-start | bytes 1572864 | tf_op jit(solution)/shard_map/all_to_all | solution.py:383
  181.7 41.1 %reduce-scatter.5.cloned.1.call-start = ((), (), s32[]{:S(2)}) async-start(), calls=%async_computation.10 | async-start | bytes 1310720 | tf_op jit(solution)/shard_map/reduce_scatter | solution.py:1059
  203.4 8.9 %collective-permute-start.10 = (bf16[512,1920]{1,0:T(8,128)(2,1)}, bf16[512,1920]{1,0:T(8,128)(2,1)}, u32[]{:S(2)}, u32[]{:S(2)}) collective-permute-start(bf16[512,1920]{1,0:T(8,128)(2,1)} %get-tuple-element.123), channel_id=1, source_target_pairs={{0,2},{2,0},{1,3},{3,1},{4,6},{6,4},{5,7},{7,5},{8,10},{10,8},{9,1... | collective-permute-start | bytes 5898248 | tf_op jit(solution)/shard_map/ppermute | solution.py:379
  203.5 8.9 %collective-permute-start.11 = (bf16[512,640]{1,0:T(8,128)(2,1)S(1)}, bf16[512,640]{1,0:T(8,128)(2,1)S(1)}, u32[]{:S(2)}, u32[]{:S(2)}) collective-permute-start(bf16[512,640]{1,0:T(8,128)(2,1)S(1)} %get-tuple-element.126), channel_id=1, source_target_pairs={{0,2},{2,0},{1,3},{3,1},{4,6},{6,4},{5,7},{7,5},{8,10},{10,8},{9,1... | collective-permute-start | bytes 1966088 | tf_op jit(solution)/shard_map/ppermute | solution.py:379
  204.1 8.3 %collective-permute-start.8 = (bf16[128,1024]{1,0:T(8,128)(2,1)S(1)}, bf16[128,1024]{1,0:T(8,128)(2,1)S(1)}, u32[]{:S(2)}, u32[]{:S(2)}) collective-permute-start(bf16[128,1024]{1,0:T(8,128)(2,1)S(1)} %get-tuple-element.119), channel_id=1, source_target_pairs={{0,1},{1,0},{2,3},{3,2},{4,5},{5,4},{6,7},{7,6},{8,9},{9,8},{10,11... | collective-permute-start | bytes 786440 | tf_op jit(solution)/shard_map/ppermute | solution.py:379
  218.7 41.4 %all-to-all-start.5 = ((bf16[32,16,2432]{2,1,0:T(8,128)(2,1)}), bf16[32,16,2432]{2,1,0:T(8,128)(2,1)S(1)}, u32[]{:S(2)}, u32[]{:S(2)}) async-start(bf16[32,16,2432]{2,1,0:T(8,128)(2,1)} %bitcast.42), calls=%async_computation.5 | async-start | bytes 4980736 | tf_op jit(solution)/shard_map/all_to_all | solution.py:383
  223.8 29.6 %collective-permute-start.12 = (bf16[16,4096]{1,0:T(8,128)(2,1)S(1)}, bf16[16,4096]{1,0:T(8,128)(2,1)S(1)}, u32[]{:S(2)}, u32[]{:S(2)}) collective-permute-start(bf16[16,4096]{1,0:T(8,128)(2,1)S(1)} %get-tuple-element.141), channel_id=1, source_target_pairs={{0,16},{16,0},{1,17},{17,1},{2,18},{18,2},{3,19},{19,3},{4,20},{20... | collective-permute-start | bytes 393224 | tf_op jit(solution)/shard_map/ppermute | solution.py:379
  229.6 30.5 %collective-permute-start.9 = (bf16[128,1024]{1,0:T(8,128)(2,1)S(1)}, bf16[128,1024]{1,0:T(8,128)(2,1)S(1)}, u32[]{:S(2)}, u32[]{:S(2)}) collective-permute-start(bf16[128,1024]{1,0:T(8,128)(2,1)S(1)} %end.1.mine_ref), channel_id=1, source_target_pairs={{0,1},{1,0},{2,3},{3,2},{4,5},{5,4},{6,7},{7,6},{8,9},{9,8},{10,11... | collective-permute-start | bytes 786440 | tf_op jit(solution)/shard_map/ppermute | solution.py:379
  260.8 3.6 %collective-permute-start.13 = (f32[2,16]{1,0:T(2,128)S(1)}, f32[2,16]{1,0:T(2,128)S(1)}, u32[]{:S(2)}, u32[]{:S(2)}) collective-permute-start(f32[2,16]{1,0:T(2,128)S(1)} %slice.28), channel_id=1, source_target_pairs={{0,1},{1,0},{2,3},{3,2},{4,5},{5,4},{6,7},{7,6},{8,9},{9,8},{10,11... | collective-permute-start | bytes 392 | tf_op jit(solution)/shard_map/ppermute | solution.py:379
  (13 other events, 10.5 us)
Sparse Core Ops, SparseCore 0:
  32.3 69.3 all-gather.1
  140.4 49.2 reduce-scatter.2
  203.6 18.9 reduce-scatter.4

commit v4 on v3

--- a/solution.py
+++ b/solution.py
@@ -474,7 +474,7 @@
 
     def one(k, _):
         for c in range(3):
-            out_ref[k, :, 512 * c : 512 * (c + 1)] = qkv_ref[:, c, :]
+            out_ref[k, :, 512 * c : 512 * (c + 1)] = qkv_ref[c]
         out_ref[k, :, 1536:] = small
         return 0
 
@@ -933,13 +933,16 @@
         prepare_kernel,
         "weights_payload",
         shape(32, 16, 1664),
-        qkv_weight,
+        qkv_weight.transpose(1, 0, 2),
         *[v.reshape(1, 16) for v in vectors],
     )
     own_q = exchange(pay_q, SPREAD).reshape(512, 1664)
     proj_rows = proj_weight.T
     pay_r = call(
-        prepare_rest_kernel, "rest_payload", shape(16, 4608), proj_rows, fc_weight, out_weight.T
+        prepare_rest_kernel,
+        "rest_payload",
+        shape(16, 4608),
+        *[far(x) for x in (proj_rows, fc_weight, out_weight.T)],
     )
     pair_r = call(
         pair_kernel,

time: 273 us -> 268 us (0.982)
    unnamed x79 -> x76, local copies, waits for them, and re-layouts: 10.8 us -> 9.07 us
  transfers between devices with their start and end apart: 22 -> 22, of which waited for: 12 -> 11; matrix products, arithmetic and copies ran while one was open for 1% -> 1% of each run, Pallas kernels for 29% -> 29%
where the time goes in v4:
time: 268 us; the launch traced here: 267 us
  waiting for transfers between devices  86.9 us (32%)
  Pallas kernels  86.4 us (32%)
  starting transfers between devices  42.4 us (16%)
  blocking collectives  25.1 us (9%)
  between operations  14.3 us (5%)
  local copies, waits for them, and re-layouts  11.7 us (4%)
    ppermute x13, waiting for transfers between devices, swap(): return lax.ppermute(field, axis, [(0, 1), (1, 0)])  44.8 us
    all_to_all x5, waiting for transfers between devices, exchange(): return lax.all_to_all(field, axes, split_axis=0, concat_axis=0, tiled=True)  42 us
    all_to_all x5, starting transfers between devices, exchange(): return lax.all_to_all(field, axes, split_axis=0, concat_axis=0, tiled=True)  28.4 us
    pallas_call x13, Pallas kernels, call(): pl.pallas_call(kernel, grid=(1,), out_shape=outs, in_specs=[SM] * scalars...  26.5 us
    all_to_all x1, blocking collectives, exchange(): return lax.all_to_all(field, axes, split_axis=0, concat_axis=0, tiled=True)  25.1 us
    pallas_call x1, Pallas kernels, attn_backward(): pl.pallas_call(backward_kernel, grid=(1,), out_shape=outs, in_specs=[SM,...  15.7 us
    ppermute x13, starting transfers between devices, swap(): return lax.ppermute(field, axis, [(0, 1), (1, 0)])  13.7 us
    pallas_call x1, Pallas kernels, wide_grads(): pl.pallas_call(wide_kernel, grid=(8,), out_shape=(shape(1024, 4096), shap...  10.3 us
  transfers between devices with their start and end apart: 22, of which 11 were waited for; matrix products, arithmetic and copies ran while one was open for 1% of the time, Pallas kernels for 29%

profile of v4, /device:TPU:0, one launch (start us, length us, event | category | flops | bytes accessed | tf_op | source)
XLA Modules:
  0.0 266.8 jit_solution(3431053824659687091)
XLA Ops:
  7.3 1.0 rest_payload.1.mine_ref
  8.2 4.0 %collective-permute-start.2 = (bf16[16,4608]{1,0:T(8,128)(2,1)S(1)}, bf16[16,4608]{1,0:T(8,128)(2,1)S(1)}, u32[]{:S(2)}, u32[]{:S(2)}) collective-permute-start(bf16[16,4608]{1,0:T(8,128)(2,1)S(1)} %rest_payload.1.mine_ref), channel_id=1, source_target_pairs={{0,16},{16,0},{1,17},{17,1},{2,18},{18,2},{3,19},{19,3},{4,20},{20... | collective-permute-start | bytes 442376 | tf_op jit(solution)/shard_map/ppermute | solution.py:379
  12.3 1.0 collective-permute-start.3
  13.3 1.6 weights_payload.1
  14.9 9.9 %all-to-all-start = ((bf16[32,16,1664]{2,1,0:T(8,128)(2,1)}), bf16[32,16,1664]{2,1,0:T(8,128)(2,1)}, u32[]{:S(2)}, u32[]{:S(2)}) async-start(bf16[32,16,1664]{2,1,0:T(8,128)(2,1)} %weights_payload.1), calls=%async_computation | async-start | bytes 3407872 | tf_op jit(solution)/shard_map/all_to_all | solution.py:383
  26.2 1.9 inputs.1
  28.9 22.4 %all-to-all-done = bf16[32,16,1664]{2,1,0:T(8,128)(2,1)} async-done(((bf16[32,16,1664]{2,1,0:T(8,128)(2,1)}), bf16[32,16,1664]{2,1,0:T(8,128)(2,1)}, u32[]{:S(2)}, u32[]{:S(2)}) %all-to-all-start) | async-done | bytes 1703968 | tf_op jit(solution)/shard_map/all_to_all | solution.py:383
  51.3 3.8 %collective-permute-done.other_ref = bf16[512,1664]{1,0:T(8,128)(2,1)S(1)} collective-permute-done((bf16[512,1664]{1,0:T(8,128)(2,1)}, bf16[512,1664]{1,0:T(8,128)(2,1)S(1)}, u32[]{:S(2)}, u32[]{:S(2)}) %collective-permute-start) | collective-permute-done | bytes 1703968 | tf_op jit(solution)/shard_map/ppermute | solution.py:379
  55.1 3.8 %qkv.1 = (bf16[8,192,256]{2,1,0:T(8,128)(2,1)S(1)}, bf16[256,512]{1,0:T(8,128)(2,1)S(1)}, bf16[256,512]{1,0:T(8,128)(2,1)S(1)}, f32[8,1024]{1,0:T(8,128)S(1)}) custom-call(bf16[256,1024]{1,0:T(8,128)(2,1)S(1)} %get-tuple-element.78.inputs_ref, bf16[512,1664]{1,0:T(8,128)(2,1)} %bitcast.9.own_ref, bf16[512,1664]{1,0:T(8,128)(2,1)S(1)} %collective-permute-done.other_ref, ...), custom_call_target="tpu_custom_call" | custom-call | flops 3449999872 | bytes 1048576 | tf_op jit(solution)/shard_map/qkv/pallas_call | solution.py:408
  58.9 25.1 %all_to_all.30.own_ref = bf16[8,192,256]{2,1,0:T(8,128)(2,1)S(1)} all-to-all(bf16[8,192,256]{2,1,0:T(8,128)(2,1)S(1)} %get-tuple-element.80), channel_id=1, replica_groups=mesh['x'=4,'zh'=2,'y'=4,'c'=2,'tp'=2] {'zh','y'}, dimensions={0} | all-to-all | bytes 1572864 | tf_op jit(solution)/shard_map/all_to_all | solution.py:383
  84.2 1.9 collective-permute-done.1.other_ref
  86.1 9.2 %attention_forward.1 = (f32[8,64,256]{2,1,0:T(8,128)S(1)}, bf16[8,2,64,256]{3,2,1,0:T(8,128)(2,1)}, f32[8,1,256]{2,1,0:T(1,128)S(1)}) custom-call(s32[4]{0:T(128)S(1)} %copy-done.18, s32[1,2]{1,0:T(1,128)S(1)} %copy-done.17, bf16[8,192,256]{2,1,0:T(8,128)(2,1)S(1)} %all_to_all.30.own_ref, bf16[8,128,256]{2,1,0:T(8,128)(2,1)S(1)} %collective-permute-done.1.other_ref), custom_call_target="tpu_custom_call" | custom-call | flops 9200000000 | bytes 1048576 | tf_op jit(solution)/shard_map/attention_forward/pallas_call | solution.py:302
  95.4 5.5 %all-to-all-start.2 = ((bf16[16,64,256]{2,1,0:T(8,128)(2,1)}), bf16[16,64,256]{2,1,0:T(8,128)(2,1)S(1)}, u32[]{:S(2)}, u32[]{:S(2)}) async-start(bf16[16,64,256]{2,1,0:T(8,128)(2,1)} %bitcast.10), calls=%async_computation.2 | async-start | bytes 1048576 | tf_op jit(solution)/shard_map/all_to_all | solution.py:383
  101.2 1.1 attention_stage.1
  102.3 1.0 copy-done.21
  103.3 1.0 copy-done.22
  104.3 0.8 copy-done.23
  105.9 4.2 %grad_act.1.gact_ref = f32[256,2048]{1,0:T(8,128)S(1)} custom-call(bf16[256,1024]{1,0:T(8,128)(2,1)} %copy-done, bf16[1024,5120]{1,0:T(8,128)(2,1)} %all-gather.2.cloned.1.call-done.weight_ref), custom_call_target="tpu_custom_call" | custom-call | flops 3449999872 | bytes 1048576 | tf_op jit(solution)/shard_map/grad_act/pallas_call | solution.py:569
  110.1 2.6 all-to-all-done.2.heads_ref
  112.7 2.8 %attn_end.1 = (f32[256,1024]{1,0:T(8,128)S(1)}, bf16[256,1024]{1,0:T(8,128)(2,1)S(1)}, bf16[512,256]{1,0:T(8,128)(2,1)S(1)}) custom-call(bf16[16,64,256]{2,1,0:T(8,128)(2,1)S(1)} %all-to-all-done.2.heads_ref, bf16[1024,5120]{1,0:T(8,128)(2,1)} %all-gather.2.cloned.1.call-done.weight_ref, bf16[256,1024]{1,0:T(8,128)(2,1)} %copy-done.19, f32[8,1024]{1,0:T(8,128)} %copy-done.3), custom_call_target="tpu_custom_call" | custom-call | flops 3449999872 | bytes 1048576 | tf_op jit(solution)/shard_map/attn_end/pallas_call | solution.py:546
  115.6 6.1 %feed_forward.1 = (bf16[256,2048]{1,0:T(8,128)(2,1)S(1)}, bf16[256,2048]{1,0:T(8,128)(2,1)S(1)}, bf16[256,1024]{1,0:T(8,128)(2,1)S(1)}) custom-call(bf16[256,1024]{1,0:T(8,128)(2,1)S(1)} %get-tuple-element.90.n_ref, f32[256,2048]{1,0:T(8,128)S(1)} %grad_act.1.gact_ref, bf16[1,2048]{1,0:T(2,128)(2,1)S(1)} %reshape.71.bias_ref, ...), custom_call_target="tpu_custom_call" | custom-call | flops 6899999744 | bytes 1048576 | tf_op jit(solution)/shard_map/feed_forward/pallas_call | solution.py:611
  122.4 10.3 %wide_grads.1 = (bf16[1024,4096]{1,0:T(8,128)(2,1)}, bf16[256,1024]{1,0:T(8,128)(2,1)S(1)}) custom-call(bf16[256,1024]{1,0:T(8,128)(2,1)S(1)} %get-tuple-element.90.n_ref, bf16[256,2048]{1,0:T(8,128)(2,1)S(1)} %get-tuple-element.91.gh_ref, bf16[256,1024]{1,0:T(8,128)(2,1)} %copy-done, bf16[256,2048]{1,0:T(8,128)(2,1)S(1)} %get-tuple-element.92.act_ref, ...), custom_call_target="tpu_custom_call" | custom-call | flops 9200000000 | bytes 1048576 | tf_op jit(solution)/shard_map/wide_grads/pallas_call | solution.py:649
  132.6 1.8 collective-permute-done.5.swapped_ref
  135.3 4.8 %middle_back.1 = (f32[256,1024]{1,0:T(8,128)}, bf16[256,1024]{1,0:T(8,128)(2,1)}, bf16[8,64,256]{2,1,0:T(8,128)(2,1)}, f32[8,1024]{1,0:T(8,128)}) custom-call(f32[256,1024]{1,0:T(8,128)} %copy-done.1, bf16[256,1024]{1,0:T(8,128)(2,1)} %copy-done.2, bf16[256,1024]{1,0:T(8,128)(2,1)} %copy-done.34, f32[8,1024]{1,0:T(8,128)} %copy-done.3, ...), custom_call_target="tpu_custom_call" | custom-call | flops 3449999872 | bytes 1048576 | tf_op jit(solution)/shard_map/middle_back/pallas_call | solution.py:692
  140.1 5.3 %all-to-all-start.3 = ((bf16[8,64,256]{2,1,0:T(8,128)(2,1)}), bf16[8,64,256]{2,1,0:T(8,128)(2,1)S(1)}, u32[]{:S(2)}, u32[]{:S(2)}) async-start(bf16[8,64,256]{2,1,0:T(8,128)(2,1)} %get-tuple-element.100), calls=%async_computation.3 | async-start | bytes 524288 | tf_op jit(solution)/shard_map/all_to_all | solution.py:383
  146.1 1.6 proj_grads.1
  148.6 5.6 %all-to-all-done.3.gout_ref = bf16[8,64,256]{2,1,0:T(8,128)(2,1)S(1)} async-done(((bf16[8,64,256]{2,1,0:T(8,128)(2,1)}), bf16[8,64,256]{2,1,0:T(8,128)(2,1)S(1)}, u32[]{:S(2)}, u32[]{:S(2)}) %all-to-all-start.3) | async-done | bytes 262176 | tf_op jit(solution)/shard_map/all_to_all | solution.py:383
  154.9 15.7 %attention_backward.1 = (bf16[8,64,256]{2,1,0:T(8,128)(2,1)S(1)}, f32[8,128,256]{2,1,0:T(8,128)S(1)}, bf16[8,128,256]{2,1,0:T(8,128)(2,1)S(1)}) custom-call(s32[4]{0:T(128)S(1)} %copy-done.18, s32[1,2]{1,0:T(1,128)S(1)} %copy-done.17, bf16[4096,80]{1,0:T(8,128)(2,1)} %copy-done.21, bf16[64,4096]{1,0:T(8,128)(2,1)} %copy-done.23, ...), custom_call_target="tpu_custom_call" | custom-call | flops 29899999232 | bytes 1048576 | tf_op jit(solution)/shard_map/attention_backward/pallas_call | solution.py:340
  170.7 2.1 collective-permute-done.7.other_ref
  172.8 1.1 merge.1
  173.8 3.5 %all-to-all-start.4 = ((bf16[8,192,256]{2,1,0:T(8,128)(2,1)}), bf16[8,192,256]{2,1,0:T(8,128)(2,1)S(1)}, u32[]{:S(2)}, u32[]{:S(2)}) async-start(bf16[8,192,256]{2,1,0:T(8,128)(2,1)} %merge.1), calls=%async_computation.4 | async-start | bytes 1572864 | tf_op jit(solution)/shard_map/all_to_all | solution.py:383
  177.4 3.5 %final.1 = (bf16[256,1024]{1,0:T(8,128)(2,1)}, f32[1,128]{1,0:T(1,128)S(1)}) custom-call(s32[4]{0:T(128)S(1)} %copy-done.18, bf16[256,1024]{1,0:T(8,128)(2,1)} %copy-done.19, f32[256,1024]{1,0:T(8,128)} %copy-done.1, bf16[256,1024]{1,0:T(8,128)(2,1)S(1)} %get-tuple-element.110.mine_ref, bf16[256,1024]{1,0:T(8,128)(2,1)S(1)} %collective-permute-done.6.swapped_ref, ...), custom_call_target="tpu_custom_call" | custom-call | flops 3449999872 | bytes 1048576 | tf_op jit(solution)/shard_map/final/pallas_call | solution.py:408
  180.9 11.4 %all-to-all-done.4.gback_ref = bf16[8,192,256]{2,1,0:T(8,128)(2,1)S(1)} async-done(((bf16[8,192,256]{2,1,0:T(8,128)(2,1)}), bf16[8,192,256]{2,1,0:T(8,128)(2,1)S(1)}, u32[]{:S(2)}, u32[]{:S(2)}) %all-to-all-start.4) | async-done | bytes 786464 | tf_op jit(solution)/shard_map/all_to_all | solution.py:383
  192.3 5.9 %back.1 = (bf16[128,1024]{1,0:T(8,128)(2,1)S(1)}, bf16[128,1024]{1,0:T(8,128)(2,1)S(1)}, f32[8,512]{1,0:T(8,128)S(1)}, bf16[512,1920]{1,0:T(8,128)(2,1)}, bf16[1...) custom-call(bf16[8,192,256]{2,1,0:T(8,128)(2,1)S(1)} %all-to-all-done.4.gback_ref, ...), custom_call_target="tpu_custom_call" | custom-call | flops 5750000128 | bytes 1048576 | tf_op jit(solution)/shard_map/back/pallas_call | solution.py:408
  198.1 0.9 copy-done.27
  199.7 1.2 collective-permute-start.8
  200.9 7.1 %collective-permute-done.8.swapped_ref = bf16[128,1024]{1,0:T(8,128)(2,1)S(1)} collective-permute-done((bf16[128,1024]{1,0:T(8,128)(2,1)S(1)}, bf16[128,1024]{1,0:T(8,128)(2,1)S(1)}, u32[]{:S(2)}, u32[]{:S(2)}) %collective-permute-start.8) | collective-permute-done | bytes 262176 | tf_op jit(solution)/shard_map/ppermute | solution.py:379
  208.0 0.8 copy-done.36
  208.8 5.5 %qkv_core_sum.1 = bf16[512,2432]{1,0:T(8,128)(2,1)} custom-call(bf16[1536,256]{1,0:T(8,128)(2,1)} %copy-done.27, bf16[256,512]{1,0:T(8,128)(2,1)} %copy-done.29, bf16[2,16,128]{2,1,0:T(8,128)(2,1)} %copy-done.33, bf16[512,1920]{1,0:T(8,128)(2,1)} %collective-permute-done.10.b_ref, bf16[512,640]{1,0:T(8,128)(2,1)} %copy-done.26, bf16[512,640]{1,0:T(8,128)(2,1)} %copy-done.36, ...), custom_call_target="tpu_custom_call" | custom-call | flops 4600000000 | bytes 1048576 | tf_op jit(solution)/shard_map/qkv_core_sum/pallas_call | solution.py:834
  214.3 4.1 %all-to-all-start.5 = ((bf16[32,16,2432]{2,1,0:T(8,128)(2,1)}), bf16[32,16,2432]{2,1,0:T(8,128)(2,1)S(1)}, u32[]{:S(2)}, u32[]{:S(2)}) async-start(bf16[32,16,2432]{2,1,0:T(8,128)(2,1)} %bitcast.43), calls=%async_computation.5 | async-start | bytes 4980736 | tf_op jit(solution)/shard_map/all_to_all | solution.py:383
  218.4 1.0 constant_dynamic-slice_fusion
  219.4 3.3 %collective-permute-start.12 = (bf16[16,4096]{1,0:T(8,128)(2,1)S(1)}, bf16[16,4096]{1,0:T(8,128)(2,1)S(1)}, u32[]{:S(2)}, u32[]{:S(2)}) collective-permute-start(bf16[16,4096]{1,0:T(8,128)(2,1)S(1)} %get-tuple-element.141), channel_id=1, source_target_pairs={{0,16},{16,0},{1,17},{17,1},{2,18},{18,2},{3,19},{19,3},{4,20},{20... | collective-permute-start | bytes 393224 | tf_op jit(solution)/shard_map/ppermute | solution.py:379
  222.7 2.5 end.1.mine_ref
  225.2 1.3 collective-permute-start.9
  226.5 22.5 %collective-permute-done.12.theirs_ref = bf16[16,4096]{1,0:T(8,128)(2,1)S(1)} collective-permute-done((bf16[16,4096]{1,0:T(8,128)(2,1)S(1)}, bf16[16,4096]{1,0:T(8,128)(2,1)S(1)}, u32[]{:S(2)}, u32[]{:S(2)}) %collective-permute-start.12) | collective-permute-done | bytes 131104 | tf_op jit(solution)/shard_map/ppermute | solution.py:379
  249.7 5.7 %collective-permute-done.9.theirs_ref = bf16[128,1024]{1,0:T(8,128)(2,1)S(1)} collective-permute-done((bf16[128,1024]{1,0:T(8,128)(2,1)S(1)}, bf16[128,1024]{1,0:T(8,128)(2,1)S(1)}, u32[]{:S(2)}, u32[]{:S(2)}) %collective-permute-start.9) | collective-permute-done | bytes 262176 | tf_op jit(solution)/shard_map/ppermute | solution.py:379
  256.9 1.5 total_qkv.1
  258.9 0.8 join.1
  (107 shorter events, 11.0 us)
Async XLA Ops:
  7.2 5.1 %copy-start.37 = (bf16[512,16]{0,1:T(8,128)(2,1)S(1)}, bf16[512,16]{0,1:T(8,128)(2,1)}, u32[]{:S(2)}) copy-start(bf16[512,16]{0,1:T(8,128)(2,1)} %param.21) | copy-start | bytes 49156
  7.2 6.1 %copy-start.8 = (bf16[16,3,512]{2,0,1:T(8,128)(2,1)S(1)}, bf16[16,3,512]{2,0,1:T(8,128)(2,1)}, u32[]{:S(2)}) copy-start(bf16[16,3,512]{2,0,1:T(8,128)(2,1)} %param.19) | copy-start | bytes 147460
  7.2 6.1 %copy-start.11 = (bf16[16]{0:T(256)(128)(2,1)S(1)}, bf16[16]{0:T(256)(128)(2,1)}, u32[]{:S(2)}) copy-start(bf16[16]{0:T(256)(128)(2,1)} %param.17) | copy-start | bytes 100
  7.2 6.1 %copy-start.12 = (bf16[16]{0:T(256)(128)(2,1)S(1)}, bf16[16]{0:T(256)(128)(2,1)}, u32[]{:S(2)}) copy-start(bf16[16]{0:T(256)(128)(2,1)} %param.18) | copy-start | bytes 100
  7.2 6.1 %copy-start.13 = (bf16[16]{0:T(256)(128)(2,1)S(1)}, bf16[16]{0:T(256)(128)(2,1)}, u32[]{:S(2)}) copy-start(bf16[16]{0:T(256)(128)(2,1)} %param.22) | copy-start | bytes 100
  7.2 6.1 %copy-start.14 = (bf16[16]{0:T(256)(128)(2,1)S(1)}, bf16[16]{0:T(256)(128)(2,1)}, u32[]{:S(2)}) copy-start(bf16[16]{0:T(256)(128)(2,1)} %param.23) | copy-start | bytes 100
  7.2 6.1 %copy-start.15 = (bf16[16]{0:T(256)(128)(2,1)S(1)}, bf16[16]{0:T(256)(128)(2,1)}, u32[]{:S(2)}) copy-start(bf16[16]{0:T(256)(128)(2,1)} %param.24) | copy-start | bytes 100
  7.3 6.1 %copy-start.16 = (bf16[16]{0:T(256)(128)(2,1)S(1)}, bf16[16]{0:T(256)(128)(2,1)}, u32[]{:S(2)}) copy-start(bf16[16]{0:T(256)(128)(2,1)} %param.28) | copy-start | bytes 100
  8.2 16.7 %collective-permute-start.2 = (bf16[16,4608]{1,0:T(8,128)(2,1)S(1)}, bf16[16,4608]{1,0:T(8,128)(2,1)S(1)}, u32[]{:S(2)}, u32[]{:S(2)}) collective-permute-start(bf16[16,4608]{1,0:T(8,128)(2,1)S(1)} %rest_payload.1.mine_ref), channel_id=1, source_target_pairs={{0,16},{16,0},{1,17},{17,1},{2,18},{18,2},{3,19},{19,3},{4,20},{20... | collective-permute-start | bytes 442376 | tf_op jit(solution)/shard_map/ppermute | solution.py:379
  12.3 12.7 %collective-permute-start.3 = (bf16[16,512]{1,0:T(8,128)(2,1)S(1)}, bf16[16,512]{1,0:T(8,128)(2,1)S(1)}, u32[]{:S(2)}, u32[]{:S(2)}) collective-permute-start(bf16[16,512]{1,0:T(8,128)(2,1)S(1)} %bitcast.46), channel_id=1, source_target_pairs={{0,1},{1,0},{2,3},{3,2},{4,5},{5,4},{6,7},{7,6},{8,9},{9,8},{10,11... | collective-permute-start | bytes 49160 | tf_op jit(solution)/shard_map/ppermute | solution.py:379
  13.3 11.7 %collective-permute-start.4 = (bf16[16,512]{1,0:T(8,128)(2,1)S(1)}, bf16[16,512]{1,0:T(8,128)(2,1)S(1)}, u32[]{:S(2)}, u32[]{:S(2)}) collective-permute-start(bf16[16,512]{1,0:T(8,128)(2,1)S(1)} %bitcast.47), channel_id=1, source_target_pairs={{0,17},{1,16},{16,1},{17,0},{2,19},{3,18},{18,3},{19,2},{4,21},{5,... | collective-permute-start | bytes 49160 | tf_op jit(solution)/shard_map/ppermute | solution.py:954
  14.9 36.3 %all-to-all-start = ((bf16[32,16,1664]{2,1,0:T(8,128)(2,1)}), bf16[32,16,1664]{2,1,0:T(8,128)(2,1)}, u32[]{:S(2)}, u32[]{:S(2)}) async-start(bf16[32,16,1664]{2,1,0:T(8,128)(2,1)} %weights_payload.1), calls=%async_computation | async-start | bytes 3407872 | tf_op jit(solution)/shard_map/all_to_all | solution.py:383
  24.8 1.0 copy-start.6
  24.9 1.3 copy-start.7
  24.9 1.3 copy-start.18
  24.9 81.0 %all-gather.2.cloned.1.call-start = ((), (), s32[]{:S(2)}) async-start(), calls=%async_computation.8 | async-start | bytes 10813440 | tf_op jit(solution)/shard_map/all_gather | solution.py:956
  26.2 28.9 %copy-start.10 = (bf16[2,512]{1,0:T(2,128)(2,1)S(1)}, bf16[2,512]{1,0:T(2,128)(2,1)}, u32[]{:S(2)}) copy-start(bf16[2,512]{1,0:T(2,128)(2,1)} %bias_ref.1) | copy-start | bytes 6148
  28.9 30.0 %copy-start.19 = (bf16[256,1024]{1,0:T(8,128)(2,1)}, bf16[256,1024]{1,0:T(8,128)(2,1)S(1)}, u32[]{:S(2)}) copy-start(bf16[256,1024]{1,0:T(8,128)(2,1)S(1)} %get-tuple-element.78.inputs_ref) | copy-start | bytes 1572868
  51.3 3.8 %collective-permute-start = (bf16[512,1664]{1,0:T(8,128)(2,1)}, bf16[512,1664]{1,0:T(8,128)(2,1)S(1)}, u32[]{:S(2)}, u32[]{:S(2)}) collective-permute-start(bf16[512,1664]{1,0:T(8,128)(2,1)} %bitcast.9.own_ref), channel_id=1, source_target_pairs={{0,2},{2,0},{1,3},{3,1},{4,6},{6,4},{5,7},{7,5},{8,10},{10,8},{9,1... | collective-permute-start | bytes 5111816 | tf_op jit(solution)/shard_map/ppermute | solution.py:379
  55.1 3.8 %copy-start.5 = (bf16[512,1664]{1,0:T(8,128)(2,1)}, bf16[512,1664]{1,0:T(8,128)(2,1)S(1)}, u32[]{:S(2)}) copy-start(bf16[512,1664]{1,0:T(8,128)(2,1)S(1)} %collective-permute-done.other_ref) | copy-start | bytes 5111812
  58.9 36.5 %copy-start.3 = (f32[8,1024]{1,0:T(8,128)}, f32[8,1024]{1,0:T(8,128)S(1)}, u32[]{:S(2)}) copy-start(f32[8,1024]{1,0:T(8,128)S(1)} %get-tuple-element.88.vectors_ref) | copy-start | bytes 98308
  58.9 36.4 %copy-start.29 = (bf16[256,512]{1,0:T(8,128)(2,1)}, bf16[256,512]{1,0:T(8,128)(2,1)S(1)}, u32[]{:S(2)}) copy-start(bf16[256,512]{1,0:T(8,128)(2,1)S(1)} %get-tuple-element.121.own_n_ref) | copy-start | bytes 786436
  58.9 36.4 %copy-start.30 = (bf16[256,512]{1,0:T(8,128)(2,1)}, bf16[256,512]{1,0:T(8,128)(2,1)S(1)}, u32[]{:S(2)}) copy-start(bf16[256,512]{1,0:T(8,128)(2,1)S(1)} %get-tuple-element.116.other_n_ref) | copy-start | bytes 786436
  58.9 27.2 %copy-start.17 = (s32[1,2]{1,0:T(1,128)S(1)}, s32[1,2]{1,0:T(1,128)}, u32[]{:S(2)}) copy-start(s32[1,2]{1,0:T(1,128)} %starts_ref.3) | copy-start | bytes 28
  84.1 17.1 %copy-start.35 = (bf16[2048]{0:T(1024)(128)(2,1)S(1)}, bf16[2048]{0:T(1024)(128)(2,1)}, u32[]{:S(2)}) copy-start(bf16[2048]{0:T(1024)(128)(2,1)} %param.26) | copy-start | bytes 12292
  84.1 2.0 collective-permute-start.1
  95.4 5.8 %copy-start.31 = (f32[8,64,256]{2,1,0:T(8,128)}, f32[8,64,256]{2,1,0:T(8,128)S(1)}, u32[]{:S(2)}) copy-start(f32[8,64,256]{2,1,0:T(8,128)S(1)} %get-tuple-element.106.out_ref) | copy-start | bytes 1572868
  95.4 17.3 %all-to-all-start.2 = ((bf16[16,64,256]{2,1,0:T(8,128)(2,1)}), bf16[16,64,256]{2,1,0:T(8,128)(2,1)S(1)}, u32[]{:S(2)}, u32[]{:S(2)}) async-start(bf16[16,64,256]{2,1,0:T(8,128)(2,1)} %bitcast.10), calls=%async_computation.2 | async-start | bytes 1048576 | tf_op jit(solution)/shard_map/all_to_all | solution.py:383
  100.9 98.1 %reduce-scatter.3.cloned.1.call-start = ((), (), s32[]{:S(2)}) async-start(), calls=%async_computation.9 | async-start | bytes 9437184 | tf_op jit(solution)/shard_map/reduce_scatter | solution.py:996
  105.9 4.3 %copy-start.25 = (bf16[8,80,256]{2,1,0:T(8,128)(2,1)}, bf16[8,80,256]{2,1,0:T(8,128)(2,1)S(1)}, u32[]{:S(2)}) copy-start(bf16[8,80,256]{2,1,0:T(8,128)(2,1)S(1)} %get-tuple-element.96.query_ref) | copy-start | bytes 983044
  115.5 6.1 %copy-start.1 = (f32[256,1024]{1,0:T(8,128)}, f32[256,1024]{1,0:T(8,128)S(1)}, u32[]{:S(2)}) copy-start(f32[256,1024]{1,0:T(8,128)S(1)} %get-tuple-element.89.middle_ref) | copy-start | bytes 3145732
  115.5 6.1 %copy-start.20 = (bf16[512,256]{1,0:T(8,128)(2,1)}, bf16[512,256]{1,0:T(8,128)(2,1)S(1)}, u32[]{:S(2)}) copy-start(bf16[512,256]{1,0:T(8,128)(2,1)S(1)} %get-tuple-element.102.heads_ref) | copy-start | bytes 786436
  121.7 11.0 %copy-start.2 = (bf16[256,1024]{1,0:T(8,128)(2,1)}, bf16[256,1024]{1,0:T(8,128)(2,1)S(1)}, u32[]{:S(2)}) copy-start(bf16[256,1024]{1,0:T(8,128)(2,1)S(1)} %get-tuple-element.98.mine_ref) | copy-start | bytes 1572868
  121.7 10.9 %copy-start.28 = (bf16[256,2048]{1,0:T(8,128)(2,1)}, bf16[256,2048]{1,0:T(8,128)(2,1)S(1)}, u32[]{:S(2)}) copy-start(bf16[256,2048]{1,0:T(8,128)(2,1)S(1)} %get-tuple-element.91.gh_ref) | copy-start | bytes 3145732
  121.7 12.7 %collective-permute-start.5 = (bf16[256,1024]{1,0:T(8,128)(2,1)S(1)}, bf16[256,1024]{1,0:T(8,128)(2,1)S(1)}, u32[]{:S(2)}, u32[]{:S(2)}) collective-permute-start(bf16[256,1024]{1,0:T(8,128)(2,1)S(1)} %get-tuple-element.98.mine_ref), channel_id=1, source_target_pairs={{0,1},{1,0},{2,3},{3,2},{4,5},{5,4},{6,7},{7,6},{8,9},{9,8},{10,11... | collective-permute-start | bytes 1572872 | tf_op jit(solution)/shard_map/ppermute | solution.py:379
  140.1 14.2 %all-to-all-start.3 = ((bf16[8,64,256]{2,1,0:T(8,128)(2,1)}), bf16[8,64,256]{2,1,0:T(8,128)(2,1)S(1)}, u32[]{:S(2)}, u32[]{:S(2)}) async-start(bf16[8,64,256]{2,1,0:T(8,128)(2,1)} %get-tuple-element.100), calls=%async_computation.3 | async-start | bytes 524288 | tf_op jit(solution)/shard_map/all_to_all | solution.py:383
  154.2 16.4 %collective-permute-start.6 = (bf16[256,1024]{1,0:T(8,128)(2,1)S(1)}, bf16[256,1024]{1,0:T(8,128)(2,1)S(1)}, u32[]{:S(2)}, u32[]{:S(2)}) collective-permute-start(bf16[256,1024]{1,0:T(8,128)(2,1)S(1)} %get-tuple-element.110.mine_ref), channel_id=1, source_target_pairs={{0,1},{1,0},{2,3},{3,2},{4,5},{5,4},{6,7},{7,6},{8,9},{9,8},{10,11... | collective-permute-start | bytes 1572872 | tf_op jit(solution)/shard_map/ppermute | solution.py:379
  170.6 2.1 collective-permute-start.7
  172.8 4.7 %copy-start.4 = (f32[8,1024]{1,0:T(8,128)S(1)}, f32[8,1024]{1,0:T(8,128)}, u32[]{:S(2)}) copy-start(f32[8,1024]{1,0:T(8,128)} %copy-done.3) | copy-start | bytes 98308
  173.8 18.5 %all-to-all-start.4 = ((bf16[8,192,256]{2,1,0:T(8,128)(2,1)}), bf16[8,192,256]{2,1,0:T(8,128)(2,1)S(1)}, u32[]{:S(2)}, u32[]{:S(2)}) async-start(bf16[8,192,256]{2,1,0:T(8,128)(2,1)} %merge.1), calls=%async_computation.4 | async-start | bytes 1572864 | tf_op jit(solution)/shard_map/all_to_all | solution.py:383
  177.4 41.0 %reduce-scatter.5.cloned.1.call-start = ((), (), s32[]{:S(2)}) async-start(), calls=%async_computation.10 | async-start | bytes 1310720 | tf_op jit(solution)/shard_map/reduce_scatter | solution.py:1062
  199.0 8.9 %collective-permute-start.10 = (bf16[512,1920]{1,0:T(8,128)(2,1)}, bf16[512,1920]{1,0:T(8,128)(2,1)}, u32[]{:S(2)}, u32[]{:S(2)}) collective-permute-start(bf16[512,1920]{1,0:T(8,128)(2,1)} %get-tuple-element.123), channel_id=1, source_target_pairs={{0,2},{2,0},{1,3},{3,1},{4,6},{6,4},{5,7},{7,5},{8,10},{10,8},{9,1... | collective-permute-start | bytes 5898248 | tf_op jit(solution)/shard_map/ppermute | solution.py:379
  199.1 8.9 %collective-permute-start.11 = (bf16[512,640]{1,0:T(8,128)(2,1)S(1)}, bf16[512,640]{1,0:T(8,128)(2,1)S(1)}, u32[]{:S(2)}, u32[]{:S(2)}) collective-permute-start(bf16[512,640]{1,0:T(8,128)(2,1)S(1)} %get-tuple-element.126), channel_id=1, source_target_pairs={{0,2},{2,0},{1,3},{3,1},{4,6},{6,4},{5,7},{7,5},{8,10},{10,8},{9,1... | collective-permute-start | bytes 1966088 | tf_op jit(solution)/shard_map/ppermute | solution.py:379
  199.7 8.3 %collective-permute-start.8 = (bf16[128,1024]{1,0:T(8,128)(2,1)S(1)}, bf16[128,1024]{1,0:T(8,128)(2,1)S(1)}, u32[]{:S(2)}, u32[]{:S(2)}) collective-permute-start(bf16[128,1024]{1,0:T(8,128)(2,1)S(1)} %get-tuple-element.119), channel_id=1, source_target_pairs={{0,1},{1,0},{2,3},{3,2},{4,5},{5,4},{6,7},{7,6},{8,9},{9,8},{10,11... | collective-permute-start | bytes 786440 | tf_op jit(solution)/shard_map/ppermute | solution.py:379
  214.3 41.2 %all-to-all-start.5 = ((bf16[32,16,2432]{2,1,0:T(8,128)(2,1)}), bf16[32,16,2432]{2,1,0:T(8,128)(2,1)S(1)}, u32[]{:S(2)}, u32[]{:S(2)}) async-start(bf16[32,16,2432]{2,1,0:T(8,128)(2,1)} %bitcast.43), calls=%async_computation.5 | async-start | bytes 4980736 | tf_op jit(solution)/shard_map/all_to_all | solution.py:383
  219.4 29.6 %collective-permute-start.12 = (bf16[16,4096]{1,0:T(8,128)(2,1)S(1)}, bf16[16,4096]{1,0:T(8,128)(2,1)S(1)}, u32[]{:S(2)}, u32[]{:S(2)}) collective-permute-start(bf16[16,4096]{1,0:T(8,128)(2,1)S(1)} %get-tuple-element.141), channel_id=1, source_target_pairs={{0,16},{16,0},{1,17},{17,1},{2,18},{18,2},{3,19},{19,3},{4,20},{20... | collective-permute-start | bytes 393224 | tf_op jit(solution)/shard_map/ppermute | solution.py:379
  225.2 30.3 %collective-permute-start.9 = (bf16[128,1024]{1,0:T(8,128)(2,1)S(1)}, bf16[128,1024]{1,0:T(8,128)(2,1)S(1)}, u32[]{:S(2)}, u32[]{:S(2)}) collective-permute-start(bf16[128,1024]{1,0:T(8,128)(2,1)S(1)} %end.1.mine_ref), channel_id=1, source_target_pairs={{0,1},{1,0},{2,3},{3,2},{4,5},{5,4},{6,7},{7,6},{8,9},{9,8},{10,11... | collective-permute-start | bytes 786440 | tf_op jit(solution)/shard_map/ppermute | solution.py:379
  256.1 3.6 %collective-permute-start.13 = (f32[2,16]{1,0:T(2,128)S(1)}, f32[2,16]{1,0:T(2,128)S(1)}, u32[]{:S(2)}, u32[]{:S(2)}) collective-permute-start(f32[2,16]{1,0:T(2,128)S(1)} %slice.28), channel_id=1, source_target_pairs={{0,1},{1,0},{2,3},{3,2},{4,5},{5,4},{6,7},{7,6},{8,9},{9,8},{10,11... | collective-permute-start | bytes 392 | tf_op jit(solution)/shard_map/ppermute | solution.py:379
  (12 other events, 9.8 us)
Sparse Core Ops, SparseCore 0:
  28.0 69.3 all-gather.1
  135.4 49.9 reduce-scatter.2
  199.2 18.9 reduce-scatter.4
